TPU v7x, 32 devices: a whole 2x2x4 slice. The times are simulated.
32 devices in a mesh: dp: 4 (over y, x), tensor: 8 (over z, core).
Axes of the slice: x: 2, y: 2, z: 4, core: 2. Of those that a mesh axis runs over, the one named last changes fastest.
Arguments:
- tokens: bfloat16 [8, 1024, 2048], P('dp', 'tensor'), may hold values from -6 to 6
- cotangent: bfloat16 [8, 1024, 2048], P('dp', 'tensor'), may hold values from -6 to 6
- lengths: int32 [8], P('dp'), may hold values from 256 to 1024, as said below
- ln1_gain: float32 [2048], replicated, may hold values from 0.25 to 1.75
- ln1_shift: float32 [2048], replicated, may hold values from -1.5 to 1.5
- qkv_weight: bfloat16 [3, 2048, 2048], P(None, None, 'tensor'), may hold values from -0.125 to 0.125
- qkv_bias: float32 [2, 2048], P(None, 'tensor'), may hold values from -2.5 to 2.5
- out_weight: bfloat16 [2048, 2048], P('tensor'), may hold values from -1 to 1
- out_bias: float32 [2048], replicated, may hold values from -1.5 to 1.5
- ln2_gain: float32 [2048], replicated, may hold values from 0.25 to 1.75
- ln2_shift: float32 [2048], replicated, may hold values from -1.5 to 1.5
- up_weight: bfloat16 [2048, 8192], P(None, 'tensor'), may hold values from -0.125 to 0.125
- up_bias: float32 [8192], P('tensor'), may hold values from -2.5 to 2.5
- down_weight: bfloat16 [8192, 2048], P('tensor'), may hold values from -0.0625 to 0.0625
- down_bias: float32 [2048], replicated, may hold values from -1.5 to 1.5
Outputs:
- output: bfloat16 [8, 1024, 2048], P('dp', 'tensor')
- input_grad: float32 [8, 1024, 2048], P('dp', 'tensor')
- ln1_gain_grad: float32 [2048], replicated
- ln1_shift_grad: float32 [2048], replicated
- qkv_weight_grad: float32 [3, 2048, 2048], P(None, None, 'tensor')
- qkv_bias_grad: float32 [2, 2048], P(None, 'tensor')
- out_weight_grad: float32 [2048, 2048], P('tensor')
- out_bias_grad: float32 [2048], replicated
- ln2_gain_grad: float32 [2048], replicated
- ln2_shift_grad: float32 [2048], replicated
- up_weight_grad: float32 [2048, 8192], P(None, 'tensor')
- up_bias_grad: float32 [8192], P('tensor')
- down_weight_grad: float32 [8192, 2048], P('tensor')
- down_bias_grad: float32 [2048], replicated
Inputs may be any that keep to these rules, and one draw needn't show every extreme that they name: A sequence's valid tokens are its first lengths[s] slots; some sequence has exactly 1024 and some exactly 256.
All inputs are finite; a program needn't handle non-finite values.
Results may differ from a plain program's by a relative error of at most 0.018.
Values may be sent and summed in bfloat16 or wider, within the bound.
A program may use at most 256 MiB of HBM per device.

v0:
```python
import jax
import jax.numpy as jnp
from jax import lax
from jax.sharding import PartitionSpec as P

HD = 128


norm_epsilon = 1e-05
block_rows = 512


def layer_norm(values, norm_gain, norm_shift):
    centre = values - jnp.mean(values, axis=-1, keepdims=True)
    spread = jnp.mean(centre * centre, axis=-1, keepdims=True)
    return centre * lax.rsqrt(spread + norm_epsilon) * norm_gain + norm_shift


def gelu_exact(values):
    return jax.nn.gelu(values, approximate=False)


def flat_product(left_rows, right_rows):
    flat = left_rows.reshape(-1, left_rows.shape[-1])
    result = jnp.dot(flat, right_rows, preferred_element_type=jnp.float32)
    return result.reshape(left_rows.shape[:-1] + (right_rows.shape[-1],))


def product_back(left_rows, right_rows):
    flat = left_rows.reshape(-1, left_rows.shape[-1])
    result = lax.dot_general(
        flat, right_rows, (((1,), (1,)), ((), ())), preferred_element_type=jnp.float32
    )
    return result.reshape(left_rows.shape[:-1] + (right_rows.shape[0],))


def rows_product(left_rows, right_rows):
    left_flat = left_rows.reshape(-1, left_rows.shape[-1])
    right_flat = right_rows.reshape(-1, right_rows.shape[-1])
    return lax.dot_general(
        left_flat, right_flat, (((0,), (0,)), ((), ())), preferred_element_type=jnp.float32
    )


def allowed_mask(first_row, row_count, slot_count, length):
    row_ids = first_row + lax.broadcasted_iota(jnp.int32, (row_count, slot_count), 0)
    col_ids = lax.broadcasted_iota(jnp.int32, (row_count, slot_count), 1)
    return (col_ids <= row_ids) & (col_ids < length)


def block_scores(query_block, key_rows, first_row, length):
    scores = jnp.einsum("qhd,khd->hqk", query_block, key_rows, preferred_element_type=jnp.float32)
    allowed = allowed_mask(first_row, query_block.shape[0], key_rows.shape[0], length)
    return jnp.where(allowed[None], scores, -1e30)


def attend_forward(query_rows, key_rows, value_rows, length):
    slot_count = query_rows.shape[0]
    step_rows = min(block_rows, slot_count)
    outputs = []
    totals = []
    for block_index in range(slot_count // step_rows):
        first_row = block_index * step_rows
        query_block = query_rows[first_row : first_row + step_rows]
        scores = block_scores(query_block, key_rows, first_row, length)
        row_peak = jnp.max(scores, axis=-1, keepdims=True)
        log_total = row_peak + jnp.log(jnp.sum(jnp.exp(scores - row_peak), axis=-1, keepdims=True))
        weights = jnp.exp(scores - log_total).astype(jnp.bfloat16)
        outputs.append(
            jnp.einsum("hqk,khd->qhd", weights, value_rows, preferred_element_type=jnp.float32)
        )
        totals.append(log_total)
    return (jnp.concatenate(outputs, axis=0), jnp.concatenate(totals, axis=1))


def attend_backward(query_rows, key_rows, value_rows, grad_rows, log_totals, length):
    slot_count = query_rows.shape[0]
    step_rows = min(block_rows, slot_count)
    grad_keys = jnp.zeros(key_rows.shape, jnp.float32)
    grad_values = jnp.zeros(value_rows.shape, jnp.float32)
    grad_queries = []
    for block_index in range(slot_count // step_rows):
        first_row = block_index * step_rows
        query_block = query_rows[first_row : first_row + step_rows]
        grad_block = grad_rows[first_row : first_row + step_rows]
        scores = block_scores(query_block, key_rows, first_row, length)
        probs = jnp.exp(scores - log_totals[:, first_row : first_row + step_rows])
        grad_probs = jnp.einsum(
            "qhd,khd->hqk", grad_block, value_rows, preferred_element_type=jnp.float32
        )
        centre = jnp.sum(probs * grad_probs, axis=-1, keepdims=True)
        grad_scores = (probs * (grad_probs - centre)).astype(jnp.bfloat16)
        grad_queries.append(
            jnp.einsum("hqk,khd->qhd", grad_scores, key_rows, preferred_element_type=jnp.float32)
        )
        grad_keys = grad_keys + jnp.einsum(
            "hqk,qhd->khd", grad_scores, query_block, preferred_element_type=jnp.float32
        )
        grad_values = grad_values + jnp.einsum(
            "hqk,qhd->khd",
            probs.astype(jnp.bfloat16),
            grad_block,
            preferred_element_type=jnp.float32,
        )
    return (jnp.concatenate(grad_queries, axis=0), grad_keys, grad_values)


def body(
    tokens,
    cotangent,
    lengths,
    ln1_gain,
    ln1_shift,
    qkv_weight,
    qkv_bias,
    out_weight,
    out_bias,
    ln2_gain,
    ln2_shift,
    up_weight,
    up_bias,
    down_weight,
    down_bias,
):
    seq_count, local_rows, model_width = tokens.shape
    part_width = qkv_weight.shape[2]
    head_count = part_width // HD
    score_scale = HD ** (-0.5)
    inputs = tokens.astype(jnp.float32)
    normed_one = layer_norm(inputs, ln1_gain, ln1_shift).astype(jnp.bfloat16)
    gathered_one = lax.all_gather(normed_one, "tensor", axis=1, tiled=True)
    slot_count = gathered_one.shape[1]
    head_shape = (seq_count, slot_count, head_count, HD)
    query_rows = (
        ((flat_product(gathered_one, qkv_weight[0]) + qkv_bias[0]) * score_scale)
        .astype(jnp.bfloat16)
        .reshape(head_shape)
    )
    key_rows = flat_product(gathered_one, qkv_weight[1]).astype(jnp.bfloat16).reshape(head_shape)
    value_rows = (
        (flat_product(gathered_one, qkv_weight[2]) + qkv_bias[1])
        .astype(jnp.bfloat16)
        .reshape(head_shape)
    )
    attended, log_totals = lax.map(
        lambda item: attend_forward(item[0], item[1], item[2], item[3]),
        (query_rows, key_rows, value_rows, lengths),
    )
    mixed_heads = attended.reshape(seq_count, slot_count, part_width).astype(jnp.bfloat16)
    attn_local = lax.psum_scatter(
        flat_product(mixed_heads, out_weight).astype(jnp.bfloat16),
        "tensor",
        scatter_dimension=1,
        tiled=True,
    ).astype(jnp.float32)
    hidden_state = inputs + attn_local + out_bias
    normed_two = layer_norm(hidden_state, ln2_gain, ln2_shift).astype(jnp.bfloat16)
    gathered_two = lax.all_gather(normed_two, "tensor", axis=1, tiled=True)
    pre_act = flat_product(gathered_two, up_weight) + up_bias
    activated = gelu_exact(pre_act).astype(jnp.bfloat16)
    mlp_local = lax.psum_scatter(
        flat_product(activated, down_weight).astype(jnp.bfloat16),
        "tensor",
        scatter_dimension=1,
        tiled=True,
    ).astype(jnp.float32)
    output = (hidden_state + mlp_local + down_bias).astype(jnp.bfloat16)
    slot_ids = lax.axis_index("tensor") * local_rows + lax.broadcasted_iota(
        jnp.int32, (seq_count, local_rows), 1
    )
    valid_rows = (slot_ids < lengths[:, None]).astype(jnp.float32)
    grad_out = cotangent.astype(jnp.float32) * valid_rows[:, :, None]
    down_bias_grad = jnp.sum(grad_out, axis=(0, 1))
    grad_mlp = lax.all_gather(grad_out.astype(jnp.bfloat16), "tensor", axis=1, tiled=True)
    down_weight_grad = rows_product(activated, grad_mlp)
    grad_act = product_back(grad_mlp, down_weight)
    unused_act, gelu_back = jax.vjp(gelu_exact, pre_act)
    grad_pre = gelu_back(grad_act)[0].astype(jnp.bfloat16)
    up_bias_grad = jnp.sum(grad_pre.astype(jnp.float32), axis=(0, 1))
    up_weight_grad = rows_product(gathered_two, grad_pre)
    norm_two_grad = lax.psum_scatter(
        product_back(grad_pre, up_weight), "tensor", scatter_dimension=1, tiled=True
    )
    unused_two, norm_two_back = jax.vjp(layer_norm, hidden_state, ln2_gain, ln2_shift)
    hidden_ln_grad, ln2_gain_grad, ln2_shift_grad = norm_two_back(norm_two_grad)
    hidden_grad = grad_out + hidden_ln_grad
    out_bias_grad = jnp.sum(hidden_grad, axis=(0, 1))
    grad_attn = lax.all_gather(hidden_grad.astype(jnp.bfloat16), "tensor", axis=1, tiled=True)
    out_weight_grad = rows_product(mixed_heads, grad_attn)
    grad_heads = product_back(grad_attn, out_weight).astype(jnp.bfloat16).reshape(head_shape)
    grad_query, grad_key, grad_value = lax.map(
        lambda item: attend_backward(item[0], item[1], item[2], item[3], item[4], item[5]),
        (query_rows, key_rows, value_rows, grad_heads, log_totals, lengths),
    )
    flat_shape = (seq_count, slot_count, part_width)
    grad_query = grad_query.reshape(flat_shape).astype(jnp.bfloat16)
    grad_key = grad_key.reshape(flat_shape).astype(jnp.bfloat16)
    grad_value = grad_value.reshape(flat_shape).astype(jnp.bfloat16)
    qkv_weight_grad = jnp.stack(
        [
            score_scale * rows_product(gathered_one, grad_query),
            rows_product(gathered_one, grad_key),
            rows_product(gathered_one, grad_value),
        ]
    )
    qkv_bias_grad = jnp.stack(
        [
            score_scale * jnp.sum(grad_query.astype(jnp.float32), axis=(0, 1)),
            jnp.sum(grad_value.astype(jnp.float32), axis=(0, 1)),
        ]
    )
    norm_one_part = (
        score_scale * product_back(grad_query, qkv_weight[0])
        + product_back(grad_key, qkv_weight[1])
        + product_back(grad_value, qkv_weight[2])
    )
    norm_one_grad = lax.psum_scatter(norm_one_part, "tensor", scatter_dimension=1, tiled=True)
    unused_one, norm_one_back = jax.vjp(layer_norm, inputs, ln1_gain, ln1_shift)
    input_ln_grad, ln1_gain_grad, ln1_shift_grad = norm_one_back(norm_one_grad)
    input_grad = hidden_grad + input_ln_grad
    (
        qkv_weight_grad,
        qkv_bias_grad,
        out_weight_grad,
        up_weight_grad,
        up_bias_grad,
        down_weight_grad,
    ) = lax.psum(
        (
            qkv_weight_grad,
            qkv_bias_grad,
            out_weight_grad,
            up_weight_grad,
            up_bias_grad,
            down_weight_grad,
        ),
        "dp",
    )
    ln1_gain_grad, ln1_shift_grad, out_bias_grad, ln2_gain_grad, ln2_shift_grad, down_bias_grad = (
        lax.psum(
            (
                ln1_gain_grad,
                ln1_shift_grad,
                out_bias_grad,
                ln2_gain_grad,
                ln2_shift_grad,
                down_bias_grad,
            ),
            ("dp", "tensor"),
        )
    )
    return (
        output,
        input_grad,
        ln1_gain_grad,
        ln1_shift_grad,
        qkv_weight_grad,
        qkv_bias_grad,
        out_weight_grad,
        out_bias_grad,
        ln2_gain_grad,
        ln2_shift_grad,
        up_weight_grad,
        up_bias_grad,
        down_weight_grad,
        down_bias_grad,
    )


def solution(mesh):
    in_specs = (
        P("dp", "tensor", None),
        P("dp", "tensor", None),
        P("dp"),
        P(),
        P(),
        P(None, None, "tensor"),
        P(None, "tensor"),
        P("tensor", None),
        P(),
        P(),
        P(),
        P(None, "tensor"),
        P("tensor"),
        P("tensor", None),
        P(),
    )
    out_specs = (
        P("dp", "tensor", None),
        P("dp", "tensor", None),
        P(),
        P(),
        P(None, None, "tensor"),
        P(None, "tensor"),
        P("tensor", None),
        P(),
        P(),
        P(),
        P(None, "tensor"),
        P("tensor"),
        P("tensor", None),
        P(),
    )
    return jax.shard_map(body, mesh=mesh, in_specs=in_specs, out_specs=out_specs, check_vma=False)
```

profile of v0, /device:TPU:0, one launch (start us, length us, event | category | flops | bytes accessed | tf_op | source)
XLA Modules:
  0.0 1511.0 jit_solution(7519367030076174390)
XLA Ops:
  7.3 1.5 convert_reduce_fusion.1
  8.8 1.6 fusion.108
  10.5 2.7 fusion.106
  13.2 84.8 %all-gather.5.cloned.1.call-done = bf16[2,1024,2048]{2,1,0:T(8,128)(2,1)} async-done(((bf16[2,128,2048]{2,1,0:T(8,128)(2,1)}), bf16[2,1024,2048]{2,1,0:T(8,128)(2,1)}) %all-gather.5.cloned.1.call-update) | async-done | bytes 8388624 | tf_op jit(solution)/shard_map/all_gather | solution.py:131
  98.1 6.0 multiply_convert_fusion.3
  105.0 7.0 convolution_convert_fusion.3
  112.0 1.6 copy.39
  113.6 7.0 add_convert_fusion.3
  121.7 19.8 %while.26 = (s32[]{:T(128)}, bf16[2,1024,2,128]{1,3,2,0:T(8,128)(2,1)}, f32[2,2,1024,1]{2,1,3,0:T(2,128)S(1)}, bf16[2,1024,2,128]{1,3,2,0:T(8,128)(2,1)}, s32[2]...) while((s32[]{:T(128)}, ...), condition=%wide.region_7.8_spmd, body=%wide.region_2.7_spmd.sunk | while | flops 1093666304 | bytes 46220012 | solution.py:145
  125.4 2.2 exponential_reduce_fusion.3
  129.0 1.3 fusion.199
  135.0 2.2 exponential_reduce_fusion.3
  138.6 1.3 fusion.199
  141.5 7.4 convolution_convert_fusion.1
  149.0 88.2 %reduce-scatter.5.cloned.1.call-done = bf16[2,128,2048]{2,1,0:T(8,128)(2,1)} async-done(((bf16[2,1024,2048]{2,1,0:T(8,128)(2,1)}), bf16[2,128,2048]{2,1,0:T(8,128)(2,1)}) %reduce-scatter.5.cloned.1.call-update) | async-done | bytes 1048592 | tf_op jit(solution)/shard_map/reduce_scatter | solution.py:150
  237.3 1.7 fusion.116
  239.0 1.8 multiply_reduce_fusion.4
  240.9 1.7 add_convert_fusion.2
  242.7 2.4 fusion.112
  245.2 77.9 %all-gather.7.cloned.1.call-done = bf16[2,1024,2048]{2,1,0:T(8,128)(2,1)} async-done(((bf16[2,128,2048]{2,1,0:T(8,128)(2,1)}), bf16[2,1024,2048]{2,1,0:T(8,128)(2,1)}) %all-gather.7.cloned.1.call-update) | async-done | bytes 8388624 | tf_op jit(solution)/shard_map/all_gather | solution.py:158
  323.1 15.6 %fusion.114 = (u8[1024,1024]{1,0:T(8,128)(4,1)S(1)}, u8[1024,1024]{1,0:T(8,128)(4,1)S(1)}, f32[2,1024,1024]{2,1,0:T(8,128)S(1)}) fusion(f32[1024]{0:T(1024)S(1)} %copy-done.47, bf16[2,1024,2048]{2,1,0:T(8,128)(2,1)} %all-gather.7.cloned.1.call-done, bf16[2048,1024]{1,0:T(8,128)(2,1)} %param.30), kind=kOutput, calls=%fused_computation.186 | convolution fusion | flops 8617197568 | bytes 23072768 | tf_op jit(solution)/shard_map/dot_general | solution.py:25
  338.7 3.4 copy-done.20
  342.1 20.5 %multiply_convert_fusion.2 = (bf16[2,1024,1024]{2,1,0:T(8,128)(2,1)}, f32[2,1024,1024]{2,1,0:T(8,128)}) fusion(f32[2,1024,1024]{2,1,0:T(8,128)S(1)} %get-tuple-element.211, f32[1024]{0:T(1024)S(1)} %copy-done.47, u8[1024,1024]{1,0:T(8,128)(4,1)S(1)} %get-tuple-element.129, u8[1024,1024]{1,0:T(8,128)(4,1)S(1)} %get-tuple-element.128), kind=kLoop, calls=%fused_computation.124 | loop fusion | flops 148897792 | bytes 23072768 | tf_op jit(solution)/shard_map/convert_element_type | solution.py:160
  362.7 43.1 %all-gather.9.cloned.1.call-done = bf16[2,1024,2048]{2,1,0:T(8,128)(2,1)} async-done(((bf16[2,128,2048]{2,1,0:T(8,128)(2,1)}), bf16[2,1024,2048]{2,1,0:T(8,128)(2,1)}) %all-gather.9.cloned.1.call-update) | async-done | bytes 8388624 | tf_op jit(solution)/shard_map/all_gather | solution.py:174
  405.7 21.1 %convert_reduce_fusion = (f32[1024]{0:T(1024)}, bf16[2,1024,1024]{2,1,0:T(8,128)(2,1)S(1)}) fusion(f32[2,1024,1024]{2,1,0:T(8,128)} %get-tuple-element.188, bf16[2,1024,2048]{2,1,0:T(8,128)(2,1)} %all-gather.9.cloned.1.call-done, bf16[1024,2048]{1,0:T(8,128)(2,1)} %param.32, f32[2,1024,1024]{2,1,0:T(8,128)} %copy-done.20, f32[1024]{0:T(1024)S(1)} %copy-done.47), kind=kOutput, calls=%fused_computation.122 | convolution fusion | flops 8625585152 | bytes 33562624 | tf_op jit(solution)/shard_map/dot_general | solution.py:31
  426.9 2.0 copy-done.52
  428.9 11.7 fusion.93
  440.7 14.1 convolution_convert_fusion
  454.9 152.7 %reduce-scatter.9.cloned.1.call-done = f32[2,128,2048]{2,1,0:T(8,128)} async-done(((f32[2,1024,2048]{2,1,0:T(8,128)}), f32[2,128,2048]{2,1,0:T(8,128)}) %reduce-scatter.9.cloned.1.call-update) | async-done | bytes 2097168 | tf_op jit(solution)/shard_map/reduce_scatter | solution.py:181
  607.6 3.5 multiply_reduce_fusion.2
  611.1 87.2 %reduce-scatter.7.cloned.1.call-done = bf16[2,128,2048]{2,1,0:T(8,128)(2,1)} async-done(((bf16[2,1024,2048]{2,1,0:T(8,128)(2,1)}), bf16[2,128,2048]{2,1,0:T(8,128)(2,1)}) %reduce-scatter.7.cloned.1.call-update) | async-done | bytes 1048592 | tf_op jit(solution)/shard_map/reduce_scatter | solution.py:161
  698.3 4.3 fusion.139
  703.9 1.3 fusion.135
  705.3 80.5 %all-gather.11.cloned.1.call-done = bf16[2,1024,2048]{2,1,0:T(8,128)(2,1)} async-done(((bf16[2,128,2048]{2,1,0:T(8,128)(2,1)}), bf16[2,1024,2048]{2,1,0:T(8,128)(2,1)}) %all-gather.11.cloned.1.call-update) | async-done | bytes 8388624 | tf_op jit(solution)/shard_map/all_gather | solution.py:188
  785.8 6.7 convolution_convert_fusion.2
  795.8 34.2 %while.27 = (s32[]{:T(128)}, bf16[2,1024,2,128]{1,3,2,0:T(8,128)(2,1)}, bf16[2,1024,2,128]{1,3,2,0:T(8,128)(2,1)}, bf16[2,1024,2,128]{1,3,2,0:T(8,128)(2,1)}, bf...) while((s32[]{:T(128)}, ...), condition=%wide.region_18.19_spmd, body=%wide.region_15.18_spmd.sunk | while | flops 2713189888 | bytes 113858456 | solution.py:191
  800.8 1.4 fusion.219
  802.2 1.7 multiply_reduce_fusion.7
  803.9 1.7 multiply_reduce_fusion.8
  805.6 2.3 multiply_convert_fusion.5
  817.6 1.3 fusion.219
  819.0 1.7 multiply_reduce_fusion.7
  820.7 1.7 multiply_reduce_fusion.8
  822.4 2.3 multiply_convert_fusion.5
  830.0 9.8 fusion.120
  839.8 9.5 fusion.117
  849.3 18.5 %add_add_fusion = f32[2,1024,2048]{2,1,0:T(8,128)} fusion(f32[2,1024,2048]{2,1,0:T(8,128)} %fusion.117, f32[2,1024,2048]{2,1,0:T(8,128)} %fusion.120, bf16[2,1024,256]{1,2,0:T(8,128)(2,1)S(1)} %bitcast.299, bf16[3,2048,256]{2,1,0:T(8,128)(2,1)} %param.24), kind=kOutput, calls=%fused_computation.114 | convolution fusion | flops 2160066560 | bytes 52428800 | tf_op jit(solution)/shard_map/dot_general | solution.py:31
  867.8 14.9 convolution_bitcast_fusion.3
  882.8 13.8 convolution_bitcast_fusion.2
  896.6 6.2 convolution_bitcast_fusion.5
  902.9 6.3 convolution_bitcast_fusion.6
  909.2 2.7 fusion.102
  911.9 3.1 pad_maximum_fusion
  915.1 3.8 convolution_bitcast_fusion.4
  919.5 10.9 all-reduce.1
  930.4 104.3 %reduce-scatter.11.cloned.1.call-done = f32[2,128,2048]{2,1,0:T(8,128)} async-done(((f32[2,1024,2048]{2,1,0:T(8,128)}), f32[2,128,2048]{2,1,0:T(8,128)}) %reduce-scatter.11.cloned.1.call-update) | async-done | bytes 2097168 | tf_op jit(solution)/shard_map/reduce_scatter | solution.py:217
  1034.7 2.3 fusion.138
  1038.0 4.2 fusion.111
  1042.2 39.5 %all-reduce = (f32[2048]{0:T(1024)}, f32[2048]{0:T(1024)}, f32[2048]{0:T(1024)}, f32[2048]{0:T(1024)}, f32[2048]{0:T(1024)}, /*index=5*/f32[2048]{0:T(1024)}) all-reduce(f32[2048]{0:T(1024)S(1)} %get-tuple-element.132, f32[2048]{0:T(1024)S(1)} %get-tuple-element.135, ...), channel_id=1, replica_groups=mesh['dp'=4,'tensor'=8] {'dp','tensor'}, use_global_device_ids=true, to_apply=%region_23.24 | all-reduce | flops 12288 | bytes 98304 | tf_op jit(solution)/shard_map/psum | solution.py:240
  1081.7 404.7 %all-reduce.5.cloned.1.call-done = (f32[3,2048,256]{2,1,0:T(8,128)}, f32[256,2048]{1,0:T(8,128)}, f32[2048,1024]{1,0:T(8,128)}, f32[1024,2048]{1,0:T(8,128)}) async-done(((f32[3,2048,256]{2,1,0:T(8,128)}, f32[256,2048]{1,0:T(8,128)}, f32[2048,1024]{1,0:T(8,128)}, f32[1024,2048]{1,0:T(8,128)}), (f32[3,2048,256]{2,1,0:T(8,128)}, f32[256,2048]{1,0:T(8,128)}, f32[2048,1024]{1,0:T(8,128)}, ...) | async-done | bytes 25165840 | tf_op jit(solution)/shard_map/psum | solution.py:228
  1486.4 6.6 copy.120
  1495.2 4.3 copy.122
  1499.5 1.3 slice-done.1
  1500.8 3.4 copy.123
  (230 shorter events, 42.3 us)
Async XLA Ops:
  7.2 134.4 %copy-start = (bf16[256,2048]{1,0:T(8,128)(2,1)S(1)}, bf16[256,2048]{1,0:T(8,128)(2,1)}, u32[]{:S(2)}) copy-start(bf16[256,2048]{1,0:T(8,128)(2,1)} %param.26) | copy-start | bytes 3145732
  7.2 6.0 copy-start.49
  7.2 90.9 %all-gather.5.cloned.1.call-start = ((), (), s32[]{:S(2)}) async-start(), calls=%async_computation.4 | async-start | bytes 9437184 | tf_op jit(solution)/shard_map/all_gather | solution.py:131
  8.8 89.3 %copy-start.33 = (f32[2,128]{1,0:T(2,128)}, f32[2,128]{1,0:T(2,128)S(1)}, u32[]{:S(2)}) copy-start(f32[2,128]{1,0:T(2,128)S(1)} %broadcast_multiply_fusion.2) | copy-start | bytes 3076
  10.4 87.6 %copy-start.41 = (f32[2,128]{1,0:T(2,128)}, f32[2,128]{1,0:T(2,128)S(1)}, u32[]{:S(2)}) copy-start(f32[2,128]{1,0:T(2,128)S(1)} %fusion.108) | copy-start | bytes 3076
  10.5 87.6 %copy-start.37 = (f32[2,128]{1,0:T(2,128)}, f32[2,128]{1,0:T(2,128)S(1)}, u32[]{:S(2)}) copy-start(f32[2,128]{1,0:T(2,128)S(1)} %fusion.136) | copy-start | bytes 3076
  13.2 224.1 %reduce-scatter.5.cloned.1.call-start = ((), (), s32[]{:S(2)}) async-start(), calls=%async_computation.5 | async-start | bytes 9437184 | tf_op jit(solution)/shard_map/reduce_scatter | solution.py:150
  113.6 8.1 copy-start.50
  125.3 2.2 copy-start.6
  128.9 1.4 copy-start.25
  135.0 2.2 copy-start.6
  141.5 7.4 copy-start.4
  148.9 88.3 %copy-start.2 = (bf16[2,128,2048]{2,1,0:T(8,128)(2,1)S(1)}, bf16[2,128,2048]{2,1,0:T(8,128)(2,1)}, u32[]{:S(2)}) copy-start(bf16[2,128,2048]{2,1,0:T(8,128)(2,1)} %param.19) | copy-start | bytes 3145732
  148.9 88.3 %copy-start.30 = (f32[2048]{0:T(1024)S(1)}, f32[2048]{0:T(1024)}, u32[]{:S(2)}) copy-start(f32[2048]{0:T(1024)} %param.27) | copy-start | bytes 24580
  149.0 91.9 %copy-start.32 = (f32[2048]{0:T(1024)S(1)}, f32[2048]{0:T(1024)}, u32[]{:S(2)}) copy-start(f32[2048]{0:T(1024)} %param.28) | copy-start | bytes 24580
  149.0 91.9 %copy-start.45 = (f32[2048]{0:T(1024)S(1)}, f32[2048]{0:T(1024)}, u32[]{:S(2)}) copy-start(f32[2048]{0:T(1024)} %param.29) | copy-start | bytes 24580
  149.0 174.1 %all-gather.7.cloned.1.call-start = ((), (), s32[]{:S(2)}) async-start(), calls=%async_computation.6 | async-start | bytes 9437184 | tf_op jit(solution)/shard_map/all_gather | solution.py:158
  237.3 3.6 copy-start.9
  240.8 82.3 %copy-start.47 = (f32[1024]{0:T(1024)S(1)}, f32[1024]{0:T(1024)}, u32[]{:S(2)}) copy-start(f32[1024]{0:T(1024)} %param.31) | copy-start | bytes 12292
  242.5 163.2 %all-gather.9.cloned.1.call-start = ((), (), s32[]{:S(2)}) async-start(), calls=%async_computation.8 | async-start | bytes 9437184 | tf_op jit(solution)/shard_map/all_gather | solution.py:174
  242.7 459.9 %copy-start.39 = (f32[2,128]{1,0:T(2,128)}, f32[2,128]{1,0:T(2,128)S(1)}, u32[]{:S(2)}) copy-start(f32[2,128]{1,0:T(2,128)S(1)} %compare_convert_fusion) | copy-start | bytes 3076
  245.1 362.4 %reduce-scatter.9.cloned.1.call-start = ((), (), s32[]{:S(2)}) async-start(), calls=%async_computation.9 | async-start | bytes 18874368 | tf_op jit(solution)/shard_map/reduce_scatter | solution.py:181
  338.7 3.4 copy-start.20
  405.7 23.2 %copy-start.51 = (bf16[2048,1024]{1,0:T(8,128)(2,1)S(1)}, bf16[2048,1024]{1,0:T(8,128)(2,1)}, u32[]{:S(2)}) copy-start(bf16[2048,1024]{1,0:T(8,128)(2,1)} %param.30) | copy-start | bytes 12582916
  426.9 2.0 copy-start.52
  440.6 257.7 %reduce-scatter.7.cloned.1.call-start = ((), (), s32[]{:S(2)}) async-start(), calls=%async_computation.7 | async-start | bytes 9437184 | tf_op jit(solution)/shard_map/reduce_scatter | solution.py:161
  454.8 243.5 %copy-start.46 = (f32[2048]{0:T(1024)S(1)}, f32[2048]{0:T(1024)}, u32[]{:S(2)}) copy-start(f32[2048]{0:T(1024)} %param.33) | copy-start | bytes 24580
  454.8 330.9 %all-gather.11.cloned.1.call-start = ((), (), s32[]{:S(2)}) async-start(), calls=%async_computation.10 | async-start | bytes 9437184 | tf_op jit(solution)/shard_map/all_gather | solution.py:188
  698.3 5.6 copy-start.18
  702.6 90.0 %copy-start.43 = (f32[2,128]{1,0:T(2,128)}, f32[2,128]{1,0:T(2,128)S(1)}, u32[]{:S(2)}) copy-start(f32[2,128]{1,0:T(2,128)S(1)} %negate_multiply_fusion.2) | copy-start | bytes 3076
  705.2 329.5 %reduce-scatter.11.cloned.1.call-start = ((), (), s32[]{:S(2)}) async-start(), calls=%async_computation.11 | async-start | bytes 18874368 | tf_op jit(solution)/shard_map/reduce_scatter | solution.py:217
  705.3 90.5 %copy-start.5 = (bf16[2,1024,2,128]{3,1,2,0:T(8,128)(2,1)S(1)}, bf16[2,1024,2,128]{3,1,2,0:T(8,128)(2,1)}, u32[]{:S(2)}) copy-start(bf16[2,1024,2,128]{3,1,2,0:T(8,128)(2,1)} %copy-done.4) | copy-start | bytes 3145732
  798.0 1.4 copy-start.8
  802.2 1.7 copy-start.13
  807.9 2.2 copy-start.22
  814.8 1.4 copy-start.8
  819.0 1.7 copy-start.13
  824.7 2.2 copy-start.22
  830.0 9.8 copy-start.24
  839.8 9.5 copy-start.14
  867.8 618.6 %all-reduce.5.cloned.1.call-start = ((), (), s32[]{:S(2)}) async-start(), calls=%async_computation.12 | async-start | bytes 50331648 | tf_op jit(solution)/shard_map/psum | solution.py:228
  867.8 15.0 copy-start.28
  896.6 12.5 slice-start.2
  902.8 6.3 copy-start.17
  902.8 6.3 slice-start.3
  902.8 12.2 slice-start.4
  909.2 5.9 slice-start.5
  911.9 3.1 copy-start.27
  918.8 115.9 %copy-start.3 = (bf16[2,128,2048]{2,1,0:T(8,128)(2,1)S(1)}, bf16[2,128,2048]{2,1,0:T(8,128)(2,1)}, u32[]{:S(2)}) copy-start(bf16[2,128,2048]{2,1,0:T(8,128)(2,1)} %param.19) | copy-start | bytes 3145732
  918.8 115.9 %copy-start.31 = (f32[2048]{0:T(1024)S(1)}, f32[2048]{0:T(1024)}, u32[]{:S(2)}) copy-start(f32[2048]{0:T(1024)} %param.22) | copy-start | bytes 24580
  918.8 115.9 %copy-start.34 = (f32[2,128]{1,0:T(2,128)S(1)}, f32[2,128]{1,0:T(2,128)}, u32[]{:S(2)}) copy-start(f32[2,128]{1,0:T(2,128)} %copy-done.33) | copy-start | bytes 3076
  918.9 118.1 %copy-start.42 = (f32[2,128]{1,0:T(2,128)S(1)}, f32[2,128]{1,0:T(2,128)}, u32[]{:S(2)}) copy-start(f32[2,128]{1,0:T(2,128)} %copy-done.41) | copy-start | bytes 3076
  918.9 118.2 %copy-start.38 = (f32[2,128]{1,0:T(2,128)S(1)}, f32[2,128]{1,0:T(2,128)}, u32[]{:S(2)}) copy-start(f32[2,128]{1,0:T(2,128)} %copy-done.37) | copy-start | bytes 3076
  918.9 119.1 %copy-start.40 = (f32[2,128]{1,0:T(2,128)S(1)}, f32[2,128]{1,0:T(2,128)}, u32[]{:S(2)}) copy-start(f32[2,128]{1,0:T(2,128)} %copy-done.39) | copy-start | bytes 3076
  918.9 119.1 %copy-start.44 = (f32[2,128]{1,0:T(2,128)S(1)}, f32[2,128]{1,0:T(2,128)}, u32[]{:S(2)}) copy-start(f32[2,128]{1,0:T(2,128)} %copy-done.43) | copy-start | bytes 3076
  919.3 118.7 %copy-start.19 = (bf16[2,128,2048]{2,1,0:T(8,128)(2,1)S(1)}, bf16[2,128,2048]{2,1,0:T(8,128)(2,1)}, u32[]{:S(2)}) copy-start(bf16[2,128,2048]{2,1,0:T(8,128)(2,1)} %param.20) | copy-start | bytes 3145732
  1034.7 2.3 copy-start.11
  1038.0 4.2 copy-start.35
  1038.0 4.2 copy-start.36
  1486.4 6.6 copy-start.29
  1486.4 8.9 copy-start.21
  1492.9 6.6 slice-start
  1495.2 5.6 slice-start.1
  1500.8 3.4 copy-start.1
  (15 other events, 17.1 us)
Sparse Core Ops, SparseCore 0:
  13.3 84.7 all-gather.4
  149.1 88.1 reduce-scatter.4
  242.7 80.3 all-gather.6
  325.1 80.5 all-gather.8
  440.7 166.7 reduce-scatter.8
  610.3 87.9 reduce-scatter.6
  705.4 80.3 all-gather.10
  867.9 166.7 reduce-scatter.10
  1039.8 446.4 all-reduce.4
where the time goes:
time: 1510 us
  waiting for transfers between devices  1120 us (74%)
  matrix products  211 us (14%)
  other arithmetic  68.2 us (5%)
  blocking collectives  50.4 us (3%)
  local copies, waits for them, and re-layouts  40.6 us (3%)
    psum x1, waiting for transfers between devices, body(): lax.psum((qkv_weight_grad, qkv_bias_grad, out_weight_grad, up_weight_grad...  405 us
    reduce_scatter x1, waiting for transfers between devices, body(): lax.psum_scatter(product_back(grad_pre, up_weight), 'tensor', scatter_dim...  153 us
    reduce_scatter x1, waiting for transfers between devices, body(): lax.psum_scatter(norm_one_part, 'tensor', scatter_dimension=1, tiled=True)  104 us
    reduce_scatter x1, waiting for transfers between devices, body(): lax.psum_scatter(flat_product(mixed_heads, out_weight).astype(jnp.bfloat1...  88.2 us
    reduce_scatter x1, waiting for transfers between devices, body(): lax.psum_scatter(flat_product(activated, down_weight).astype(jnp.bfloat16...  87.2 us
    all_gather x1, waiting for transfers between devices, body(): gathered_one = lax.all_gather(normed_one, 'tensor', axis=1, tiled=True)  84.8 us
    all_gather x1, waiting for transfers between devices, body(): lax.all_gather(hidden_grad.astype(jnp.bfloat16), 'tensor', axis=1, tiled=...  80.5 us
    all_gather x1, waiting for transfers between devices, body(): gathered_two = lax.all_gather(normed_two, 'tensor', axis=1, tiled=True)  77.9 us
  transfers between devices with their start and end apart: 9, of which 9 were waited for; matrix products, arithmetic and copies ran while one was open for 8% of the time, Pallas kernels for 0%

commit v1 on v0

--- a/solution.py
+++ b/solution.py
@@ -40,6 +40,10 @@
     return lax.dot_general(
         left_flat, right_flat, (((0,), (0,)), ((), ())), preferred_element_type=jnp.float32
     )
+
+
+def sum_groups(part):
+    return lax.psum(part.astype(jnp.bfloat16), "dp").astype(jnp.float32)
 
 
 def allowed_mask(first_row, row_count, slot_count, length):
@@ -172,15 +176,18 @@
     grad_out = cotangent.astype(jnp.float32) * valid_rows[:, :, None]
     down_bias_grad = jnp.sum(grad_out, axis=(0, 1))
     grad_mlp = lax.all_gather(grad_out.astype(jnp.bfloat16), "tensor", axis=1, tiled=True)
-    down_weight_grad = rows_product(activated, grad_mlp)
+    down_weight_grad = sum_groups(rows_product(activated, grad_mlp))
     grad_act = product_back(grad_mlp, down_weight)
     unused_act, gelu_back = jax.vjp(gelu_exact, pre_act)
     grad_pre = gelu_back(grad_act)[0].astype(jnp.bfloat16)
     up_bias_grad = jnp.sum(grad_pre.astype(jnp.float32), axis=(0, 1))
-    up_weight_grad = rows_product(gathered_two, grad_pre)
+    up_weight_grad = sum_groups(rows_product(gathered_two, grad_pre))
     norm_two_grad = lax.psum_scatter(
-        product_back(grad_pre, up_weight), "tensor", scatter_dimension=1, tiled=True
-    )
+        product_back(grad_pre, up_weight).astype(jnp.bfloat16),
+        "tensor",
+        scatter_dimension=1,
+        tiled=True,
+    ).astype(jnp.float32)
     unused_two, norm_two_back = jax.vjp(layer_norm, hidden_state, ln2_gain, ln2_shift)
     hidden_ln_grad, ln2_gain_grad, ln2_shift_grad = norm_two_back(norm_two_grad)
     hidden_grad = grad_out + hidden_ln_grad
@@ -203,6 +210,11 @@
             rows_product(gathered_one, grad_value),
         ]
     )
+    qkv_weight_grad, out_weight_grad, up_weight_grad, down_weight_grad = lax.optimization_barrier(
+        (qkv_weight_grad, out_weight_grad, up_weight_grad, down_weight_grad)
+    )
+    qkv_weight_grad = sum_groups(qkv_weight_grad)
+    out_weight_grad = sum_groups(out_weight_grad)
     qkv_bias_grad = jnp.stack(
         [
             score_scale * jnp.sum(grad_query.astype(jnp.float32), axis=(0, 1)),
@@ -214,28 +226,13 @@
         + product_back(grad_key, qkv_weight[1])
         + product_back(grad_value, qkv_weight[2])
     )
-    norm_one_grad = lax.psum_scatter(norm_one_part, "tensor", scatter_dimension=1, tiled=True)
+    norm_one_grad = lax.psum_scatter(
+        norm_one_part.astype(jnp.bfloat16), "tensor", scatter_dimension=1, tiled=True
+    ).astype(jnp.float32)
     unused_one, norm_one_back = jax.vjp(layer_norm, inputs, ln1_gain, ln1_shift)
     input_ln_grad, ln1_gain_grad, ln1_shift_grad = norm_one_back(norm_one_grad)
     input_grad = hidden_grad + input_ln_grad
-    (
-        qkv_weight_grad,
-        qkv_bias_grad,
-        out_weight_grad,
-        up_weight_grad,
-        up_bias_grad,
-        down_weight_grad,
-    ) = lax.psum(
-        (
-            qkv_weight_grad,
-            qkv_bias_grad,
-            out_weight_grad,
-            up_weight_grad,
-            up_bias_grad,
-            down_weight_grad,
-        ),
-        "dp",
-    )
+    qkv_bias_grad, up_bias_grad = lax.psum((qkv_bias_grad, up_bias_grad), "dp")
     ln1_gain_grad, ln1_shift_grad, out_bias_grad, ln2_gain_grad, ln2_shift_grad, down_bias_grad = (
         lax.psum(
             (

time: 1510 us -> 1150 us (0.76)
  waiting for transfers between devices: 1120 us -> 766 us
  local copies, waits for them, and re-layouts: 40.6 us -> 21.9 us
  other arithmetic: 68.2 us -> 86.7 us
    psum x1 -> x2, waiting for transfers between devices: 405 us -> 208 us  [sum_groups(): return lax.psum(part.astype(jnp.bfloat16), 'dp').astype(jnp.float32)]
    reduce_scatter x2, waiting for transfers between devices: 257 us -> 146 us  [the longest x1 85.6 us: body(): lax.psum_scatter(norm_one_part.astype(jnp.bfloat16), 'tensor', scatter_di...]
    reduce_scatter x1, waiting for transfers between devices: 87.2 us -> 43.9 us  [body(): lax.psum_scatter(flat_product(activated, down_weight).astype(jnp.bfloat16...]
    unnamed x100 -> x108, local copies, waits for them, and re-layouts: 25 us -> 6.49 us
    convert_element_type x0 -> x4, other arithmetic: none -> 17.5 us  [sum_groups(): return lax.psum(part.astype(jnp.bfloat16), 'dp').astype(jnp.float32)]
  transfers between devices with their start and end apart: 9 -> 10, of which waited for: 9 -> 10; matrix products, arithmetic and copies ran while one was open for 8% -> 13% of each run, Pallas kernels for 0% -> 0%
where the time goes in v1:
time: 1150 us
  waiting for transfers between devices  766 us (67%)
  matrix products  206 us (18%)
  other arithmetic  86.7 us (8%)
  blocking collectives  52.1 us (5%)
  local copies, waits for them, and re-layouts  21.9 us (2%)
  between operations  15.1 us (1%)
    psum x2, waiting for transfers between devices, sum_groups(): return lax.psum(part.astype(jnp.bfloat16), 'dp').astype(jnp.float32)  208 us
    reduce_scatter x1, waiting for transfers between devices, body(): lax.psum_scatter(flat_product(mixed_heads, out_weight).astype(jnp.bfloat1...  88.2 us
    reduce_scatter x1, waiting for transfers between devices, body(): lax.psum_scatter(norm_one_part.astype(jnp.bfloat16), 'tensor', scatter_di...  85.6 us
    all_gather x1, waiting for transfers between devices, body(): gathered_one = lax.all_gather(normed_one, 'tensor', axis=1, tiled=True)  84.8 us
    all_gather x1, waiting for transfers between devices, body(): gathered_two = lax.all_gather(normed_two, 'tensor', axis=1, tiled=True)  77.9 us
    dot_general x6, matrix products, product_back(): lax.dot_general(flat, right_rows, (((1,), (1,)), ((), ())), preferred_ele...  74.2 us
    all_gather x1, waiting for transfers between devices, body(): lax.all_gather(hidden_grad.astype(jnp.bfloat16), 'tensor', axis=1, tiled=...  73.7 us
    reduce_scatter x1, waiting for transfers between devices, body(): lax.psum_scatter(product_back(grad_pre, up_weight).astype(jnp.bfloat16),...  60.7 us
  transfers between devices with their start and end apart: 10, of which 10 were waited for; matrix products, arithmetic and copies ran while one was open for 13% of the time, Pallas kernels for 0%

profile of v1, /device:TPU:0, one launch (start us, length us, event | category | flops | bytes accessed | tf_op | source)
XLA Modules:
  0.0 1150.2 jit_solution(2478492900703800159)
XLA Ops:
  7.3 1.5 convert_reduce_fusion.3
  8.8 1.6 fusion.109
  10.5 2.7 fusion.107
  13.2 84.8 %all-gather.5.cloned.1.call-done = bf16[2,1024,2048]{2,1,0:T(8,128)(2,1)} async-done(((bf16[2,128,2048]{2,1,0:T(8,128)(2,1)}), bf16[2,1024,2048]{2,1,0:T(8,128)(2,1)}) %all-gather.5.cloned.1.call-update) | async-done | bytes 8388624 | tf_op jit(solution)/shard_map/all_gather | solution.py:135
  98.1 6.0 multiply_convert_fusion.3
  105.0 7.0 convolution_convert_fusion.4
  112.0 1.6 copy.39
  113.6 7.0 add_convert_fusion.4
  121.8 19.8 %while.26 = (s32[]{:T(128)}, bf16[2,1024,2,128]{1,3,2,0:T(8,128)(2,1)}, f32[2,2,1024,1]{2,1,3,0:T(2,128)S(1)}, bf16[2,1024,2,128]{1,3,2,0:T(8,128)(2,1)}, s32[2]...) while((s32[]{:T(128)}, ...), condition=%wide.region_7.8_spmd, body=%wide.region_2.7_spmd.sunk | while | flops 1093666304 | bytes 46220012 | solution.py:149
  125.4 2.2 exponential_reduce_fusion.3
  135.1 2.2 exponential_reduce_fusion.3
  141.6 7.4 convolution_convert_fusion.2
  149.1 88.2 %reduce-scatter.5.cloned.1.call-done = bf16[2,128,2048]{2,1,0:T(8,128)(2,1)} async-done(((bf16[2,1024,2048]{2,1,0:T(8,128)(2,1)}), bf16[2,128,2048]{2,1,0:T(8,128)(2,1)}) %reduce-scatter.5.cloned.1.call-update) | async-done | bytes 1048592 | tf_op jit(solution)/shard_map/reduce_scatter | solution.py:154
  237.3 1.7 fusion.119
  239.1 1.8 multiply_reduce_fusion.2
  240.9 1.7 add_convert_fusion.3
  242.7 2.4 fusion.115
  245.3 77.9 %all-gather.7.cloned.1.call-done = bf16[2,1024,2048]{2,1,0:T(8,128)(2,1)} async-done(((bf16[2,128,2048]{2,1,0:T(8,128)(2,1)}), bf16[2,1024,2048]{2,1,0:T(8,128)(2,1)}) %all-gather.7.cloned.1.call-update) | async-done | bytes 8388624 | tf_op jit(solution)/shard_map/all_gather | solution.py:162
  323.2 15.6 %fusion.117 = (u8[1024,1024]{1,0:T(8,128)(4,1)S(1)}, u8[1024,1024]{1,0:T(8,128)(4,1)S(1)}, f32[2,1024,1024]{2,1,0:T(8,128)S(1)}) fusion(f32[1024]{0:T(1024)S(1)} %copy-done.55, bf16[2,1024,2048]{2,1,0:T(8,128)(2,1)} %all-gather.7.cloned.1.call-done, bf16[2048,1024]{1,0:T(8,128)(2,1)} %param.30), kind=kOutput, calls=%fused_computation.194 | convolution fusion | flops 8617197568 | bytes 23072768 | tf_op jit(solution)/shard_map/dot_general | solution.py:25
  338.8 3.4 copy-done.21
  342.2 20.5 %multiply_convert_fusion.2 = (bf16[2,1024,1024]{2,1,0:T(8,128)(2,1)}, f32[2,1024,1024]{2,1,0:T(8,128)}) fusion(f32[2,1024,1024]{2,1,0:T(8,128)S(1)} %get-tuple-element.218, f32[1024]{0:T(1024)S(1)} %copy-done.55, u8[1024,1024]{1,0:T(8,128)(4,1)S(1)} %get-tuple-element.137, u8[1024,1024]{1,0:T(8,128)(4,1)S(1)} %get-tuple-element.136), kind=kLoop, calls=%fused_computation.126 | loop fusion | flops 148897792 | bytes 23072768 | tf_op jit(solution)/shard_map/convert_element_type | solution.py:164
  362.8 43.1 %all-gather.9.cloned.1.call-done = bf16[2,1024,2048]{2,1,0:T(8,128)(2,1)} async-done(((bf16[2,128,2048]{2,1,0:T(8,128)(2,1)}), bf16[2,1024,2048]{2,1,0:T(8,128)(2,1)}) %all-gather.9.cloned.1.call-update) | async-done | bytes 8388624 | tf_op jit(solution)/shard_map/all_gather | solution.py:178
  405.8 21.1 %convert_reduce_fusion = (f32[1024]{0:T(1024)}, bf16[2,1024,1024]{2,1,0:T(8,128)(2,1)S(1)}) fusion(f32[2,1024,1024]{2,1,0:T(8,128)} %get-tuple-element.195, bf16[2,1024,2048]{2,1,0:T(8,128)(2,1)} %all-gather.9.cloned.1.call-done, bf16[1024,2048]{1,0:T(8,128)(2,1)} %param.32, f32[2,1024,1024]{2,1,0:T(8,128)} %copy-done.21, f32[1024]{0:T(1024)S(1)} %copy-done.55), kind=kOutput, calls=%fused_computation.124 | convolution fusion | flops 8625585152 | bytes 33562624 | tf_op jit(solution)/shard_map/dot_general | solution.py:31
  427.0 2.0 copy-done.60
  429.0 10.9 convolution_convert_fusion
  440.0 14.4 %bitcast_convert_fusion.1 = bf16[2048,1024]{1,0:T(8,128)(2,1)} fusion(bf16[2,1024,2048]{2,1,0:T(8,128)(2,1)} %all-gather.7.cloned.1.call-done, bf16[2,1024,1024]{2,1,0:T(8,128)(2,1)} %copy-done.60), kind=kOutput, calls=%fused_computation.123 | convolution fusion | flops 8592031744 | bytes 16777216 | tf_op jit(solution)/shard_map/dot_general | solution.py:40
  454.3 13.1 %bitcast_convert_fusion = bf16[1024,2048]{1,0:T(8,128)(2,1)} fusion(bf16[2,1024,1024]{2,1,0:T(8,128)(2,1)S(1)} %copy-done.29, bf16[2,1024,2048]{2,1,0:T(8,128)(2,1)} %all-gather.9.cloned.1.call-done), kind=kOutput, calls=%fused_computation.122 | convolution fusion | flops 8592031744 | bytes 16777216 | tf_op jit(solution)/shard_map/dot_general | solution.py:40
  467.5 60.7 %reduce-scatter.9.cloned.1.call-done = bf16[2,128,2048]{2,1,0:T(8,128)(2,1)} async-done(((bf16[2,1024,2048]{2,1,0:T(8,128)(2,1)}), bf16[2,128,2048]{2,1,0:T(8,128)(2,1)}) %reduce-scatter.9.cloned.1.call-update) | async-done | bytes 1048592 | tf_op jit(solution)/shard_map/reduce_scatter | solution.py:185
  528.2 3.1 convert_reduce_fusion.2
  531.3 2.5 fusion.131
  534.4 2.1 fusion.141
  537.0 166.4 %all-reduce.9.cloned.1.call-done = (bf16[2048,1024]{1,0:T(8,128)(2,1)}, bf16[1024,2048]{1,0:T(8,128)(2,1)}) async-done(((bf16[2048,1024]{1,0:T(8,128)(2,1)}, bf16[1024,2048]{1,0:T(8,128)(2,1)}), (bf16[2048,1024]{1,0:T(8,128)(2,1)}, bf16[1024,2048]{1,0:T(8,128)(2,1)})) %all-reduce.9.cloned.1.call-update) | async-done | bytes 8388624 | tf_op jit(solution)/shard_map/psum | solution.py:46
  703.4 6.8 convert_element_type.191
  710.2 4.6 convert_element_type.193
  714.8 73.7 %all-gather.11.cloned.1.call-done = bf16[2,1024,2048]{2,1,0:T(8,128)(2,1)} async-done(((bf16[2,128,2048]{2,1,0:T(8,128)(2,1)}), bf16[2,1024,2048]{2,1,0:T(8,128)(2,1)}) %all-gather.11.cloned.1.call-update) | async-done | bytes 8388624 | tf_op jit(solution)/shard_map/all_gather | solution.py:195
  788.5 6.7 convolution_convert_fusion.3
  798.5 33.2 %while.27 = (s32[]{:T(128)}, bf16[2,1024,2,128]{1,3,2,0:T(8,128)(2,1)}, bf16[2,1024,2,128]{1,3,2,0:T(8,128)(2,1)}, bf16[2,1024,2,128]{1,3,2,0:T(8,128)(2,1)}, bf...) while((s32[]{:T(128)}, ...), condition=%wide.region_18.19_spmd, body=%wide.region_15.18_spmd.sunk | while | flops 2713189888 | bytes 113858456 | solution.py:198
  803.0 1.4 fusion.221
  804.4 1.7 multiply_reduce_fusion.5
  806.1 1.7 multiply_reduce_fusion.6
  807.8 2.3 multiply_convert_fusion.5
  819.6 1.4 fusion.221
  821.0 1.7 multiply_reduce_fusion.5
  822.7 1.7 multiply_reduce_fusion.6
  824.4 2.3 multiply_convert_fusion.5
  831.8 6.3 convolution_bitcast_fusion.3
  838.1 6.1 convolution_bitcast_fusion.4
  844.3 2.6 fusion.101
  846.9 2.0 pad_maximum_fusion
  848.9 3.3 convolution_bitcast_fusion.2
  852.5 9.4 fusion.124
  861.8 9.9 fusion.121
  871.8 16.1 %add_convert_fusion = bf16[2,1024,2048]{2,1,0:T(8,128)(2,1)} fusion(f32[2,1024,2048]{2,1,0:T(8,128)} %fusion.121, f32[2,1024,2048]{2,1,0:T(8,128)} %fusion.124, bf16[2,1024,256]{1,2,0:T(8,128)(2,1)S(1)} %bitcast.300, bf16[3,2048,256]{2,1,0:T(8,128)(2,1)} %param.24), kind=kOutput, calls=%fused_computation.114 | convolution fusion | flops 2164260864 | bytes 44040192 | tf_op jit(solution)/shard_map/dot_general | solution.py:31
  887.9 14.1 %convolution_convert_fusion.1 = bf16[2,1024,2048]{2,1,0:T(8,128)(2,1)} fusion(bf16[2,1024,1024]{2,1,0:T(8,128)(2,1)} %get-tuple-element.194, bf16[1024,2048]{1,0:T(8,128)(2,1)} %param.32), kind=kOutput, calls=%fused_computation.141 | convolution fusion | flops 8594128896 | bytes 16777216 | tf_op jit(solution)/shard_map/dot_general | solution.py:25
  902.7 11.2 all-reduce.1
  913.9 41.2 %all-reduce.7.cloned.1.call-done = (bf16[3,2048,256]{2,1,0:T(8,128)(2,1)}, bf16[256,2048]{1,0:T(8,128)(2,1)}) async-done(((bf16[3,2048,256]{2,1,0:T(8,128)(2,1)}, bf16[256,2048]{1,0:T(8,128)(2,1)}), (bf16[3,2048,256]{2,1,0:T(8,128)(2,1)}, bf16[256,2048]{1,0:T(8,128)(2,1)})) %all-reduce.7.cloned.1.call-update) | async-done | bytes 4194320 | tf_op jit(solution)/shard_map/psum | solution.py:46
  955.1 2.9 convert_element_type.199
  958.2 3.2 convert_element_type.195
  961.4 85.6 %reduce-scatter.11.cloned.1.call-done = bf16[2,128,2048]{2,1,0:T(8,128)(2,1)} async-done(((bf16[2,1024,2048]{2,1,0:T(8,128)(2,1)}), bf16[2,128,2048]{2,1,0:T(8,128)(2,1)}) %reduce-scatter.11.cloned.1.call-update) | async-done | bytes 1048592 | tf_op jit(solution)/shard_map/reduce_scatter | solution.py:229
  1047.0 1.8 fusion.110
  1048.9 4.5 fusion.112
  1053.4 40.9 %all-reduce = (f32[2048]{0:T(1024)}, f32[2048]{0:T(1024)}, f32[2048]{0:T(1024)}, f32[2048]{0:T(1024)}, f32[2048]{0:T(1024)}, /*index=5*/f32[2048]{0:T(1024)}) all-reduce(f32[2048]{0:T(1024)S(1)} %get-tuple-element.146, f32[2048]{0:T(1024)S(1)} %get-tuple-element.147, ...), channel_id=1, replica_groups=mesh['dp'=4,'tensor'=8] {'dp','tensor'}, use_global_device_ids=true, to_apply=%region_23.24 | all-reduce | flops 12288 | bytes 98304 | tf_op jit(solution)/shard_map/psum | solution.py:237
  1094.3 43.9 %reduce-scatter.7.cloned.1.call-done = bf16[2,128,2048]{2,1,0:T(8,128)(2,1)} async-done(((bf16[2,1024,2048]{2,1,0:T(8,128)(2,1)}), bf16[2,128,2048]{2,1,0:T(8,128)(2,1)}) %reduce-scatter.7.cloned.1.call-update) | async-done | bytes 1048592 | tf_op jit(solution)/shard_map/reduce_scatter | solution.py:165
  1138.2 4.8 add_add_fusion.2
  (244 shorter events, 41.4 us)
Async XLA Ops:
  7.2 134.4 %copy-start = (bf16[256,2048]{1,0:T(8,128)(2,1)S(1)}, bf16[256,2048]{1,0:T(8,128)(2,1)}, u32[]{:S(2)}) copy-start(bf16[256,2048]{1,0:T(8,128)(2,1)} %param.26) | copy-start | bytes 3145732
  7.2 6.0 copy-start.57
  7.2 90.9 %all-gather.5.cloned.1.call-start = ((), (), s32[]{:S(2)}) async-start(), calls=%async_computation.4 | async-start | bytes 9437184 | tf_op jit(solution)/shard_map/all_gather | solution.py:135
  8.8 89.3 %copy-start.38 = (f32[2,128]{1,0:T(2,128)}, f32[2,128]{1,0:T(2,128)S(1)}, u32[]{:S(2)}) copy-start(f32[2,128]{1,0:T(2,128)S(1)} %broadcast_multiply_fusion.2) | copy-start | bytes 3076
  10.4 87.6 %copy-start.51 = (f32[2,128]{1,0:T(2,128)}, f32[2,128]{1,0:T(2,128)S(1)}, u32[]{:S(2)}) copy-start(f32[2,128]{1,0:T(2,128)S(1)} %fusion.109) | copy-start | bytes 3076
  10.5 87.6 %copy-start.47 = (f32[2,128]{1,0:T(2,128)}, f32[2,128]{1,0:T(2,128)S(1)}, u32[]{:S(2)}) copy-start(f32[2,128]{1,0:T(2,128)S(1)} %fusion.138) | copy-start | bytes 3076
  13.2 224.2 %reduce-scatter.5.cloned.1.call-start = ((), (), s32[]{:S(2)}) async-start(), calls=%async_computation.5 | async-start | bytes 9437184 | tf_op jit(solution)/shard_map/reduce_scatter | solution.py:154
  113.6 8.1 copy-start.58
  125.4 2.2 copy-start.9
  135.0 2.2 copy-start.9
  141.6 7.4 copy-start.4
  149.0 88.3 %copy-start.2 = (bf16[2,128,2048]{2,1,0:T(8,128)(2,1)S(1)}, bf16[2,128,2048]{2,1,0:T(8,128)(2,1)}, u32[]{:S(2)}) copy-start(bf16[2,128,2048]{2,1,0:T(8,128)(2,1)} %param.19) | copy-start | bytes 3145732
  149.0 88.3 %copy-start.31 = (f32[2048]{0:T(1024)S(1)}, f32[2048]{0:T(1024)}, u32[]{:S(2)}) copy-start(f32[2048]{0:T(1024)} %param.27) | copy-start | bytes 24580
  149.0 91.9 %copy-start.33 = (f32[2048]{0:T(1024)S(1)}, f32[2048]{0:T(1024)}, u32[]{:S(2)}) copy-start(f32[2048]{0:T(1024)} %param.28) | copy-start | bytes 24580
  149.0 91.9 %copy-start.53 = (f32[2048]{0:T(1024)S(1)}, f32[2048]{0:T(1024)}, u32[]{:S(2)}) copy-start(f32[2048]{0:T(1024)} %param.29) | copy-start | bytes 24580
  149.0 174.1 %all-gather.7.cloned.1.call-start = ((), (), s32[]{:S(2)}) async-start(), calls=%async_computation.6 | async-start | bytes 9437184 | tf_op jit(solution)/shard_map/all_gather | solution.py:162
  237.3 3.6 copy-start.6
  239.1 294.8 %copy-start.36 = (f32[2,128]{1,0:T(2,128)}, f32[2,128]{1,0:T(2,128)S(1)}, u32[]{:S(2)}) copy-start(f32[2,128]{1,0:T(2,128)S(1)} %broadcast_multiply_fusion.1) | copy-start | bytes 3076
  240.9 82.3 %copy-start.55 = (f32[1024]{0:T(1024)S(1)}, f32[1024]{0:T(1024)}, u32[]{:S(2)}) copy-start(f32[1024]{0:T(1024)} %param.31) | copy-start | bytes 12292
  240.9 292.9 %copy-start.40 = (f32[2,128]{1,0:T(2,128)}, f32[2,128]{1,0:T(2,128)S(1)}, u32[]{:S(2)}) copy-start(f32[2,128]{1,0:T(2,128)S(1)} %fusion.139) | copy-start | bytes 3076
  242.6 163.2 %all-gather.9.cloned.1.call-start = ((), (), s32[]{:S(2)}) async-start(), calls=%async_computation.8 | async-start | bytes 9437184 | tf_op jit(solution)/shard_map/all_gather | solution.py:178
  242.7 291.1 %copy-start.43 = (f32[2,128]{1,0:T(2,128)}, f32[2,128]{1,0:T(2,128)S(1)}, u32[]{:S(2)}) copy-start(f32[2,128]{1,0:T(2,128)S(1)} %compare_convert_fusion) | copy-start | bytes 3076
  245.2 283.0 %reduce-scatter.9.cloned.1.call-start = ((), (), s32[]{:S(2)}) async-start(), calls=%async_computation.9 | async-start | bytes 9437184 | tf_op jit(solution)/shard_map/reduce_scatter | solution.py:185
  338.8 3.4 copy-start.21
  405.8 23.1 %copy-start.59 = (bf16[2048,1024]{1,0:T(8,128)(2,1)S(1)}, bf16[2048,1024]{1,0:T(8,128)(2,1)}, u32[]{:S(2)}) copy-start(bf16[2048,1024]{1,0:T(8,128)(2,1)} %param.30) | copy-start | bytes 12582916
  439.9 263.5 %all-reduce.9.cloned.1.call-start = ((), (), s32[]{:S(2)}) async-start(), calls=%async_computation.13 | async-start | bytes 16777216 | tf_op jit(solution)/shard_map/psum | solution.py:46
  440.0 14.4 %copy-start.29 = (bf16[2,1024,1024]{2,1,0:T(8,128)(2,1)S(1)}, bf16[2,1024,1024]{2,1,0:T(8,128)(2,1)}, u32[]{:S(2)}) copy-start(bf16[2,1024,1024]{2,1,0:T(8,128)(2,1)} %get-tuple-element.194) | copy-start | bytes 12582916
  467.5 321.0 %all-gather.11.cloned.1.call-start = ((), (), s32[]{:S(2)}) async-start(), calls=%async_computation.10 | async-start | bytes 9437184 | tf_op jit(solution)/shard_map/all_gather | solution.py:195
  528.2 6.2 copy-start.7
  528.2 6.2 copy-start.12
  528.2 6.2 copy-start.14
  531.3 2.5 copy-start.45
  536.6 418.5 %all-reduce.7.cloned.1.call-start = ((), (), s32[]{:S(2)}) async-start(), calls=%async_computation.12 | async-start | bytes 8388608 | tf_op jit(solution)/shard_map/psum | solution.py:46
  703.4 6.8 copy-start.22
  714.8 83.7 %copy-start.5 = (bf16[2,1024,2,128]{3,1,2,0:T(8,128)(2,1)S(1)}, bf16[2,1024,2,128]{3,1,2,0:T(8,128)(2,1)}, u32[]{:S(2)}) copy-start(bf16[2,1024,2,128]{3,1,2,0:T(8,128)(2,1)} %copy-done.4) | copy-start | bytes 3145732
  810.1 2.3 copy-start.23
  826.7 2.3 copy-start.23
  831.7 6.3 copy-start.25
  831.7 12.5 %slice-start = ((s8[8388608]{0:T(1024)(128)(4,1)}), s8[4194304]{0:T(1024)(128)(4,1)S(1)}, s32[]{:S(2)}) async-start(s8[8388608]{0:T(1024)(128)(4,1)} %bitcast.315), calls=%async_computation.14 | async-start | bytes 8388608
  838.1 6.1 copy-start.20
  838.1 6.1 slice-start.1
  838.1 10.7 slice-start.2
  844.2 4.6 slice-start.3
  852.2 194.8 %reduce-scatter.11.cloned.1.call-start = ((), (), s32[]{:S(2)}) async-start(), calls=%async_computation.11 | async-start | bytes 9437184 | tf_op jit(solution)/shard_map/reduce_scatter | solution.py:229
  861.8 9.9 copy-start.17
  887.9 250.4 %reduce-scatter.7.cloned.1.call-start = ((), (), s32[]{:S(2)}) async-start(), calls=%async_computation.7 | async-start | bytes 9437184 | tf_op jit(solution)/shard_map/reduce_scatter | solution.py:165
  955.1 2.9 copy-start.30
  958.0 89.0 %copy-start.3 = (bf16[2,128,2048]{2,1,0:T(8,128)(2,1)S(1)}, bf16[2,128,2048]{2,1,0:T(8,128)(2,1)}, u32[]{:S(2)}) copy-start(bf16[2,128,2048]{2,1,0:T(8,128)(2,1)} %param.19) | copy-start | bytes 3145732
  958.0 89.0 %copy-start.35 = (f32[2048]{0:T(1024)S(1)}, f32[2048]{0:T(1024)}, u32[]{:S(2)}) copy-start(f32[2048]{0:T(1024)} %param.22) | copy-start | bytes 24580
  958.0 89.0 %copy-start.39 = (f32[2,128]{1,0:T(2,128)S(1)}, f32[2,128]{1,0:T(2,128)}, u32[]{:S(2)}) copy-start(f32[2,128]{1,0:T(2,128)} %copy-done.38) | copy-start | bytes 3076
  958.0 90.8 %copy-start.52 = (f32[2,128]{1,0:T(2,128)S(1)}, f32[2,128]{1,0:T(2,128)}, u32[]{:S(2)}) copy-start(f32[2,128]{1,0:T(2,128)} %copy-done.51) | copy-start | bytes 3076
  958.1 90.8 %copy-start.8 = (bf16[2,128,2048]{2,1,0:T(8,128)(2,1)S(1)}, bf16[2,128,2048]{2,1,0:T(8,128)(2,1)}, u32[]{:S(2)}) copy-start(bf16[2,128,2048]{2,1,0:T(8,128)(2,1)} %reduce-scatter.5.cloned.1.call-done) | copy-start | bytes 3145732
  958.1 90.8 %copy-start.13 = (bf16[2,128,2048]{2,1,0:T(8,128)(2,1)S(1)}, bf16[2,128,2048]{2,1,0:T(8,128)(2,1)}, u32[]{:S(2)}) copy-start(bf16[2,128,2048]{2,1,0:T(8,128)(2,1)} %reduce-scatter.9.cloned.1.call-done) | copy-start | bytes 3145732
  958.1 90.8 %copy-start.32 = (f32[2048]{0:T(1024)S(1)}, f32[2048]{0:T(1024)}, u32[]{:S(2)}) copy-start(f32[2048]{0:T(1024)} %param.27) | copy-start | bytes 24580
  958.1 90.8 %copy-start.34 = (f32[2048]{0:T(1024)S(1)}, f32[2048]{0:T(1024)}, u32[]{:S(2)}) copy-start(f32[2048]{0:T(1024)} %param.28) | copy-start | bytes 24580
  958.1 90.8 %copy-start.37 = (f32[2,128]{1,0:T(2,128)S(1)}, f32[2,128]{1,0:T(2,128)}, u32[]{:S(2)}) copy-start(f32[2,128]{1,0:T(2,128)} %copy-done.36) | copy-start | bytes 3076
  958.1 90.8 %copy-start.41 = (f32[2,128]{1,0:T(2,128)S(1)}, f32[2,128]{1,0:T(2,128)}, u32[]{:S(2)}) copy-start(f32[2,128]{1,0:T(2,128)} %copy-done.40) | copy-start | bytes 3076
  958.1 90.8 %copy-start.44 = (f32[2,128]{1,0:T(2,128)S(1)}, f32[2,128]{1,0:T(2,128)}, u32[]{:S(2)}) copy-start(f32[2,128]{1,0:T(2,128)} %copy-done.43) | copy-start | bytes 3076
  958.1 90.8 %copy-start.46 = (f32[2,128]{1,0:T(2,128)S(1)}, f32[2,128]{1,0:T(2,128)}, u32[]{:S(2)}) copy-start(f32[2,128]{1,0:T(2,128)} %copy-done.45) | copy-start | bytes 3076
  958.1 90.8 %copy-start.48 = (f32[2,128]{1,0:T(2,128)S(1)}, f32[2,128]{1,0:T(2,128)}, u32[]{:S(2)}) copy-start(f32[2,128]{1,0:T(2,128)} %copy-done.47) | copy-start | bytes 3076
  958.2 90.8 %copy-start.50 = (f32[2,128]{1,0:T(2,128)S(1)}, f32[2,128]{1,0:T(2,128)}, u32[]{:S(2)}) copy-start(f32[2,128]{1,0:T(2,128)} %copy-done.49) | copy-start | bytes 3076
  961.4 92.0 %copy-start.42 = (f32[2048]{0:T(1024)S(1)}, f32[2048]{0:T(1024)}, u32[]{:S(2)}) copy-start(f32[2048]{0:T(1024)} %get-tuple-element.143) | copy-start | bytes 24580
  961.4 176.8 %copy-start.54 = (f32[2048]{0:T(1024)S(1)}, f32[2048]{0:T(1024)}, u32[]{:S(2)}) copy-start(f32[2048]{0:T(1024)} %param.33) | copy-start | bytes 24580
  1094.3 48.7 %copy-start.1 = (bf16[256,2048]{1,0:T(8,128)(2,1)S(1)}, bf16[256,2048]{1,0:T(8,128)(2,1)}, u32[]{:S(2)}) copy-start(bf16[256,2048]{1,0:T(8,128)(2,1)} %param.26) | copy-start | bytes 3145732
  (22 other events, 28.1 us)
Sparse Core Ops, SparseCore 0:
  13.3 84.7 all-gather.4
  149.1 88.1 reduce-scatter.4
  242.7 80.4 all-gather.6
  325.2 80.5 all-gather.8
  440.0 88.1 reduce-scatter.8
  532.4 170.9 all-reduce.8
  705.7 82.7 all-gather.10
  852.3 102.7 all-reduce.6
  957.4 89.5 reduce-scatter.10
  1049.2 89.0 reduce-scatter.6

commit v2 on v1

--- a/solution.py
+++ b/solution.py
@@ -1,6 +1,10 @@
+import functools
+
 import jax
 import jax.numpy as jnp
 from jax import lax
+from jax.experimental import pallas as pl
+from jax.experimental.pallas import tpu as pltpu
 from jax.sharding import PartitionSpec as P
 
 HD = 128
@@ -107,6 +111,444 @@
             preferred_element_type=jnp.float32,
         )
     return (jnp.concatenate(grad_queries, axis=0), grad_keys, grad_values)
+
+
+MESH = pl.DeviceIdType.MESH
+UP, DOWN, SIDE = 0, 1, 2
+VMEM = pltpu.VMEM
+DMA = pltpu.SemaphoreType.DMA
+f32 = jnp.float32
+bf16 = jnp.bfloat16
+
+
+class Place:
+    def __init__(self, n):
+        self.n, self.chips = n, n // 2
+        self.me = lax.axis_index("tensor")
+        self.chip, self.core = self.me // 2, lax.rem(self.me, 2)
+        self.side = self.me + 1 - 2 * self.core
+        self.below = self.chip > 0
+        self.above = self.chip < self.chips - 1
+
+    def greet(self):
+        barrier = pltpu.get_barrier_semaphore()
+
+        def tell(target):
+            pl.semaphore_signal(
+                barrier, inc=1, device_id={"tensor": target}, device_id_type=MESH
+            )
+
+        tell(self.side)
+        pl.when(self.below)(lambda: tell(self.me - 2))
+        pl.when(self.above)(lambda: tell(self.me + 2))
+        peers = 1 + self.below.astype(jnp.int32) + self.above.astype(jnp.int32)
+        pl.semaphore_wait(barrier, peers)
+
+
+def rows_of(index, rows):
+    return pl.ds(pl.multiple_of(index * rows, rows), rows)
+
+
+class Gather:
+    def __init__(self, at, rows, buf, send, recv):
+        self.at, self.rows, self.buf, self.send, self.recv = at, rows, buf, send, recv
+        self.seqs = buf.shape[0]
+
+    @staticmethod
+    def scratch(n, seqs):
+        return [DMA((3, seqs, n // 2)), DMA((seqs, n))]
+
+    def piece(self, s, o, k):
+        return self.buf.at[s, rows_of(2 * o + k, self.rows)]
+
+    def copy(self, s, o, kind):
+        at = self.at
+        target = (at.me + 2, at.me - 2, at.side)[kind]
+        piece = self.piece(s, o, at.core)
+        return pltpu.make_async_remote_copy(
+            src_ref=piece,
+            dst_ref=piece,
+            send_sem=self.send.at[kind, s, o],
+            recv_sem=self.recv.at[s, 2 * o + at.core],
+            device_id={"tensor": target},
+            device_id_type=MESH,
+        )
+
+    def arrived(self, s, o, k):
+        at = self.at
+        piece = self.piece(s, o, k)
+        pltpu.make_async_remote_copy(
+            src_ref=piece,
+            dst_ref=piece,
+            send_sem=self.send.at[SIDE, s, o],
+            recv_sem=self.recv.at[s, 2 * o + k],
+            device_id={"tensor": at.side},
+            device_id_type=MESH,
+        ).wait_recv()
+
+    def start(self, s):
+        at = self.at
+        pl.when(at.above)(lambda: self.copy(s, at.chip, UP).start())
+        pl.when(at.below)(lambda: self.copy(s, at.chip, DOWN).start())
+        self.copy(s, at.chip, SIDE).start()
+
+    def units(self):
+        return self.seqs * (1 + 2 * (self.at.chips - 1))
+
+    def unit(self, u):
+        at = self.at
+        per = 1 + 2 * (at.chips - 1)
+        s, v = u // per, lax.rem(u, per)
+        d = (v + 1) // 2
+        o = at.chip + (2 * lax.rem(v, 2) - 1) * d
+        return s, o, (o >= 0) & (o < at.chips) & (u >= 0) & (u < self.units()), v == 0
+
+    def forward(self, u):
+        at = self.at
+        s, o, there, own = self.unit(u)
+
+        @pl.when(there & jnp.logical_not(own))
+        def _():
+            self.arrived(s, o, at.core)
+            pl.when((o < at.chip) & at.above)(lambda: self.copy(s, o, UP).start())
+            pl.when((o > at.chip) & at.below)(lambda: self.copy(s, o, DOWN).start())
+            self.copy(s, o, SIDE).start()
+
+    def finish(self):
+        at = self.at
+
+        def one(i, carry):
+            s, o = i // at.chips, lax.rem(i, at.chips)
+            pl.when((o <= at.chip) & at.above)(lambda: self.copy(s, o, UP).wait_send())
+            pl.when((o >= at.chip) & at.below)(lambda: self.copy(s, o, DOWN).wait_send())
+            self.copy(s, o, SIDE).wait_send()
+            return carry
+
+        lax.fori_loop(0, self.seqs * at.chips, one, 0)
+
+
+class Scatter:
+    def __init__(self, at, rows, part, side, link, side_send, side_recv, send, recv):
+        self.at, self.rows = at, rows
+        self.part, self.side, self.link = part, side, link
+        self.side_send, self.side_recv, self.send, self.recv = side_send, side_recv, send, recv
+        self.seqs = part.shape[0]
+
+    @staticmethod
+    def scratch(n, seqs, rows, width):
+        chips = n // 2
+        return [
+            VMEM((seqs, chips, 2 * rows, width), bf16),
+            VMEM((seqs, chips, rows, width), bf16),
+            VMEM((seqs, chips + 1, rows, width), bf16),
+            DMA((seqs, chips)),
+            DMA((seqs, chips)),
+            DMA((seqs, chips)),
+            DMA((seqs, chips + 1)),
+        ]
+
+    def units(self):
+        return self.seqs * (2 * self.at.chips - 1)
+
+    def unit(self, u):
+        at = self.at
+        per = 2 * at.chips - 1
+        s, v = u // per, lax.rem(u, per)
+        j = v // 2
+        up = lax.rem(v, 2) == 0
+        last = v == per - 1
+        o = jnp.where(last, at.chip, jnp.where(up, at.chips - 1 - j, j))
+        there = last | jnp.where(up, o > at.chip, o < at.chip)
+        return s, o, there & (u >= 0) & (u < self.units())
+
+    def side_copy(self, s, o):
+        at = self.at
+        return pltpu.make_async_remote_copy(
+            src_ref=self.part.at[s, o, rows_of(1 - at.core, self.rows)],
+            dst_ref=self.side.at[s, o],
+            send_sem=self.side_send.at[s, o],
+            recv_sem=self.side_recv.at[s, o],
+            device_id={"tensor": at.side},
+            device_id_type=MESH,
+        )
+
+    def link_copy(self, s, o, slot, target):
+        return pltpu.make_async_remote_copy(
+            src_ref=self.part.at[s, o, rows_of(self.at.core, self.rows)],
+            dst_ref=self.link.at[s, slot],
+            send_sem=self.send.at[s, o],
+            recv_sem=self.recv.at[s, slot],
+            device_id={"tensor": target},
+            device_id_type=MESH,
+        )
+
+    def share(self, s, o):
+        self.side_copy(s, o).start()
+
+    def blocks(self, body):
+        step = 16
+        lax.fori_loop(0, self.rows // step, lambda i, c: (body(pl.multiple_of(i * step, step), step), c)[1], 0)
+
+    def add_up(self, s, o, slots):
+        base = self.at.core * self.rows
+
+        def body(first, step):
+            here = pl.ds(pl.multiple_of(base + first, step), step)
+            there = pl.ds(first, step)
+            total = self.part[s, o, here].astype(f32) + self.side[s, o, there].astype(f32)
+            for slot in slots:
+                total += self.link[s, slot, there].astype(f32)
+            self.part[s, o, here] = total.astype(bf16)
+
+        self.blocks(body)
+
+    def pass_on(self, u, final):
+        at = self.at
+        s, o, there = self.unit(u)
+
+        @pl.when(there)
+        def _():
+            self.side_copy(s, o).wait_recv()
+
+            @pl.when(o > at.chip)
+            def _():
+                @pl.when(at.below)
+                def _():
+                    self.link_copy(s, o, o, at.me).wait_recv()
+                    self.add_up(s, o, [o])
+
+                pl.when(jnp.logical_not(at.below))(lambda: self.add_up(s, o, []))
+                self.link_copy(s, o, o, at.me + 2).start()
+
+            @pl.when(o < at.chip)
+            def _():
+                @pl.when(at.above)
+                def _():
+                    self.link_copy(s, o, o, at.me).wait_recv()
+                    self.add_up(s, o, [o])
+
+                pl.when(jnp.logical_not(at.above))(lambda: self.add_up(s, o, []))
+                slot = jnp.where(o == at.chip - 1, at.chips, o)
+                self.link_copy(s, o, slot, at.me - 2).start()
+
+            @pl.when(o == at.chip)
+            def _():
+                pl.when(at.below)(lambda: self.link_copy(s, o, o, at.me).wait_recv())
+                pl.when(at.above)(lambda: self.link_copy(s, o, at.chips, at.me).wait_recv())
+                for slot, used in ((o, at.below), (at.chips, at.above)):
+                    @pl.when(jnp.logical_not(used))
+                    def _():
+                        def clear(first, step):
+                            self.link[s, slot, pl.ds(first, step)] = jnp.zeros(
+                                (step, self.link.shape[-1]), bf16
+                            )
+
+                        self.blocks(clear)
+                base = at.core * self.rows
+
+                def body(first, step):
+                    here = pl.ds(pl.multiple_of(base + first, step), step)
+                    there = pl.ds(first, step)
+                    total = self.part[s, o, here].astype(f32) + self.side[s, o, there].astype(f32)
+                    total += self.link[s, o, there].astype(f32)
+                    total += self.link[s, at.chips, there].astype(f32)
+                    final(s, there, total)
+
+                self.blocks(body)
+
+    def finish(self):
+        at = self.at
+
+        def one(i, carry):
+            s, o = i // at.chips, lax.rem(i, at.chips)
+            self.side_copy(s, o).wait_send()
+            pl.when(o != at.chip)(lambda: self.link_copy(s, o, o, at.side).wait_send())
+            return carry
+
+        lax.fori_loop(0, self.seqs * at.chips, one, 0)
+
+
+def norm_rows(values, gain, shift):
+    centre = values - jnp.mean(values, axis=-1, keepdims=True)
+    spread = jnp.mean(centre * centre, axis=-1, keepdims=True)
+    return centre * lax.rsqrt(spread + norm_epsilon) * gain + shift
+
+
+def gather_project_kernel(
+    n, tokens, gain, shift, weight, bias, gathered, heads, buf, send, recv, out_sem
+):
+    at = Place(n)
+    seqs, rows, width = tokens.shape
+    ring = Gather(at, rows, buf, send, recv)
+    at.greet()
+    for s in range(seqs):
+        def block(i, carry):
+            first = pl.multiple_of(i * 16, 16)
+            values = norm_rows(tokens[s, pl.ds(first, 16)].astype(f32), gain[...], shift[...])
+            buf[s, pl.ds(pl.multiple_of(at.me * rows + first, 16), 16)] = values.astype(bf16)
+            return carry
+
+        lax.fori_loop(0, rows // 16, block, 0)
+        ring.start(s)
+
+    def keep(s, o):
+        here = rows_of(o, 2 * rows)
+        return pltpu.make_async_copy(buf.at[s, here], gathered.at[s, here], out_sem.at[s, o])
+
+    def step(u, carry):
+        ring.forward(u)
+        s, o, there, own = ring.unit(u - 2)
+
+        @pl.when(there)
+        def _():
+            ring.arrived(s, o, 1 - at.core)
+            keep(s, o).start()
+            here = rows_of(o, 2 * rows)
+            for j in range(3):
+                total = jnp.dot(buf[s, here], weight[j], preferred_element_type=f32)
+                if j == 0:
+                    total = (total + bias[0:1]) * HD ** (-0.5)
+                if j == 2:
+                    total = total + bias[1:2]
+                heads[j, s, here] = total.astype(bf16)
+
+        return carry
+
+    lax.fori_loop(0, ring.units() + 2, step, 0)
+    ring.finish()
+
+    def close(i, carry):
+        keep(i // at.chips, lax.rem(i, at.chips)).wait()
+        return carry
+
+    lax.fori_loop(0, seqs * at.chips, close, 0)
+
+
+def whole(count):
+    return [pl.BlockSpec(memory_space=VMEM)] * count
+
+
+def gather_project(n, tokens, gain, shift, weight, bias):
+    seqs, rows, width = tokens.shape
+    part = weight.shape[2]
+    return pl.pallas_call(
+        functools.partial(gather_project_kernel, n),
+        out_shape=(
+            jax.ShapeDtypeStruct((seqs, n * rows, width), bf16),
+            jax.ShapeDtypeStruct((3, seqs, n * rows, part), bf16),
+        ),
+        in_specs=whole(5),
+        out_specs=(pl.BlockSpec(memory_space=pl.ANY), pl.BlockSpec(memory_space=VMEM)),
+        scratch_shapes=[VMEM((seqs, n * rows, width), bf16)]
+        + Gather.scratch(n, seqs)
+        + [DMA((seqs, n // 2))],
+        compiler_params=pltpu.CompilerParams(
+            collective_id=0, has_side_effects=True, vmem_limit_bytes=40 * 2**20
+        ),
+        name="gather_project",
+    )(tokens, gain, shift, weight, bias)
+
+
+def project_scatter_kernel(
+    n, mixed, weight, tokens, bias, gain, shift, hidden, normed, *scratch
+):
+    at = Place(n)
+    seqs, rows, width = tokens.shape
+    line = Scatter(at, rows, *scratch)
+    at.greet()
+
+    def final(s, there, total):
+        values = tokens[s, there].astype(f32) + total + bias[...]
+        hidden[s, there] = values
+        normed[s, there] = norm_rows(values, gain[...], shift[...]).astype(bf16)
+
+    def step(u, carry):
+        s, o, there = line.unit(u)
+
+        @pl.when(there)
+        def _():
+            here = rows_of(o, 2 * rows)
+            for j in range(width // 512):
+                cols = pl.ds(j * 512, 512)
+                total = jnp.dot(mixed[s, here], weight[:, cols], preferred_element_type=f32)
+                line.part[s, o, :, cols] = total.astype(bf16)
+            line.share(s, o)
+
+        line.pass_on(u - 1, final)
+        return carry
+
+    lax.fori_loop(0, line.units() + 1, step, 0)
+    line.finish()
+
+
+def project_scatter(n, mixed, weight, tokens, bias, gain, shift):
+    seqs, rows, width = tokens.shape
+    return pl.pallas_call(
+        functools.partial(project_scatter_kernel, n),
+        out_shape=(
+            jax.ShapeDtypeStruct((seqs, rows, width), f32),
+            jax.ShapeDtypeStruct((seqs, rows, width), bf16),
+        ),
+        in_specs=whole(6),
+        out_specs=tuple(whole(2)),
+        scratch_shapes=Scatter.scratch(n, seqs, rows, width),
+        compiler_params=pltpu.CompilerParams(
+            collective_id=1, has_side_effects=True, vmem_limit_bytes=40 * 2**20
+        ),
+        name="project_scatter",
+    )(mixed, weight, tokens, bias, gain, shift)
+
+
+def heads_scatter_kernel(n, query, key, value, weight, grad, *scratch):
+    at = Place(n)
+    seqs, rows, width = grad.shape
+    line = Scatter(at, rows, *scratch)
+    at.greet()
+
+    def final(s, there, total):
+        grad[s, there] = total
+
+    def step(u, carry):
+        s, o, there = line.unit(u)
+
+        @pl.when(there)
+        def _():
+            here = rows_of(o, 2 * rows)
+            for j in range(width // 512):
+                cols = pl.ds(j * 512, 512)
+                total = 0.0
+                for part, scale, i in ((query, HD ** (-0.5), 0), (key, 1.0, 1), (value, 1.0, 2)):
+                    total += scale * lax.dot_general(
+                        part[s, here],
+                        weight[i, cols],
+                        (((1,), (1,)), ((), ())),
+                        preferred_element_type=f32,
+                    )
+                line.part[s, o, :, cols] = total.astype(bf16)
+            line.share(s, o)
+
+        line.pass_on(u - 1, final)
+        return carry
+
+    lax.fori_loop(0, line.units() + 1, step, 0)
+    line.finish()
+
+
+def heads_scatter(n, query, key, value, weight):
+    seqs, slots, part = query.shape
+    width = weight.shape[1]
+    rows = slots // n
+    return pl.pallas_call(
+        functools.partial(heads_scatter_kernel, n),
+        out_shape=jax.ShapeDtypeStruct((seqs, rows, width), f32),
+        in_specs=whole(4),
+        out_specs=whole(1)[0],
+        scratch_shapes=Scatter.scratch(n, seqs, rows, width),
+        compiler_params=pltpu.CompilerParams(
+            collective_id=2, has_side_effects=True, vmem_limit_bytes=40 * 2**20
+        ),
+        name="heads_scatter",
+    )(query, key, value, weight)
 
 
 def body(
@@ -131,34 +573,21 @@
     head_count = part_width // HD
     score_scale = HD ** (-0.5)
     inputs = tokens.astype(jnp.float32)
-    normed_one = layer_norm(inputs, ln1_gain, ln1_shift).astype(jnp.bfloat16)
-    gathered_one = lax.all_gather(normed_one, "tensor", axis=1, tiled=True)
+    n = lax.axis_size("tensor")
+    gathered_one, heads = gather_project(
+        n, tokens, ln1_gain[None], ln1_shift[None], qkv_weight, qkv_bias
+    )
     slot_count = gathered_one.shape[1]
     head_shape = (seq_count, slot_count, head_count, HD)
-    query_rows = (
-        ((flat_product(gathered_one, qkv_weight[0]) + qkv_bias[0]) * score_scale)
-        .astype(jnp.bfloat16)
-        .reshape(head_shape)
-    )
-    key_rows = flat_product(gathered_one, qkv_weight[1]).astype(jnp.bfloat16).reshape(head_shape)
-    value_rows = (
-        (flat_product(gathered_one, qkv_weight[2]) + qkv_bias[1])
-        .astype(jnp.bfloat16)
-        .reshape(head_shape)
-    )
+    query_rows, key_rows, value_rows = [heads[j].reshape(head_shape) for j in range(3)]
     attended, log_totals = lax.map(
         lambda item: attend_forward(item[0], item[1], item[2], item[3]),
         (query_rows, key_rows, value_rows, lengths),
     )
     mixed_heads = attended.reshape(seq_count, slot_count, part_width).astype(jnp.bfloat16)
-    attn_local = lax.psum_scatter(
-        flat_product(mixed_heads, out_weight).astype(jnp.bfloat16),
-        "tensor",
-        scatter_dimension=1,
-        tiled=True,
-    ).astype(jnp.float32)
-    hidden_state = inputs + attn_local + out_bias
-    normed_two = layer_norm(hidden_state, ln2_gain, ln2_shift).astype(jnp.bfloat16)
+    hidden_state, normed_two = project_scatter(
+        n, mixed_heads, out_weight, tokens, out_bias[None], ln2_gain[None], ln2_shift[None]
+    )
     gathered_two = lax.all_gather(normed_two, "tensor", axis=1, tiled=True)
     pre_act = flat_product(gathered_two, up_weight) + up_bias
     activated = gelu_exact(pre_act).astype(jnp.bfloat16)
@@ -221,14 +650,7 @@
             jnp.sum(grad_value.astype(jnp.float32), axis=(0, 1)),
         ]
     )
-    norm_one_part = (
-        score_scale * product_back(grad_query, qkv_weight[0])
-        + product_back(grad_key, qkv_weight[1])
-        + product_back(grad_value, qkv_weight[2])
-    )
-    norm_one_grad = lax.psum_scatter(
-        norm_one_part.astype(jnp.bfloat16), "tensor", scatter_dimension=1, tiled=True
-    ).astype(jnp.float32)
+    norm_one_grad = heads_scatter(n, grad_query, grad_key, grad_value, qkv_weight)
     unused_one, norm_one_back = jax.vjp(layer_norm, inputs, ln1_gain, ln1_shift)
     input_ln_grad, ln1_gain_grad, ln1_shift_grad = norm_one_back(norm_one_grad)
     input_grad = hidden_grad + input_ln_grad

time: 1150 us -> 1120 us (0.974)
  Pallas kernels: 0 us -> 279 us
  waiting for transfers between devices: 766 us -> 494 us
  matrix products: 206 us -> 147 us
  local copies, waits for them, and re-layouts: 21.9 us -> 55.6 us
  other arithmetic: 86.7 us -> 74.4 us
    pallas_call x0 -> x3, Pallas kernels: none -> 279 us  [the longest x1 102 us: project_scatter(): pl.pallas_call(functools.partial(project_scatter_kernel, n), out_shape=(j...]
    reduce_scatter x2 -> x0, waiting for transfers between devices: 174 us -> none  [the longest x1 88.2 us: body(): lax.psum_scatter(flat_product(mixed_heads, out_weight).astype(jnp.bfloat1...]
    all_gather x1 -> x0, waiting for transfers between devices: 84.8 us -> none  [body(): gathered_one = lax.all_gather(normed_one, 'tensor', axis=1, tiled=True)]
    reduce_scatter x1, waiting for transfers between devices: 43.9 us -> 85.3 us  [body(): lax.psum_scatter(flat_product(activated, down_weight).astype(jnp.bfloat16...]
    psum x2, waiting for transfers between devices: 208 us -> 167 us  [sum_groups(): return lax.psum(part.astype(jnp.bfloat16), 'dp').astype(jnp.float32)]
    dot_general x6 -> x3, matrix products: 74.2 us -> 39.1 us  [product_back(): lax.dot_general(flat, right_rows, (((1,), (1,)), ((), ())), preferred_ele...]
    dot_general x6 -> x2, matrix products: 57.1 us -> 29.6 us  [flat_product(): result = jnp.dot(flat, right_rows, preferred_element_type=jnp.float32)]
    unnamed x108 -> x88, local copies, waits for them, and re-layouts: 6.49 us -> 22 us
  transfers between devices with their start and end apart: 10 -> 7, of which waited for: 10 -> 6; matrix products, arithmetic and copies ran while one was open for 13% -> 10% of each run, Pallas kernels for 0% -> 9%
where the time goes in v2:
time: 1120 us
  waiting for transfers between devices  494 us (44%)
  Pallas kernels  279 us (25%)
  matrix products  147 us (13%)
  other arithmetic  74.4 us (7%)
  local copies, waits for them, and re-layouts  55.6 us (5%)
  blocking collectives  50.2 us (4%)
  between operations  14.8 us (1%)
    psum x2, waiting for transfers between devices, sum_groups(): return lax.psum(part.astype(jnp.bfloat16), 'dp').astype(jnp.float32)  167 us
    pallas_call x1, Pallas kernels, project_scatter(): pl.pallas_call(functools.partial(project_scatter_kernel, n), out_shape=(j...  102 us
    pallas_call x1, Pallas kernels, heads_scatter(): pl.pallas_call(functools.partial(heads_scatter_kernel, n), out_shape=jax....  98.8 us
    reduce_scatter x1, waiting for transfers between devices, body(): lax.psum_scatter(flat_product(activated, down_weight).astype(jnp.bfloat16...  85.3 us
    all_gather x1, waiting for transfers between devices, body(): gathered_two = lax.all_gather(normed_two, 'tensor', axis=1, tiled=True)  78.8 us
    pallas_call x1, Pallas kernels, gather_project(): pl.pallas_call(functools.partial(gather_project_kernel, n), out_shape=(ja...  78.3 us
    all_gather x1, waiting for transfers between devices, body(): lax.all_gather(hidden_grad.astype(jnp.bfloat16), 'tensor', axis=1, tiled=...  72.6 us
    reduce_scatter x1, waiting for transfers between devices, body(): lax.psum_scatter(product_back(grad_pre, up_weight).astype(jnp.bfloat16),...  46.4 us
  transfers between devices with their start and end apart: 7, of which 6 were waited for; matrix products, arithmetic and copies ran while one was open for 10% of the time, Pallas kernels for 9%

profile of v2, /device:TPU:0, one launch (start us, length us, event | category | flops | bytes accessed | tf_op | source)
XLA Modules:
  0.0 1116.3 jit_solution(4610666913170668684)
XLA Ops:
  8.5 1.9 copy-done.2
  12.4 78.3 %gather_project.1 = (bf16[2,1024,2048]{2,1,0:T(8,128)(2,1)}, bf16[3,2,1024,256]{3,2,1,0:T(8,128)(2,1)S(1)}) custom-call(bf16[2,128,2048]{2,1,0:T(8,128)(2,1)S(1)} %copy-done, f32[1,2048]{1,0:T(1,128)S(1)} %bitcast.262, f32[1,2048]{1,0:T(1,128)S(1)} %bitcast.263, bf16[3,2048,256]{2,1,0:T(8,128)(2,1)S(1)} %copy-done.2, f32[2,256]{1,0:T(2,128)S(1)} %copy-done.17), custom_call_target="tpu_custom_call" | custom-call | tf_op jit(solution)/shard_map/gather_project/pallas_call | solution.py:434
  92.4 2.2 reshape_squeeze.9
  97.1 28.2 %while.26 = (s32[]{:T(128)}, bf16[2,1024,2,128]{1,3,2,0:T(8,128)(2,1)}, f32[2,2,1024,1]{2,1,3,0:T(2,128)S(1)}, bf16[2,1024,2,128]{3,2,1,0:T(2,128)(2,1)}, s32[2]...) while((s32[]{:T(128)}, ...), condition=%wide.region_5.6_spmd, body=%wide.region_0.5_spmd.sunk | while | flops 1093666304 | bytes 46220008 | solution.py:583
  98.3 1.4 constant_dynamic-slice_fusion.4
  101.4 1.9 select_reduce_fusion.4
  103.3 1.9 select_reduce_fusion.5
  105.2 2.2 exponential_reduce_fusion.3
  108.8 1.3 fusion.165
  112.4 1.4 constant_dynamic-slice_fusion.4
  115.5 1.9 select_reduce_fusion.4
  117.4 1.9 select_reduce_fusion.5
  119.2 2.2 exponential_reduce_fusion.3
  122.9 1.3 fusion.165
  125.3 2.6 copy.64.mixed
  130.4 102.2 %project_scatter.1 = (f32[2,128,2048]{2,1,0:T(8,128)S(1)}, bf16[2,128,2048]{2,1,0:T(8,128)(2,1)S(1)}) custom-call(bf16[2,1024,256]{2,1,0:T(8,128)(2,1)S(1)} %copy-done.4, bf16[256,2048]{1,0:T(8,128)(2,1)S(1)} %copy-done.8, bf16[2,128,2048]{2,1,0:T(8,128)(2,1)S(1)} %copy-done.1, f32[1,2048]{1,0:T(1,128)S(1)} %bitcast.264, f32[1,2048]{1,0:T(1,128)S(1)} %bitcast.261, ...), custom_call_target="tpu_custom_call" | custom-call | tf_op jit(solution)/shard_map/project_scatter/pallas_call | solution.py:486
  233.7 2.4 fusion.103
  236.4 78.8 %all-gather.4.cloned.1.call-done = bf16[2,1024,2048]{2,1,0:T(8,128)(2,1)} async-done(((bf16[2,128,2048]{2,1,0:T(8,128)(2,1)}), bf16[2,1024,2048]{2,1,0:T(8,128)(2,1)}) %all-gather.4.cloned.1.call-update) | async-done | bytes 8388624 | tf_op jit(solution)/shard_map/all_gather | solution.py:591
  315.2 15.6 %fusion.105 = (u8[1024,1024]{1,0:T(8,128)(4,1)S(1)}, u8[1024,1024]{1,0:T(8,128)(4,1)S(1)}, f32[2,1024,1024]{2,1,0:T(8,128)S(1)}) fusion(f32[1024]{0:T(1024)S(1)} %copy-done.47, bf16[2,1024,2048]{2,1,0:T(8,128)(2,1)} %all-gather.4.cloned.1.call-done, bf16[2048,1024]{1,0:T(8,128)(2,1)} %param.30), kind=kOutput, calls=%fused_computation.176 | convolution fusion | flops 8617197568 | bytes 23072768 | tf_op jit(solution)/shard_map/dot_general | solution.py:29
  330.9 3.4 copy-done.32
  334.3 20.5 %multiply_convert_fusion.2 = (bf16[2,1024,1024]{2,1,0:T(8,128)(2,1)}, f32[2,1024,1024]{2,1,0:T(8,128)}) fusion(f32[2,1024,1024]{2,1,0:T(8,128)S(1)} %get-tuple-element.233, f32[1024]{0:T(1024)S(1)} %copy-done.47, u8[1024,1024]{1,0:T(8,128)(4,1)S(1)} %get-tuple-element.145, u8[1024,1024]{1,0:T(8,128)(4,1)S(1)} %get-tuple-element.144), kind=kLoop, calls=%fused_computation.120 | loop fusion | flops 148897792 | bytes 23072768 | tf_op jit(solution)/shard_map/convert_element_type | solution.py:593
  354.8 43.2 %all-gather.6.cloned.1.call-done = bf16[2,1024,2048]{2,1,0:T(8,128)(2,1)} async-done(((bf16[2,128,2048]{2,1,0:T(8,128)(2,1)}), bf16[2,1024,2048]{2,1,0:T(8,128)(2,1)}) %all-gather.6.cloned.1.call-update) | async-done | bytes 8388624 | tf_op jit(solution)/shard_map/all_gather | solution.py:607
  398.0 21.4 %convert_reduce_fusion = (f32[1024]{0:T(1024)}, bf16[2,1024,1024]{2,1,0:T(8,128)(2,1)S(1)}) fusion(f32[2,1024,1024]{2,1,0:T(8,128)} %get-tuple-element.205, bf16[2,1024,2048]{2,1,0:T(8,128)(2,1)} %all-gather.6.cloned.1.call-done, bf16[1024,2048]{1,0:T(8,128)(2,1)} %param.32, f32[2,1024,1024]{2,1,0:T(8,128)} %copy-done.32, f32[1024]{0:T(1024)S(1)} %copy-done.47), kind=kOutput, calls=%fused_computation.118 | convolution fusion | flops 8625585152 | bytes 33562624 | tf_op jit(solution)/shard_map/dot_general | solution.py:35
  419.4 1.9 copy-done.52
  421.4 10.9 convolution_convert_fusion
  432.4 13.9 %convolution_convert_fusion.1 = bf16[2,1024,2048]{2,1,0:T(8,128)(2,1)} fusion(bf16[2,1024,1024]{2,1,0:T(8,128)(2,1)} %get-tuple-element.204, bf16[1024,2048]{1,0:T(8,128)(2,1)} %param.32), kind=kOutput, calls=%fused_computation.135 | convolution fusion | flops 8594128896 | bytes 16777216 | tf_op jit(solution)/shard_map/dot_general | solution.py:29
  446.4 14.4 %bitcast_convert_fusion.1 = bf16[2048,1024]{1,0:T(8,128)(2,1)} fusion(bf16[2,1024,2048]{2,1,0:T(8,128)(2,1)} %all-gather.4.cloned.1.call-done, bf16[2,1024,1024]{2,1,0:T(8,128)(2,1)} %copy-done.52), kind=kOutput, calls=%fused_computation.117 | convolution fusion | flops 8592031744 | bytes 16777216 | tf_op jit(solution)/shard_map/dot_general | solution.py:44
  460.8 13.1 %bitcast_convert_fusion = bf16[1024,2048]{1,0:T(8,128)(2,1)} fusion(bf16[2,1024,1024]{2,1,0:T(8,128)(2,1)S(1)} %copy-done.40, bf16[2,1024,2048]{2,1,0:T(8,128)(2,1)} %all-gather.6.cloned.1.call-done), kind=kOutput, calls=%fused_computation.116 | convolution fusion | flops 8592031744 | bytes 16777216 | tf_op jit(solution)/shard_map/dot_general | solution.py:44
  474.2 46.4 %reduce-scatter.5.cloned.1.call-done = bf16[2,128,2048]{2,1,0:T(8,128)(2,1)} async-done(((bf16[2,1024,2048]{2,1,0:T(8,128)(2,1)}), bf16[2,128,2048]{2,1,0:T(8,128)(2,1)}) %reduce-scatter.5.cloned.1.call-update) | async-done | bytes 1048592 | tf_op jit(solution)/shard_map/reduce_scatter | solution.py:614
  520.6 2.5 multiply_reduce_fusion.2
  523.2 2.8 fusion.101
  526.0 85.3 %reduce-scatter.3.cloned.1.call-done = bf16[2,128,2048]{2,1,0:T(8,128)(2,1)} async-done(((bf16[2,1024,2048]{2,1,0:T(8,128)(2,1)}), bf16[2,128,2048]{2,1,0:T(8,128)(2,1)}) %reduce-scatter.3.cloned.1.call-update) | async-done | bytes 1048592 | tf_op jit(solution)/shard_map/reduce_scatter | solution.py:594
  611.3 4.8 fusion.112
  619.1 167.4 %all-reduce.9.cloned.1.call-done = (bf16[2048,1024]{1,0:T(8,128)(2,1)}, bf16[1024,2048]{1,0:T(8,128)(2,1)}) async-done(((bf16[2048,1024]{1,0:T(8,128)(2,1)}, bf16[1024,2048]{1,0:T(8,128)(2,1)}), (bf16[2048,1024]{1,0:T(8,128)(2,1)}, bf16[1024,2048]{1,0:T(8,128)(2,1)})) %all-reduce.9.cloned.1.call-update) | async-done | bytes 8388624 | tf_op jit(solution)/shard_map/psum | solution.py:50
  786.5 6.8 convert_element_type.138
  793.3 4.9 convert_element_type.140
  798.2 72.6 %all-gather.8.cloned.1.call-done = bf16[2,1024,2048]{2,1,0:T(8,128)(2,1)} async-done(((bf16[2,128,2048]{2,1,0:T(8,128)(2,1)}), bf16[2,1024,2048]{2,1,0:T(8,128)(2,1)}) %all-gather.8.cloned.1.call-update) | async-done | bytes 8388624 | tf_op jit(solution)/shard_map/all_gather | solution.py:624
  870.8 6.7 convolution_convert_fusion.2
  880.8 38.6 %while.27 = (s32[]{:T(128)}, bf16[2,1024,2,128]{1,3,2,0:T(8,128)(2,1)}, bf16[2,1024,2,128]{1,3,2,0:T(8,128)(2,1)}, bf16[2,1024,2,128]{1,3,2,0:T(8,128)(2,1)}, bf...) while((s32[]{:T(128)}, ...), condition=%wide.region_15.16_spmd, body=%wide.region_12.15_spmd.sunk | while | flops 2713189888 | bytes 114904488 | solution.py:627
  882.1 1.4 constant_dynamic-slice_fusion.5
  884.1 1.8 fusion.180
  887.9 1.3 fusion.185
  889.3 1.8 multiply_reduce_fusion.5
  891.1 1.8 multiply_reduce_fusion.6
  892.9 2.3 multiply_convert_fusion.4
  901.4 1.4 constant_dynamic-slice_fusion.5
  903.3 1.8 fusion.180
  907.2 1.3 fusion.185
  908.5 1.8 multiply_reduce_fusion.5
  910.3 1.8 multiply_reduce_fusion.6
  912.1 2.3 multiply_convert_fusion.4
  919.5 6.3 convolution_bitcast_fusion.3
  925.9 2.6 convolution_bitcast_fusion.4
  928.5 2.6 fusion.89
  931.1 2.0 pad_maximum_fusion
  933.1 3.3 convolution_bitcast_fusion.2
  940.2 2.4 copy.66.key
  942.7 1.9 copy-done.3
  948.3 98.8 %heads_scatter.1 = f32[2,128,2048]{2,1,0:T(8,128)S(1)} custom-call(bf16[2,1024,256]{2,1,0:T(8,128)(2,1)S(1)} %copy-done.6, bf16[2,1024,256]{2,1,0:T(8,128)(2,1)S(1)} %copy-done.7, bf16[2,1024,256]{2,1,0:T(8,128)(2,1)S(1)} %copy-done.5, bf16[3,2048,256]{2,1,0:T(8,128)(2,1)S(1)} %copy-done.3), custom_call_target="tpu_custom_call" | custom-call | tf_op jit(solution)/shard_map/heads_scatter/pallas_call | solution.py:541
  1047.6 10.2 all-reduce.1
  1059.5 39.9 %all-reduce = (f32[2048]{0:T(1024)}, f32[2048]{0:T(1024)}, f32[2048]{0:T(1024)}, f32[2048]{0:T(1024)}, f32[2048]{0:T(1024)}, /*index=5*/f32[2048]{0:T(1024)}) all-reduce(f32[2048]{0:T(1024)S(1)} %get-tuple-element.148, f32[2048]{0:T(1024)S(1)} %get-tuple-element.152, ...), channel_id=1, replica_groups=mesh['dp'=4,'tensor'=8] {'dp','tensor'}, use_global_device_ids=true, to_apply=%region_21.22 | all-reduce | flops 12288 | bytes 98304 | tf_op jit(solution)/shard_map/psum | solution.py:659
  1099.4 3.6 add_add_fusion.2
  1103.1 2.9 convert_element_type.146
  1106.0 3.2 convert_element_type.142
  (218 shorter events, 55.5 us)
Async XLA Ops:
  7.2 308.0 %all-gather.4.cloned.1.call-start = ((), (), s32[]{:S(2)}) async-start(), calls=%async_computation.2 | async-start | bytes 9437184 | tf_op jit(solution)/shard_map/all_gather | solution.py:591
  7.2 1.2 copy-start
  8.5 1.9 copy-start.2
  92.4 4.7 copy-start.49
  97.0 30.8 %copy-start.1 = (bf16[2,128,2048]{2,1,0:T(8,128)(2,1)S(1)}, bf16[2,128,2048]{2,1,0:T(8,128)(2,1)}, u32[]{:S(2)}) copy-start(bf16[2,128,2048]{2,1,0:T(8,128)(2,1)} %tokens.3) | copy-start | bytes 3145732
  97.1 30.8 %copy-start.11 = (f32[2048]{0:T(1024)S(1)}, f32[2048]{0:T(1024)}, u32[]{:S(2)}) copy-start(f32[2048]{0:T(1024)} %param.28) | copy-start | bytes 24580
  97.1 30.9 %copy-start.15 = (f32[2048]{0:T(1024)S(1)}, f32[2048]{0:T(1024)}, u32[]{:S(2)}) copy-start(f32[2048]{0:T(1024)} %param.27) | copy-start | bytes 24580
  97.1 30.9 %copy-start.16 = (f32[2048]{0:T(1024)S(1)}, f32[2048]{0:T(1024)}, u32[]{:S(2)}) copy-start(f32[2048]{0:T(1024)} %param.29) | copy-start | bytes 24580
  105.1 2.3 copy-start.23
  108.7 1.4 copy-start.37
  119.2 2.3 copy-start.23
  122.8 1.4 copy-start.37
  125.3 2.6 copy-start.18
  127.9 187.3 %copy-start.47 = (f32[1024]{0:T(1024)S(1)}, f32[1024]{0:T(1024)}, u32[]{:S(2)}) copy-start(f32[1024]{0:T(1024)} %param.31) | copy-start | bytes 12292
  127.9 1.2 copy-start.4
  129.1 1.2 copy-start.8
  233.6 164.4 %all-gather.6.cloned.1.call-start = ((), (), s32[]{:S(2)}) async-start(), calls=%async_computation.4 | async-start | bytes 9437184 | tf_op jit(solution)/shard_map/all_gather | solution.py:607
  236.2 284.4 %reduce-scatter.5.cloned.1.call-start = ((), (), s32[]{:S(2)}) async-start(), calls=%async_computation.5 | async-start | bytes 9437184 | tf_op jit(solution)/shard_map/reduce_scatter | solution.py:614
  330.9 3.4 copy-start.32
  398.0 23.4 %copy-start.51 = (bf16[2048,1024]{1,0:T(8,128)(2,1)S(1)}, bf16[2048,1024]{1,0:T(8,128)(2,1)}, u32[]{:S(2)}) copy-start(bf16[2048,1024]{1,0:T(8,128)(2,1)} %param.30) | copy-start | bytes 12582916
  419.4 1.9 copy-start.52
  432.3 179.0 %reduce-scatter.3.cloned.1.call-start = ((), (), s32[]{:S(2)}) async-start(), calls=%async_computation.3 | async-start | bytes 9437184 | tf_op jit(solution)/shard_map/reduce_scatter | solution.py:594
  446.3 340.1 %all-reduce.9.cloned.1.call-start = ((), (), s32[]{:S(2)}) async-start(), calls=%async_computation.8 | async-start | bytes 16777216 | tf_op jit(solution)/shard_map/psum | solution.py:50
  446.4 14.4 %copy-start.40 = (bf16[2,1024,1024]{2,1,0:T(8,128)(2,1)S(1)}, bf16[2,1024,1024]{2,1,0:T(8,128)(2,1)}, u32[]{:S(2)}) copy-start(bf16[2,1024,1024]{2,1,0:T(8,128)(2,1)} %get-tuple-element.204) | copy-start | bytes 12582916
  473.9 396.9 %all-gather.8.cloned.1.call-start = ((), (), s32[]{:S(2)}) async-start(), calls=%async_computation.6 | async-start | bytes 9437184 | tf_op jit(solution)/shard_map/all_gather | solution.py:624
  474.0 137.3 %copy-start.46 = (f32[2048]{0:T(1024)S(1)}, f32[2048]{0:T(1024)}, u32[]{:S(2)}) copy-start(f32[2048]{0:T(1024)} %param.33) | copy-start | bytes 24580
  616.1 1.3 copy-start.22
  618.6 484.4 %all-reduce.7.cloned.1.call-start = ((), (), s32[]{:S(2)}) async-start(), calls=%async_computation.7 | async-start | bytes 8388608 | tf_op jit(solution)/shard_map/psum | solution.py:50
  786.5 6.8 copy-start.33
  793.3 77.5 %copy-start.9 = (bf16[256,2048]{1,0:T(8,128)(2,1)S(1)}, bf16[256,2048]{1,0:T(8,128)(2,1)}, u32[]{:S(2)}) copy-start(bf16[256,2048]{1,0:T(8,128)(2,1)} %weight.4) | copy-start | bytes 3145732
  798.2 82.6 %copy-start.19 = (bf16[2,1024,2,128]{3,1,2,0:T(8,128)(2,1)S(1)}, bf16[2,1024,2,128]{3,1,2,0:T(8,128)(2,1)}, u32[]{:S(2)}) copy-start(bf16[2,1024,2,128]{3,1,2,0:T(8,128)(2,1)} %copy-done.18) | copy-start | bytes 3145732
  880.8 5.0 copy-start.20
  884.1 2.5 copy-start.21
  886.6 1.3 copy-start.24
  889.3 1.8 copy-start.25
  895.2 2.2 copy-start.34
  896.9 1.2 copy-start.28
  898.1 1.0 copy-start.35
  900.1 5.0 copy-start.20
  903.3 2.5 copy-start.21
  905.8 1.3 copy-start.24
  908.5 1.8 copy-start.25
  914.4 2.2 copy-start.34
  916.1 1.2 copy-start.28
  919.5 6.3 copy-start.36
  919.5 6.4 copy-start.50
  925.9 2.6 copy-start.30
  925.9 7.2 slice-start
  928.5 4.6 slice-start.1
  931.1 2.0 copy-start.39
  936.4 1.2 copy-start.26
  942.7 1.9 copy-start.3
  944.6 1.2 copy-start.5
  945.8 1.2 copy-start.6
  947.0 1.2 copy-start.7
  948.3 98.9 %copy-start.27 = (bf16[2,1024,2,128]{1,3,2,0:T(8,128)(2,1)S(1)}, bf16[2,1024,2,128]{1,3,2,0:T(8,128)(2,1)}, u32[]{:S(2)}) copy-start(bf16[2,1024,2,128]{1,3,2,0:T(8,128)(2,1)} %get-tuple-element.121) | copy-start | bytes 3145732
  948.3 98.9 %copy-start.31 = (bf16[2,1024,2,128]{1,3,2,0:T(8,128)(2,1)S(1)}, bf16[2,1024,2,128]{1,3,2,0:T(8,128)(2,1)}, u32[]{:S(2)}) copy-start(bf16[2,1024,2,128]{1,3,2,0:T(8,128)(2,1)} %get-tuple-element.119) | copy-start | bytes 3145732
  948.3 99.3 %copy-start.48 = (f32[1024]{0:T(1024)S(1)}, f32[1024]{0:T(1024)}, u32[]{:S(2)}) copy-start(f32[1024]{0:T(1024)} %get-tuple-element.234) | copy-start | bytes 12292
  948.3 109.6 %copy-start.13 = (f32[2048]{0:T(1024)S(1)}, f32[2048]{0:T(1024)}, u32[]{:S(2)}) copy-start(f32[2048]{0:T(1024)} %param.22) | copy-start | bytes 24580
  1047.1 12.3 %copy-start.42 = (f32[2048]{0:T(1024)S(1)}, f32[2048]{0:T(1024)}, u32[]{:S(2)}) copy-start(f32[2048]{0:T(1024)} %get-tuple-element.155) | copy-start | bytes 24580
  1047.1 12.3 %copy-start.43 = (f32[2048]{0:T(1024)S(1)}, f32[2048]{0:T(1024)}, u32[]{:S(2)}) copy-start(f32[2048]{0:T(1024)} %get-tuple-element.146) | copy-start | bytes 24580
  1047.2 12.3 %copy-start.44 = (f32[2048]{0:T(1024)S(1)}, f32[2048]{0:T(1024)}, u32[]{:S(2)}) copy-start(f32[2048]{0:T(1024)} %get-tuple-element.202) | copy-start | bytes 24580
  1047.2 12.3 %copy-start.45 = (f32[2048]{0:T(1024)S(1)}, f32[2048]{0:T(1024)}, u32[]{:S(2)}) copy-start(f32[2048]{0:T(1024)} %get-tuple-element.228) | copy-start | bytes 24580
  1103.1 2.9 copy-start.41
  (9 other events, 7.9 us)
Sparse Core Ops, SparseCore 0:
  233.7 81.4 all-gather.3
  317.4 80.5 all-gather.5
  432.4 88.1 reduce-scatter.4
  523.3 87.9 reduce-scatter.2
  615.5 170.9 all-reduce.8
  788.0 82.7 all-gather.7
  936.6 102.7 all-reduce.6

commit v3 on v2

--- a/solution.py
+++ b/solution.py
@@ -46,8 +46,9 @@
     )
 
 
-def sum_groups(part):
-    return lax.psum(part.astype(jnp.bfloat16), "dp").astype(jnp.float32)
+def sum_groups(parts):
+    parts = [part.astype(jnp.bfloat16) for part in parts]
+    return [total.astype(jnp.float32) for total in lax.psum(parts, "dp")]
 
 
 def allowed_mask(first_row, row_count, slot_count, length):
@@ -252,13 +253,14 @@
 
     def unit(self, u):
         at = self.at
-        per = 2 * at.chips - 1
-        s, v = u // per, lax.rem(u, per)
-        j = v // 2
+        per = 2 * (at.chips - 1)
+        v = lax.rem(u, per)
+        last = u >= self.seqs * per
+        s = jnp.where(last, u - self.seqs * per, u // per)
         up = lax.rem(v, 2) == 0
-        last = v == per - 1
-        o = jnp.where(last, at.chip, jnp.where(up, at.chips - 1 - j, j))
-        there = last | jnp.where(up, o > at.chip, o < at.chip)
+        away = jnp.where(up, at.chips - 1 - v // 2, v // 2)
+        o = jnp.where(last, at.chip, away)
+        there = last | jnp.where(up, away > at.chip, away < at.chip)
         return s, o, there & (u >= 0) & (u < self.units())
 
     def side_copy(self, s, o):
@@ -474,10 +476,10 @@
                 line.part[s, o, :, cols] = total.astype(bf16)
             line.share(s, o)
 
-        line.pass_on(u - 1, final)
+        line.pass_on(u - 2, final)
         return carry
 
-    lax.fori_loop(0, line.units() + 1, step, 0)
+    lax.fori_loop(0, line.units() + 2, step, 0)
     line.finish()
 
 
@@ -527,10 +529,10 @@
                 line.part[s, o, :, cols] = total.astype(bf16)
             line.share(s, o)
 
-        line.pass_on(u - 1, final)
+        line.pass_on(u - 2, final)
         return carry
 
-    lax.fori_loop(0, line.units() + 1, step, 0)
+    lax.fori_loop(0, line.units() + 2, step, 0)
     line.finish()
 
 
@@ -549,6 +551,299 @@
         ),
         name="heads_scatter",
     )(query, key, value, weight)
+
+
+def normal_cdf(values):
+    x = jnp.clip(values * 0.7071067811865476, -3.832506856900711, 3.832506856900711)
+    x2 = x * x
+    top = 0.00022905065861350646
+    for c in (0.0034082910107109506, 0.050955695062380861, 0.18520832239976145, 1.128379143519084):
+        top = top * x2 + c
+    low = -1.1791602954361697e-7
+    for c in (
+        0.000023547966471313185,
+        0.0010179625278914885,
+        0.014070470171167667,
+        0.11098505178285362,
+        0.49746925110067538,
+        1.0,
+    ):
+        low = low * x2 + c
+    return 0.5 + 0.5 * (x * top / low)
+
+
+NT = (((1,), (1,)), ((), ()))
+TN = (((0,), (0,)), ((), ()))
+
+
+def mlp_kernel(
+    n,
+    normed,
+    grad_all,
+    up_weight,
+    up_bias,
+    down_weight,
+    mlp_part,
+    norm_grad,
+    up_grad,
+    up_bias_grad,
+    down_grad,
+    buf,
+    send,
+    recv,
+    *scratch,
+):
+    at = Place(n)
+    seqs, rows, width = normed.shape
+    units_wide = up_weight.shape[1]
+    line = Scatter(at, rows, *scratch[:7])
+    act, pre, out_stage, out_sem, up_stage, up_sem, down_stage, down_sem = scratch[7:]
+    ring = Gather(at, rows, buf, send, recv)
+    at.greet()
+    for s in range(seqs):
+        buf[s, rows_of(at.me, rows)] = normed[s]
+        ring.start(s)
+    up_bias_grad[...] = jnp.zeros_like(up_bias_grad)
+    ft = min(512, units_wide)
+
+    def out_copy(s, o):
+        return pltpu.make_async_copy(
+            out_stage, mlp_part.at[s, rows_of(o, 2 * rows)], out_sem.at[0]
+        )
+
+    def work(s, o, first):
+        ring.arrived(s, o, 1 - at.core)
+        here = rows_of(o, 2 * rows)
+        for j in range(units_wide // ft):
+            cols = pl.ds(j * ft, ft)
+            value = jnp.dot(buf[s, here], up_weight[:, cols], preferred_element_type=f32)
+            value = value + up_bias[:, cols]
+            spread = normal_cdf(value)
+            act[s, here, cols] = (value * spread).astype(bf16)
+            slope = spread + value * (0.3989422804014327 * jnp.exp(-0.5 * value * value))
+            grad = lax.dot_general(
+                grad_all[s, here], down_weight[cols], NT, preferred_element_type=f32
+            )
+            grad = (grad * slope).astype(bf16)
+            pre[s, here, cols] = grad
+            up_bias_grad[:, cols] += jnp.sum(grad.astype(f32), axis=0, keepdims=True)
+        for j in range(width // 512):
+            cols = pl.ds(j * 512, 512)
+            line.part[s, o, :, cols] = lax.dot_general(
+                pre[s, here], up_weight[cols], NT, preferred_element_type=f32
+            ).astype(bf16)
+        line.share(s, o)
+        pl.when(jnp.logical_not(first))(lambda: out_copy(s, o).wait())
+        for j in range(width // 512):
+            cols = pl.ds(j * 512, 512)
+            out_stage[:, cols] = jnp.dot(
+                act[s, here], down_weight[:, cols], preferred_element_type=f32
+            ).astype(bf16)
+        out_copy(s, o).start()
+
+    def final(s, there, total):
+        norm_grad[s, there] = total
+
+    down_tiles = down_grad.shape[0] // down_stage.shape[1]
+    up_tiles = up_grad.shape[0] // up_stage.shape[1]
+    flat = seqs * rows * n
+
+    def down_copy(t):
+        size = down_stage.shape[1]
+        return pltpu.make_async_copy(
+            down_stage.at[t % 2], down_grad.at[pl.ds(t * size, size)], down_sem.at[t % 2]
+        )
+
+    def up_copy(t):
+        size = up_stage.shape[1]
+        return pltpu.make_async_copy(
+            up_stage.at[t % 2], up_grad.at[pl.ds(t * size, size)], up_sem.at[t % 2]
+        )
+
+    def weight_tile(i):
+        for t in range(down_tiles):
+            @pl.when(i == t)
+            def _():
+                size = down_stage.shape[1]
+                if t >= 2:
+                    down_copy(t - 2).wait()
+                total = 0.0
+                for s in range(seqs):
+                    total += lax.dot_general(
+                        act[s, :, pl.ds(t * size, size)], grad_all[s], TN, preferred_element_type=f32
+                    )
+                down_stage[t % 2] = total.astype(bf16)
+                down_copy(t).start()
+        for t in range(up_tiles):
+            @pl.when(i == t + down_tiles)
+            def _():
+                size = up_stage.shape[1]
+                if t >= 2:
+                    up_copy(t - 2).wait()
+                total = 0.0
+                for s in range(seqs):
+                    total += lax.dot_general(
+                        buf[s, :, pl.ds(t * size, size)], pre[s], TN, preferred_element_type=f32
+                    )
+                up_stage[t % 2] = total.astype(bf16)
+                up_copy(t).start()
+
+    lag = ring.units() // seqs + 2
+
+    def step(u, carry):
+        ring.forward(u)
+        line.pass_on(u - lag, final)
+        s, o, there, own = ring.unit(u - 1)
+        pl.when(there)(lambda: work(s, o, u == 1))
+        weight_tile(u - ring.units() - 1)
+        return carry
+
+    count = max(line.units() + lag, ring.units() + 1 + down_tiles + up_tiles)
+    lax.fori_loop(0, count, step, 0)
+    ring.finish()
+    line.finish()
+    for t in range(max(down_tiles - 2, 0), down_tiles):
+        down_copy(t).wait()
+    for t in range(max(up_tiles - 2, 0), up_tiles):
+        up_copy(t).wait()
+    out_copy(0, 0).wait()
+
+
+def mlp_block(n, normed, grad_all, up_weight, up_bias, down_weight):
+    seqs, rows, width = normed.shape
+    slots = n * rows
+    units = up_weight.shape[1]
+    hbm = pl.BlockSpec(memory_space=pl.ANY)
+    vmem = pl.BlockSpec(memory_space=VMEM)
+    down_size, up_size = min(256, units), 512
+    return pl.pallas_call(
+        functools.partial(mlp_kernel, n),
+        out_shape=(
+            jax.ShapeDtypeStruct((seqs, slots, width), bf16),
+            jax.ShapeDtypeStruct((seqs, rows, width), f32),
+            jax.ShapeDtypeStruct((width, units), bf16),
+            jax.ShapeDtypeStruct((1, units), f32),
+            jax.ShapeDtypeStruct((units, width), bf16),
+        ),
+        in_specs=whole(5),
+        out_specs=(hbm, vmem, hbm, vmem, hbm),
+        scratch_shapes=[VMEM((seqs, slots, width), bf16)]
+        + Gather.scratch(n, seqs)
+        + Scatter.scratch(n, seqs, rows, width)
+        + [
+            VMEM((seqs, slots, units), bf16),
+            VMEM((seqs, slots, units), bf16),
+            VMEM((2 * rows, width), bf16),
+            DMA((1,)),
+            VMEM((2, up_size, units), bf16),
+            DMA((2,)),
+            VMEM((2, down_size, width), bf16),
+            DMA((2,)),
+        ],
+        compiler_params=pltpu.CompilerParams(
+            collective_id=3, has_side_effects=True, vmem_limit_bytes=60 * 2**20
+        ),
+        name="mlp_block",
+    )(normed, grad_all, up_weight, up_bias, down_weight)
+
+
+def attn_grad_kernel(
+    n,
+    grad,
+    mlp_part,
+    hidden,
+    bias,
+    weight,
+    mixed,
+    output,
+    grad_heads,
+    weight_grad,
+    buf,
+    send,
+    recv,
+    *scratch,
+):
+    at = Place(n)
+    seqs, rows, width = grad.shape
+    line = Scatter(at, rows, *scratch[:7])
+    load_sem = scratch[7]
+    ring = Gather(at, rows, buf, send, recv)
+
+    def load(s, o):
+        return pltpu.make_async_copy(
+            mlp_part.at[s, rows_of(o, 2 * rows)], line.part.at[s, o], load_sem.at[s, o]
+        )
+
+    def load_unit(u, carry):
+        s, o, there = line.unit(u)
+        pl.when(there)(lambda: load(s, o).start())
+        return carry
+
+    lax.fori_loop(0, line.units(), load_unit, 0)
+    at.greet()
+    for s in range(seqs):
+        buf[s, rows_of(at.me, rows)] = grad[s]
+        ring.start(s)
+
+    def final(s, there, total):
+        output[s, there] = (hidden[s, there] + total + bias[...]).astype(bf16)
+
+    def step(u, carry):
+        ring.forward(u)
+        s, o, there = line.unit(u)
+
+        @pl.when(there)
+        def _():
+            load(s, o).wait()
+            line.share(s, o)
+
+        line.pass_on(u - 1, final)
+        s, o, there, own = ring.unit(u - 1)
+
+        @pl.when(there)
+        def _():
+            ring.arrived(s, o, 1 - at.core)
+            here = rows_of(o, 2 * rows)
+            grad_heads[s, here] = lax.dot_general(
+                buf[s, here], weight[...], NT, preferred_element_type=f32
+            ).astype(bf16)
+
+        return carry
+
+    lax.fori_loop(0, max(line.units(), ring.units()) + 1, step, 0)
+    for j in range(width // 512):
+        cols = pl.ds(j * 512, 512)
+        total = 0.0
+        for s in range(seqs):
+            total += lax.dot_general(mixed[s], buf[s, :, cols], TN, preferred_element_type=f32)
+        weight_grad[:, cols] = total.astype(bf16)
+    ring.finish()
+    line.finish()
+
+
+def attn_grad(n, grad, mlp_part, hidden, bias, weight, mixed):
+    seqs, rows, width = grad.shape
+    slots = n * rows
+    part = weight.shape[0]
+    vmem = pl.BlockSpec(memory_space=VMEM)
+    return pl.pallas_call(
+        functools.partial(attn_grad_kernel, n),
+        out_shape=(
+            jax.ShapeDtypeStruct((seqs, rows, width), bf16),
+            jax.ShapeDtypeStruct((seqs, slots, part), bf16),
+            jax.ShapeDtypeStruct((part, width), bf16),
+        ),
+        in_specs=[vmem, pl.BlockSpec(memory_space=pl.ANY), vmem, vmem, vmem, vmem],
+        out_specs=tuple(whole(3)),
+        scratch_shapes=[VMEM((seqs, slots, width), bf16)]
+        + Gather.scratch(n, seqs)
+        + Scatter.scratch(n, seqs, rows, width)
+        + [DMA((seqs, n // 2))],
+        compiler_params=pltpu.CompilerParams(
+            collective_id=4, has_side_effects=True, vmem_limit_bytes=48 * 2**20
+        ),
+        name="attn_grad",
+    )(grad, mlp_part, hidden, bias, weight, mixed)
 
 
 def body(
@@ -588,16 +883,6 @@
     hidden_state, normed_two = project_scatter(
         n, mixed_heads, out_weight, tokens, out_bias[None], ln2_gain[None], ln2_shift[None]
     )
-    gathered_two = lax.all_gather(normed_two, "tensor", axis=1, tiled=True)
-    pre_act = flat_product(gathered_two, up_weight) + up_bias
-    activated = gelu_exact(pre_act).astype(jnp.bfloat16)
-    mlp_local = lax.psum_scatter(
-        flat_product(activated, down_weight).astype(jnp.bfloat16),
-        "tensor",
-        scatter_dimension=1,
-        tiled=True,
-    ).astype(jnp.float32)
-    output = (hidden_state + mlp_local + down_bias).astype(jnp.bfloat16)
     slot_ids = lax.axis_index("tensor") * local_rows + lax.broadcasted_iota(
         jnp.int32, (seq_count, local_rows), 1
     )
@@ -605,25 +890,25 @@
     grad_out = cotangent.astype(jnp.float32) * valid_rows[:, :, None]
     down_bias_grad = jnp.sum(grad_out, axis=(0, 1))
     grad_mlp = lax.all_gather(grad_out.astype(jnp.bfloat16), "tensor", axis=1, tiled=True)
-    down_weight_grad = sum_groups(rows_product(activated, grad_mlp))
-    grad_act = product_back(grad_mlp, down_weight)
-    unused_act, gelu_back = jax.vjp(gelu_exact, pre_act)
-    grad_pre = gelu_back(grad_act)[0].astype(jnp.bfloat16)
-    up_bias_grad = jnp.sum(grad_pre.astype(jnp.float32), axis=(0, 1))
-    up_weight_grad = sum_groups(rows_product(gathered_two, grad_pre))
-    norm_two_grad = lax.psum_scatter(
-        product_back(grad_pre, up_weight).astype(jnp.bfloat16),
-        "tensor",
-        scatter_dimension=1,
-        tiled=True,
-    ).astype(jnp.float32)
+    mlp_part, norm_two_grad, up_weight_grad, up_bias_grad, down_weight_grad = mlp_block(
+        n, normed_two, grad_mlp, up_weight, up_bias[None], down_weight
+    )
+    up_bias_grad = up_bias_grad[0]
+    up_weight_grad, down_weight_grad = sum_groups((up_weight_grad, down_weight_grad))
     unused_two, norm_two_back = jax.vjp(layer_norm, hidden_state, ln2_gain, ln2_shift)
     hidden_ln_grad, ln2_gain_grad, ln2_shift_grad = norm_two_back(norm_two_grad)
     hidden_grad = grad_out + hidden_ln_grad
     out_bias_grad = jnp.sum(hidden_grad, axis=(0, 1))
-    grad_attn = lax.all_gather(hidden_grad.astype(jnp.bfloat16), "tensor", axis=1, tiled=True)
-    out_weight_grad = rows_product(mixed_heads, grad_attn)
-    grad_heads = product_back(grad_attn, out_weight).astype(jnp.bfloat16).reshape(head_shape)
+    output, grad_heads, out_weight_grad = attn_grad(
+        n,
+        hidden_grad.astype(jnp.bfloat16),
+        mlp_part,
+        hidden_state,
+        down_bias[None],
+        out_weight,
+        mixed_heads,
+    )
+    grad_heads = grad_heads.reshape(head_shape)
     grad_query, grad_key, grad_value = lax.map(
         lambda item: attend_backward(item[0], item[1], item[2], item[3], item[4], item[5]),
         (query_rows, key_rows, value_rows, grad_heads, log_totals, lengths),
@@ -642,8 +927,7 @@
     qkv_weight_grad, out_weight_grad, up_weight_grad, down_weight_grad = lax.optimization_barrier(
         (qkv_weight_grad, out_weight_grad, up_weight_grad, down_weight_grad)
     )
-    qkv_weight_grad = sum_groups(qkv_weight_grad)
-    out_weight_grad = sum_groups(out_weight_grad)
+    qkv_weight_grad, out_weight_grad = sum_groups((qkv_weight_grad, out_weight_grad))
     qkv_bias_grad = jnp.stack(
         [
             score_scale * jnp.sum(grad_query.astype(jnp.float32), axis=(0, 1)),

time: 1120 us -> 1020 us (0.911)
  Pallas kernels: 279 us -> 672 us
  waiting for transfers between devices: 494 us -> 121 us
  matrix products: 147 us -> 45.4 us
  other arithmetic: 74.4 us -> 49.3 us
    pallas_call x0 -> x2, Pallas kernels: none -> 339 us  [the longest x1 187 us: mlp_block(): pl.pallas_call(functools.partial(mlp_kernel, n), out_shape=(jax.ShapeDtyp...]
    all_gather x2 -> x0, waiting for transfers between devices: 151 us -> none  [the longest x1 78.8 us: body(): gathered_two = lax.all_gather(normed_two, 'tensor', axis=1, tiled=True)]
    reduce_scatter x2 -> x0, waiting for transfers between devices: 132 us -> none  [the longest x1 85.3 us: body(): lax.psum_scatter(flat_product(activated, down_weight).astype(jnp.bfloat16...]
    dot_general x5 -> x0, matrix products: 68.6 us -> none  [the longest x3 39.1 us: product_back(): lax.dot_general(flat, right_rows, (((1,), (1,)), ((), ())), preferred_ele...]
    pallas_call x1, Pallas kernels: 78.3 us -> 145 us  [gather_project(): pl.pallas_call(functools.partial(gather_project_kernel, n), out_shape=(ja...]
    psum x2, waiting for transfers between devices: 167 us -> 121 us  [sum_groups(): return [total.astype(jnp.float32) for total in lax.psum(parts, 'dp')]]
    all_gather x1, waiting for transfers between devices: 43.2 us -> 0.02 us  [body(): lax.all_gather(grad_out.astype(jnp.bfloat16), 'tensor', axis=1, tiled=True)]
    dot_general x6 -> x3, matrix products: 42.3 us -> 13.1 us  [rows_product(): lax.dot_general(left_flat, right_flat, (((0,), (0,)), ((), ())), preferre...]
  transfers between devices with their start and end apart: 7 -> 3, of which waited for: 6 -> 1; matrix products, arithmetic and copies ran while one was open for 10% -> 10% of each run, Pallas kernels for 9% -> 33%
where the time goes in v3:
time: 1020 us; the launch traced here: 1010 us
  Pallas kernels  672 us (66%)
  waiting for transfers between devices  121 us (12%)
  local copies, waits for them, and re-layouts  53.2 us (5%)
  blocking collectives  50.6 us (5%)
  other arithmetic  49.3 us (5%)
  matrix products  45.4 us (4%)
  between operations  14.7 us (1%)
    pallas_call x1, Pallas kernels, mlp_block(): pl.pallas_call(functools.partial(mlp_kernel, n), out_shape=(jax.ShapeDtyp...  187 us
    pallas_call x1, Pallas kernels, attn_grad(): pl.pallas_call(functools.partial(attn_grad_kernel, n), out_shape=(jax.Sha...  152 us
    pallas_call x1, Pallas kernels, gather_project(): pl.pallas_call(functools.partial(gather_project_kernel, n), out_shape=(ja...  145 us
    psum x2, waiting for transfers between devices, sum_groups(): return [total.astype(jnp.float32) for total in lax.psum(parts, 'dp')]  121 us
    pallas_call x1, Pallas kernels, heads_scatter(): pl.pallas_call(functools.partial(heads_scatter_kernel, n), out_shape=jax....  95.4 us
    pallas_call x1, Pallas kernels, project_scatter(): pl.pallas_call(functools.partial(project_scatter_kernel, n), out_shape=(j...  92.2 us
    psum x1, blocking collectives, body(): lax.psum((ln1_gain_grad, ln1_shift_grad, out_bias_grad, ln2_gain_grad, ln...  40 us
  transfers between devices with their start and end apart: 3, of which 1 were waited for; matrix products, arithmetic and copies ran while one was open for 10% of the time, Pallas kernels for 33%

profile of v3, /device:TPU:0, one launch (start us, length us, event | category | flops | bytes accessed | tf_op | source)
XLA Modules:
  0.0 1006.4 jit_solution(3294141833072498903)
XLA Ops:
  8.1 2.4 fusion.84
  10.7 1.9 copy-done.2
  12.5 144.7 %gather_project.1 = (bf16[2,1024,2048]{2,1,0:T(8,128)(2,1)}, bf16[3,2,1024,256]{3,2,1,0:T(8,128)(2,1)S(1)}) custom-call(bf16[2,128,2048]{2,1,0:T(8,128)(2,1)S(1)} %copy-done.1, f32[1,2048]{1,0:T(1,128)S(1)} %bitcast.225, f32[1,2048]{1,0:T(1,128)S(1)} %bitcast.227, bf16[3,2048,256]{2,1,0:T(8,128)(2,1)S(1)} %copy-done.2, f32[2,256]{1,0:T(2,128)S(1)} %copy-done.20), custom_call_target="tpu_custom_call" | custom-call | tf_op jit(solution)/shard_map/gather_project/pallas_call | solution.py:436
  157.3 1.5 fusion.92
  159.2 2.1 reshape_squeeze.9
  161.4 1.3 reshape_squeeze.10
  164.9 28.1 %while.26 = (s32[]{:T(128)}, bf16[2,1024,2,128]{1,3,2,0:T(8,128)(2,1)}, f32[2,2,1024,1]{2,1,3,0:T(2,128)S(1)}, bf16[2,1024,2,128]{3,2,1,0:T(2,128)(2,1)}, s32[2]...) while((s32[]{:T(128)}, ...), condition=%wide.region_5.6_spmd, body=%wide.region_0.5_spmd.sunk | while | flops 1093666304 | bytes 46220008 | solution.py:878
  166.2 1.4 constant_dynamic-slice_fusion.7
  167.6 1.1 copy.91
  169.2 1.9 select_reduce_fusion.4
  171.1 1.9 select_reduce_fusion.5
  173.0 2.2 exponential_reduce_fusion.3
  175.2 1.3 fusion.131
  176.6 1.3 fusion.132
  180.2 1.4 constant_dynamic-slice_fusion.7
  183.3 1.9 select_reduce_fusion.4
  185.2 1.9 select_reduce_fusion.5
  187.0 2.2 exponential_reduce_fusion.3
  189.3 1.3 fusion.131
  190.7 1.3 fusion.132
  193.1 2.7 copy.58.mixed
  195.8 1.2 copy-done.4
  197.0 1.2 copy-done.5
  198.2 92.2 %project_scatter.1 = (f32[2,128,2048]{2,1,0:T(8,128)S(1)}, bf16[2,128,2048]{2,1,0:T(8,128)(2,1)S(1)}) custom-call(bf16[2,1024,256]{2,1,0:T(8,128)(2,1)S(1)} %copy-done.4, bf16[256,2048]{1,0:T(8,128)(2,1)S(1)} %copy-done.5, bf16[2,128,2048]{2,1,0:T(8,128)(2,1)S(1)} %copy-done.1, f32[1,2048]{1,0:T(1,128)S(1)} %bitcast.228, f32[1,2048]{1,0:T(1,128)S(1)} %bitcast.226, ...), custom_call_target="tpu_custom_call" | custom-call | tf_op jit(solution)/shard_map/project_scatter/pallas_call | solution.py:488
  292.0 187.3 %mlp_block.1 = (bf16[2,1024,2048]{2,1,0:T(8,128)(2,1)}, f32[2,128,2048]{2,1,0:T(8,128)}, bf16[2048,1024]{1,0:T(8,128)(2,1)}, f32[1,1024]{1,0:T(1,128)}, bf16[1024,2048]{1,0:T(8,128)(2,1)}) custom-call(bf16[2,128,2048]{2,1,0:T(8,128)(2,1)} %copy-done.10, bf16[2,1024,2048]{2,1,0:T(8,128)(2,1)} %all-gather.2.cloned.1.call-done.grad_all, ...), custom_call_target="tpu_custom_call" | custom-call | tf_op jit(solution)/shard_map/mlp_block/pallas_call | solution.py:719
  479.3 3.1 multiply_reduce_fusion.2
  485.0 152.2 %attn_grad.1 = (bf16[2,128,2048]{2,1,0:T(8,128)(2,1)S(1)}, bf16[2,1024,256]{2,1,0:T(8,128)(2,1)S(1)}, bf16[256,2048]{1,0:T(8,128)(2,1)}) custom-call(bf16[2,128,2048]{2,1,0:T(8,128)(2,1)S(1)} %fusion.87.grad, bf16[2,1024,2048]{2,1,0:T(8,128)(2,1)} %get-tuple-element.127.mlp_part, f32[2,128,2048]{2,1,0:T(8,128)} %copy-done, f32[1,2048]{1,0:T(1,128)S(1)} %bitcast.230, ...), custom_call_target="tpu_custom_call" | custom-call | tf_op jit(solution)/shard_map/attn_grad/pallas_call | solution.py:829
  638.1 1.1 reshape.307
  642.7 38.0 %while.27 = (s32[]{:T(128)}, bf16[2,1024,2,128]{1,3,2,0:T(8,128)(2,1)}, bf16[2,1024,2,128]{1,3,2,0:T(8,128)(2,1)}, bf16[2,1024,2,128]{1,3,2,0:T(8,128)(2,1)}, bf...) while((s32[]{:T(128)}, ...), condition=%wide.region_13.14_spmd, body=%wide.region_10.13_spmd.sunk | while | flops 2713189888 | bytes 103369048 | solution.py:912
  644.0 1.4 constant_dynamic-slice_fusion.8
  645.4 1.4 constant_dynamic-slice_fusion.9
  648.8 1.3 fusion.151
  650.3 1.3 fusion.152
  651.7 1.5 multiply_reduce_fusion.8
  653.2 1.5 multiply_reduce_fusion.7
  654.7 2.3 multiply_convert_fusion.3
  662.9 1.4 constant_dynamic-slice_fusion.8
  664.3 1.5 constant_dynamic-slice_fusion.9
  667.8 1.3 fusion.151
  669.2 1.3 fusion.152
  670.5 1.5 multiply_reduce_fusion.8
  672.0 1.5 multiply_reduce_fusion.7
  673.5 2.3 multiply_convert_fusion.3
  680.7 6.7 convolution_bitcast_fusion.2
  687.4 2.6 convolution_bitcast_fusion.3
  690.0 3.9 fusion.74
  693.9 2.0 pad_maximum_fusion
  695.9 120.5 %all-reduce.9.cloned.1.call-done = (bf16[2048,1024]{1,0:T(8,128)(2,1)}, bf16[1024,2048]{1,0:T(8,128)(2,1)}) async-done(((bf16[2048,1024]{1,0:T(8,128)(2,1)}, bf16[1024,2048]{1,0:T(8,128)(2,1)}), (bf16[2048,1024]{1,0:T(8,128)(2,1)}, bf16[1024,2048]{1,0:T(8,128)(2,1)})) %all-reduce.9.cloned.1.call-update) | async-done | bytes 8388624 | tf_op jit(solution)/shard_map/psum | solution.py:51
  816.4 6.8 convert_element_type.93
  823.2 4.4 convert_element_type.94
  828.9 1.3 copy.61.value
  830.2 2.3 copy.59.query
  832.5 1.3 copy.60.key
  833.7 2.0 copy-done.3
  835.8 1.2 copy-done.7
  837.0 1.2 copy-done.8
  838.2 1.2 copy-done.9
  839.5 95.4 %heads_scatter.1 = f32[2,128,2048]{2,1,0:T(8,128)S(1)} custom-call(bf16[2,1024,256]{2,1,0:T(8,128)(2,1)S(1)} %copy-done.8, bf16[2,1024,256]{2,1,0:T(8,128)(2,1)S(1)} %copy-done.9, bf16[2,1024,256]{2,1,0:T(8,128)(2,1)S(1)} %copy-done.7, bf16[3,2048,256]{2,1,0:T(8,128)(2,1)S(1)} %copy-done.3), custom_call_target="tpu_custom_call" | custom-call | tf_op jit(solution)/shard_map/heads_scatter/pallas_call | solution.py:543
  934.9 1.6 convert_reduce_fusion.1
  936.5 10.6 %all-reduce.1 = (f32[2,256]{1,0:T(2,128)}, f32[1024]{0:T(1024)}) all-reduce(f32[2,256]{1,0:T(2,128)S(1)} %pad_maximum_fusion.1, f32[1024]{0:T(1024)S(1)} %bitcast.240), channel_id=1, replica_groups=mesh['dp'=4,'tensor'=8] {'dp'}, use_global_device_ids=true, to_apply=%region_27.28 | all-reduce | flops 1536 | bytes 12288 | tf_op jit(solution)/shard_map/psum | solution.py:941
  949.7 2.6 fusion.83
  952.3 40.0 %all-reduce = (f32[2048]{0:T(1024)}, f32[2048]{0:T(1024)}, f32[2048]{0:T(1024)}, f32[2048]{0:T(1024)}, f32[2048]{0:T(1024)}, /*index=5*/f32[2048]{0:T(1024)}) all-reduce(f32[2048]{0:T(1024)S(1)} %get-tuple-element.162, f32[2048]{0:T(1024)S(1)} %get-tuple-element.165, ...), channel_id=1, replica_groups=mesh['dp'=4,'tensor'=8] {'dp','tensor'}, use_global_device_ids=true, to_apply=%region_19.20 | all-reduce | flops 12288 | bytes 98304 | tf_op jit(solution)/shard_map/psum | solution.py:943
  992.2 2.9 convert_element_type.99
  995.2 3.2 convert_element_type.96
  (187 shorter events, 39.5 us)
Async XLA Ops:
  7.2 3.4 copy-start.1
  7.2 3.4 copy-start.13
  7.2 3.4 copy-start.20
  7.2 3.4 copy-start.16
  7.2 284.8 %all-gather.2.cloned.1.call-start = ((), (), s32[]{:S(2)}) async-start(), calls=%async_computation | async-start | bytes 9437184 | tf_op jit(solution)/shard_map/all_gather | solution.py:892
  8.1 475.0 %copy-start.43 = (f32[2,128]{1,0:T(2,128)}, f32[2,128]{1,0:T(2,128)S(1)}, u32[]{:S(2)}) copy-start(f32[2,128]{1,0:T(2,128)S(1)} %compare_convert_fusion) | copy-start | bytes 3076
  10.5 805.9 %all-reduce.9.cloned.1.call-start = ((), (), s32[]{:S(2)}) async-start(), calls=%async_computation.2 | async-start | bytes 16777216 | tf_op jit(solution)/shard_map/psum | solution.py:51
  10.6 1.9 copy-start.2
  162.7 2.2 copy-start.48
  173.0 2.3 copy-start.26
  176.6 1.4 copy-start.38
  178.0 1.0 copy-start.39
  187.0 2.3 copy-start.26
  190.6 1.4 copy-start.38
  192.1 1.0 copy-start.39
  193.1 2.7 copy-start.21
  193.1 2.7 copy-start.15
  193.1 2.7 copy-start.17
  193.1 2.7 copy-start.18
  195.8 1.2 copy-start.4
  197.0 1.2 copy-start.5
  290.4 1.0 copy-start.10
  291.4 191.0 %copy-start = (f32[2,128,2048]{2,1,0:T(8,128)}, f32[2,128,2048]{2,1,0:T(8,128)S(1)}, u32[]{:S(2)}) copy-start(f32[2,128,2048]{2,1,0:T(8,128)S(1)} %get-tuple-element.126.hidden) | copy-start | bytes 6291460
  479.3 3.1 copy-start.33
  482.4 1.2 copy-start.31
  483.0 1.3 copy-start.24
  483.1 1.3 copy-start.45
  483.6 1.4 copy-start.6
  483.6 1.4 copy-start.19
  637.2 1.0 copy-start.11
  639.3 3.4 copy-start.22
  639.3 352.9 %all-reduce.7.cloned.1.call-start = ((), (), s32[]{:S(2)}) async-start(), calls=%async_computation.1 | async-start | bytes 8388608 | tf_op jit(solution)/shard_map/psum | solution.py:51
  642.7 4.6 copy-start.23
  648.8 1.5 copy-start.27
  651.6 3.0 copy-start.28
  658.7 1.2 copy-start.35
  660.5 1.1 copy-start.36
  661.6 4.7 copy-start.23
  667.8 1.4 copy-start.27
  670.5 3.0 copy-start.28
  677.6 1.2 copy-start.35
  679.3 1.1 copy-start.36
  680.7 6.7 copy-start.37
  680.7 6.8 copy-start.49
  816.4 6.8 copy-start.34
  827.7 1.2 copy-start.29
  833.7 2.0 copy-start.3
  835.8 1.2 copy-start.7
  837.0 1.2 copy-start.8
  838.2 1.2 copy-start.9
  839.5 95.4 %copy-start.30 = (bf16[2,1024,2,128]{1,3,2,0:T(8,128)(2,1)S(1)}, bf16[2,1024,2,128]{1,3,2,0:T(8,128)(2,1)}, u32[]{:S(2)}) copy-start(bf16[2,1024,2,128]{1,3,2,0:T(8,128)(2,1)} %get-tuple-element.133) | copy-start | bytes 3145732
  934.9 1.6 copy-start.47
  934.9 12.2 %copy-start.14 = (f32[2048]{0:T(1024)S(1)}, f32[2048]{0:T(1024)}, u32[]{:S(2)}) copy-start(f32[2048]{0:T(1024)} %param.22) | copy-start | bytes 24580
  947.8 1.6 copy-start.25
  947.8 1.8 copy-start.32
  947.8 1.8 copy-start.44
  947.8 1.8 copy-start.46
  949.7 2.6 copy-start.41
  949.7 2.6 copy-start.42
  992.2 2.9 copy-start.40
  995.2 3.2 copy-start.12
Sparse Core Ops, SparseCore 0:
  10.7 112.4 all-gather.1
  639.4 176.9 all-reduce.8
  827.8 104.8 all-reduce.6

commit v4 on v3

--- a/solution.py
+++ b/solution.py
@@ -120,6 +120,8 @@
 DMA = pltpu.SemaphoreType.DMA
 f32 = jnp.float32
 bf16 = jnp.bfloat16
+NT = (((1,), (1,)), ((), ()))
+TN = (((0,), (0,)), ((), ()))
 
 
 class Place:
@@ -130,8 +132,19 @@
         self.side = self.me + 1 - 2 * self.core
         self.below = self.chip > 0
         self.above = self.chip < self.chips - 1
-
-    def greet(self):
+        self.group = lax.axis_index("dp")
+        self.group_bits = lax.axis_size("dp").bit_length() - 1
+        self.bits = n.bit_length() - 1
+
+    def group_peer(self, q):
+        mine = lax.rem(self.group // 2**q, 2)
+        return self.group + (1 - 2 * mine) * 2**q, mine
+
+    def peer(self, q):
+        mine = lax.rem(self.me // 2**q, 2)
+        return self.me + (1 - 2 * mine) * 2**q
+
+    def greet(self, groups=False, cube=False):
         barrier = pltpu.get_barrier_semaphore()
 
         def tell(target):
@@ -143,6 +156,16 @@
         pl.when(self.below)(lambda: tell(self.me - 2))
         pl.when(self.above)(lambda: tell(self.me + 2))
         peers = 1 + self.below.astype(jnp.int32) + self.above.astype(jnp.int32)
+        if groups:
+            for q in range(self.group_bits):
+                pl.semaphore_signal(
+                    barrier, inc=1, device_id={"dp": self.group_peer(q)[0]}, device_id_type=MESH
+                )
+            peers = peers + self.group_bits
+        if cube:
+            for q in range(self.bits):
+                tell(self.peer(q))
+            peers = peers + self.bits
         pl.semaphore_wait(barrier, peers)
 
 
@@ -208,6 +231,8 @@
         at = self.at
         s, o, there, own = self.unit(u)
 
+        pl.when(there & own & (s > 0))(lambda: self.start(s))
+
         @pl.when(there & jnp.logical_not(own))
         def _():
             self.arrived(s, o, at.core)
@@ -370,10 +395,205 @@
         lax.fori_loop(0, self.seqs * at.chips, one, 0)
 
 
+class GroupSum:
+    def __init__(self, at, rows, tiles, inbox, send, recv, keep_sem, out, turn=0, skip=0):
+        self.at, self.tiles, self.inbox, self.send, self.recv = at, tiles, inbox, send, recv
+        self.keep_sem, self.out, self.skip, self.turn, self.rows = keep_sem, out, skip, turn, rows
+        self.bits = at.group_bits
+        self.count = send.shape[0]
+
+    @staticmethod
+    def scratch(dp, count, rows, width, skip=0):
+        phases = 2 * (dp.bit_length() - 1)
+        return [
+            VMEM((count, rows >> skip, width), bf16),
+            VMEM((count, rows - rows // dp, width), bf16),
+            DMA((count, phases)),
+            DMA((count, phases)),
+            DMA((count,)),
+        ]
+
+    def peer(self, t, i):
+        which = lax.rem(t + i + self.turn, self.bits)
+        peer, mine = 0, 0
+        for q in range(self.bits):
+            other, bit = self.at.group_peer(q)
+            peer = peer + jnp.where(which == q, other, 0)
+            mine = mine + jnp.where(which == q, bit, 0)
+        return peer, mine
+
+    def base(self, t, i):
+        first = 0
+        for p in range(i):
+            first = first + self.peer(t, p)[1] * (self.rows >> (p + 1))
+        return first
+
+    def span(self, first, size):
+        return pl.ds(pl.multiple_of(first, 16), size)
+
+    def tile(self, t, first, size):
+        return self.tiles.at[t, self.span(first - self.base(t, self.skip), size)]
+
+    def box(self, t, i):
+        return self.inbox.at[t, pl.ds(self.rows - (self.rows >> i), self.rows >> (i + 1))]
+
+    def remote(self, source, target, t, phase, peer):
+        return pltpu.make_async_remote_copy(
+            src_ref=source,
+            dst_ref=target,
+            send_sem=self.send.at[t, phase],
+            recv_sem=self.recv.at[t, phase],
+            device_id={"dp": peer},
+            device_id_type=MESH,
+        )
+
+    def halve(self, t, i):
+        peer, mine = self.peer(t, i)
+        half = self.rows >> (i + 1)
+        source = self.tile(t, self.base(t, i) + (1 - mine) * half, half)
+        return self.remote(source, self.box(t, i), t, i, peer)
+
+    def add(self, t, i):
+        half = self.rows >> (i + 1)
+        keep = self.base(t, i + 1) - self.base(t, self.skip)
+        box = self.rows - (self.rows >> i)
+
+        def body(j, carry):
+            here = self.span(keep + j * 16, 16)
+            there = self.span(box + j * 16, 16)
+            total = self.tiles[t, here].astype(f32) + self.inbox[t, there].astype(f32)
+            self.tiles[t, here] = total.astype(bf16)
+            return carry
+
+        lax.fori_loop(0, half // 16, body, 0)
+
+    def keep(self, t):
+        first, size = self.base(t, self.bits), self.rows >> self.bits
+        return pltpu.make_async_copy(
+            self.tile(t, first, size), self.out.at[t, self.span(first, size)], self.keep_sem.at[t]
+        )
+
+    def double(self, t, i, back=False):
+        peer, mine = self.peer(t, i)
+        half = self.rows >> (i + 1)
+        first = self.base(t, i) + ((1 - mine) if back else mine) * half
+        piece = self.out.at[t, self.span(first, half)]
+        source = piece
+        if i == self.bits - 1 and not back:
+            source = self.tile(t, first, half)
+        return self.remote(source, piece, t, 2 * self.bits - 1 - i, peer)
+
+    def events(self):
+        return self.count * (2 * self.bits + 1 - self.skip)
+
+    def event(self, e, loaded=None):
+        k, t = e // self.count + self.skip, lax.rem(e, self.count)
+        bits = self.bits
+
+        def at_stage(stage):
+            if stage == 0:
+                self.halve(t, 0).start()
+            elif stage <= bits:
+                if stage > self.skip:
+                    self.halve(t, stage - 1).wait_recv()
+                else:
+                    loaded(t)
+                self.add(t, stage - 1)
+                if stage < bits:
+                    self.halve(t, stage).start()
+                else:
+                    self.keep(t).start()
+                    self.double(t, bits - 1).start()
+            else:
+                i = 2 * bits - stage
+                self.double(t, i, back=True).wait_recv()
+                if i == bits - 1:
+                    self.keep(t).wait()
+                if i > 0:
+                    self.double(t, i - 1).start()
+
+        for stage in range(self.skip, 2 * bits + 1):
+            pl.when((k == stage) & (e >= 0))(functools.partial(at_stage, stage))
+
+    def finish(self):
+        def one(t, carry):
+            for i in range(self.bits):
+                if i >= self.skip:
+                    self.halve(t, i).wait_send()
+                self.double(t, i).wait_send()
+            return carry
+
+        lax.fori_loop(0, self.count, one, 0)
+
+
+class SmallSum:
+    def __init__(self, at, rows, inbox, send, recv, everywhere):
+        self.at, self.rows, self.inbox, self.send, self.recv = at, rows, inbox, send, recv
+        self.phases = at.group_bits + (at.bits if everywhere else 0)
+
+    @staticmethod
+    def scratch(dp, n, count, width, everywhere):
+        phases = (dp.bit_length() - 1) + (n.bit_length() - 1 if everywhere else 0)
+        return [
+            VMEM((phases + 1, count, width), f32),
+            VMEM((phases, count, width), f32),
+            DMA((phases,)),
+            DMA((phases,)),
+        ]
+
+    def copy(self, i):
+        at = self.at
+        if i < at.group_bits:
+            target = {"dp": at.group_peer(i)[0]}
+        else:
+            target = {"tensor": at.peer(i - at.group_bits)}
+        return pltpu.make_async_remote_copy(
+            src_ref=self.rows.at[i],
+            dst_ref=self.inbox.at[i],
+            send_sem=self.send.at[i],
+            recv_sem=self.recv.at[i],
+            device_id=target,
+            device_id_type=MESH,
+        )
+
+    def event(self, e):
+        def run(i):
+            if i > 0:
+                self.copy(i - 1).wait_recv()
+                self.rows[i] = self.rows[i - 1] + self.inbox[i - 1]
+            if i < self.phases:
+                self.copy(i).start()
+
+        for i in range(self.phases + 1):
+            if isinstance(e, int):
+                if e == i:
+                    run(i)
+            else:
+                pl.when(e == i)(functools.partial(run, i))
+
+    def finish(self):
+        for i in range(self.phases):
+            self.copy(i).wait_send()
+
+
 def norm_rows(values, gain, shift):
     centre = values - jnp.mean(values, axis=-1, keepdims=True)
     spread = jnp.mean(centre * centre, axis=-1, keepdims=True)
     return centre * lax.rsqrt(spread + norm_epsilon) * gain + shift
+
+
+def norm_rows_back(values, grad, gain):
+    centre = values - jnp.mean(values, axis=-1, keepdims=True)
+    scale = lax.rsqrt(jnp.mean(centre * centre, axis=-1, keepdims=True) + norm_epsilon)
+    unit = centre * scale
+    w = grad * gain
+    back = w - jnp.mean(w, axis=-1, keepdims=True)
+    back = scale * (back - unit * jnp.mean(w * unit, axis=-1, keepdims=True))
+    return back, grad * unit
+
+
+def add_row(ref, row, values):
+    ref[row : row + 1] += jnp.sum(values, axis=0, keepdims=True)
 
 
 def gather_project_kernel(
@@ -391,7 +611,8 @@
             return carry
 
         lax.fori_loop(0, rows // 16, block, 0)
-        ring.start(s)
+        if s == 0:
+            ring.start(s)
 
     def keep(s, o):
         here = rows_of(o, 2 * rows)
@@ -501,14 +722,56 @@
     )(mixed, weight, tokens, bias, gain, shift)
 
 
-def heads_scatter_kernel(n, query, key, value, weight, grad, *scratch):
+def heads_scatter_kernel(
+    n,
+    query,
+    key,
+    value,
+    weight,
+    gathered,
+    out_part,
+    tokens,
+    gain,
+    hidden_grad,
+    bias_part,
+    grad,
+    sums_all,
+    weight_grad,
+    out_grad,
+    bias_grad,
+    *scratch,
+):
     at = Place(n)
-    seqs, rows, width = grad.shape
-    line = Scatter(at, rows, *scratch)
-    at.greet()
+    seqs, rows, width = hidden_grad.shape
+    line = Scatter(at, rows, *scratch[:7])
+    weight_sum = GroupSum(at, width, *scratch[7:12], weight_grad)
+    out_sum = GroupSum(at, out_part.shape[0], *scratch[12:17], out_grad, turn=1)
+    small = SmallSum(at, *scratch[17:21], True)
+    small_bias = SmallSum(at, *scratch[21:25], False)
+    out_sum.tiles[0] = out_part[...]
+    small.rows[0] = jnp.zeros(small.rows.shape[1:], f32)
+    small_bias.rows[0] = bias_part[...]
+    at.greet(groups=True, cube=True)
 
     def final(s, there, total):
-        grad[s, there] = total
+        back, terms = norm_rows_back(tokens[s, there].astype(f32), total, gain[...])
+        grad[s, there] = hidden_grad[s, there] + back
+        small.rows[0, 0:1] += jnp.sum(terms, axis=0, keepdims=True)
+        small.rows[0, 1:2] += jnp.sum(total, axis=0, keepdims=True)
+
+    parts = ((query, HD ** (-0.5)), (key, 1.0), (value, 1.0))
+
+    def weight_tile(j):
+        for first in range(0, width, 512):
+            total = 0.0
+            for s in range(seqs):
+                total += lax.dot_general(
+                    gathered[s, :, pl.ds(first, 512)],
+                    parts[j][0][s],
+                    TN,
+                    preferred_element_type=f32,
+                )
+            weight_sum.tiles[j, pl.ds(first, 512)] = (parts[j][1] * total).astype(bf16)
 
     def step(u, carry):
         s, o, there = line.unit(u)
@@ -519,38 +782,64 @@
             for j in range(width // 512):
                 cols = pl.ds(j * 512, 512)
                 total = 0.0
-                for part, scale, i in ((query, HD ** (-0.5), 0), (key, 1.0, 1), (value, 1.0, 2)):
-                    total += scale * lax.dot_general(
-                        part[s, here],
-                        weight[i, cols],
-                        (((1,), (1,)), ((), ())),
-                        preferred_element_type=f32,
+                for i in range(3):
+                    total += parts[i][1] * lax.dot_general(
+                        parts[i][0][s, here], weight[i, cols], NT, preferred_element_type=f32
                     )
                 line.part[s, o, :, cols] = total.astype(bf16)
             line.share(s, o)
 
         line.pass_on(u - 2, final)
+        for j in range(3):
+            pl.when(u == j)(functools.partial(weight_tile, j))
+        pl.when(u < weight_sum.events())(lambda: weight_sum.event(u))
+        pl.when(lax.rem(u, 3) == 0)(lambda: out_sum.event(u // 3))
+        small_bias.event(u)
         return carry
 
-    lax.fori_loop(0, line.units() + 2, step, 0)
+    count = max(line.units() + 2, weight_sum.events(), 3 * out_sum.events())
+    lax.fori_loop(0, count, step, 0)
+    for e in range(small.phases + 1):
+        small.event(e)
+    sums_all[...] = small.rows[small.phases]
+    bias_grad[...] = small_bias.rows[small_bias.phases]
     line.finish()
-
-
-def heads_scatter(n, query, key, value, weight):
+    weight_sum.finish()
+    out_sum.finish()
+    small.finish()
+    small_bias.finish()
+
+
+def heads_scatter(
+    n, query, key, value, weight, gathered, out_part, tokens, gain, hidden_grad, bias_part
+):
     seqs, slots, part = query.shape
     width = weight.shape[1]
     rows = slots // n
+    dp = lax.axis_size("dp")
+    vmem = pl.BlockSpec(memory_space=VMEM)
+    hbm = pl.BlockSpec(memory_space=pl.ANY)
     return pl.pallas_call(
         functools.partial(heads_scatter_kernel, n),
-        out_shape=jax.ShapeDtypeStruct((seqs, rows, width), f32),
-        in_specs=whole(4),
-        out_specs=whole(1)[0],
-        scratch_shapes=Scatter.scratch(n, seqs, rows, width),
+        out_shape=(
+            jax.ShapeDtypeStruct((seqs, rows, width), f32),
+            jax.ShapeDtypeStruct((2, width), f32),
+            jax.ShapeDtypeStruct((3, width, part), bf16),
+            jax.ShapeDtypeStruct((1, part, width), bf16),
+            jax.ShapeDtypeStruct((2, part), f32),
+        ),
+        in_specs=whole(10),
+        out_specs=(vmem, vmem, hbm, hbm, vmem),
+        scratch_shapes=Scatter.scratch(n, seqs, rows, width)
+        + GroupSum.scratch(dp, 3, width, part)
+        + GroupSum.scratch(dp, 1, part, width)
+        + SmallSum.scratch(dp, n, 2, width, True)
+        + SmallSum.scratch(dp, n, 2, part, False),
         compiler_params=pltpu.CompilerParams(
-            collective_id=2, has_side_effects=True, vmem_limit_bytes=40 * 2**20
+            collective_id=2, has_side_effects=True, vmem_limit_bytes=62 * 2**20
         ),
         name="heads_scatter",
-    )(query, key, value, weight)
+    )(query, key, value, weight, gathered, out_part, tokens, gain, hidden_grad, bias_part)
 
 
 def normal_cdf(values):
@@ -572,10 +861,6 @@
     return 0.5 + 0.5 * (x * top / low)
 
 
-NT = (((1,), (1,)), ((), ()))
-TN = (((0,), (0,)), ((), ()))
-
-
 def mlp_kernel(
     n,
     normed,
@@ -583,11 +868,17 @@
     up_weight,
     up_bias,
     down_weight,
+    hidden,
+    gain,
     mlp_part,
-    norm_grad,
+    hidden_grad,
+    grad_low,
+    sums,
     up_grad,
     up_bias_grad,
     down_grad,
+    up_box,
+    down_box,
     buf,
     send,
     recv,
@@ -597,13 +888,14 @@
     seqs, rows, width = normed.shape
     units_wide = up_weight.shape[1]
     line = Scatter(at, rows, *scratch[:7])
-    act, pre, out_stage, out_sem, up_stage, up_sem, down_stage, down_sem = scratch[7:]
+    act, pre, out_stage, out_sem, up_stage, down_stage, tile_sem, half_send, half_recv = scratch[7:]
     ring = Gather(at, rows, buf, send, recv)
-    at.greet()
+    at.greet(groups=True)
     for s in range(seqs):
         buf[s, rows_of(at.me, rows)] = normed[s]
-        ring.start(s)
+    ring.start(0)
     up_bias_grad[...] = jnp.zeros_like(up_bias_grad)
+    sums[...] = jnp.zeros_like(sums)
     ft = min(512, units_wide)
 
     def out_copy(s, o):
@@ -642,51 +934,62 @@
         out_copy(s, o).start()
 
     def final(s, there, total):
-        norm_grad[s, there] = total
-
-    down_tiles = down_grad.shape[0] // down_stage.shape[1]
-    up_tiles = up_grad.shape[0] // up_stage.shape[1]
-    flat = seqs * rows * n
-
-    def down_copy(t):
-        size = down_stage.shape[1]
-        return pltpu.make_async_copy(
-            down_stage.at[t % 2], down_grad.at[pl.ds(t * size, size)], down_sem.at[t % 2]
+        back, terms = norm_rows_back(hidden[s, there], total, gain[...])
+        first = pl.multiple_of(at.me * rows + there.start, 16)
+        grad_out = grad_all[s, pl.ds(first, there.size)].astype(f32)
+        grad = grad_out + back
+        hidden_grad[s, there] = grad
+        grad_low[s, there] = grad.astype(bf16)
+        add_row(sums, 0, terms)
+        add_row(sums, 1, total)
+        add_row(sums, 2, grad)
+        add_row(sums, 3, grad_out)
+
+    kinds = ((down_stage, down_grad, down_box, 0), (up_stage, up_grad, up_box, 1))
+
+    def tile_copy(kind, t):
+        stage, grad, box, turn = kinds[kind]
+        return pltpu.make_async_copy(stage, grad.at[t], tile_sem.at[kind])
+
+    def tile_half(kind, t):
+        stage, grad, box, turn = kinds[kind]
+        half = box.shape[1]
+        which = (t + turn) % at.group_bits
+        peer, mine = at.group_peer(which)
+        return pltpu.make_async_remote_copy(
+            src_ref=grad.at[t, rows_of(1 - mine, half)],
+            dst_ref=box.at[t],
+            send_sem=half_send.at[kind, t],
+            recv_sem=half_recv.at[kind, t],
+            device_id={"dp": peer},
+            device_id_type=MESH,
         )
 
-    def up_copy(t):
-        size = up_stage.shape[1]
-        return pltpu.make_async_copy(
-            up_stage.at[t % 2], up_grad.at[pl.ds(t * size, size)], up_sem.at[t % 2]
-        )
+    def tile_sent(kind, t):
+        tile_copy(kind, t).wait()
+        tile_half(kind, t).start()
+
+    order = [(i % 2, i // 2) for i in range(8)]
 
     def weight_tile(i):
-        for t in range(down_tiles):
-            @pl.when(i == t)
+        for j, (kind, t) in enumerate(order):
+            @pl.when(i == j)
             def _():
-                size = down_stage.shape[1]
-                if t >= 2:
-                    down_copy(t - 2).wait()
+                stage = kinds[kind][0]
+                cols = pl.ds(t * stage.shape[0], stage.shape[0])
                 total = 0.0
                 for s in range(seqs):
-                    total += lax.dot_general(
-                        act[s, :, pl.ds(t * size, size)], grad_all[s], TN, preferred_element_type=f32
-                    )
-                down_stage[t % 2] = total.astype(bf16)
-                down_copy(t).start()
-        for t in range(up_tiles):
-            @pl.when(i == t + down_tiles)
-            def _():
-                size = up_stage.shape[1]
-                if t >= 2:
-                    up_copy(t - 2).wait()
-                total = 0.0
-                for s in range(seqs):
-                    total += lax.dot_general(
-                        buf[s, :, pl.ds(t * size, size)], pre[s], TN, preferred_element_type=f32
-                    )
-                up_stage[t % 2] = total.astype(bf16)
-                up_copy(t).start()
+                    if kind == 0:
+                        left, right = act[s, :, cols], grad_all[s]
+                    else:
+                        left, right = buf[s, :, cols], pre[s]
+                    total += lax.dot_general(left, right, TN, preferred_element_type=f32)
+                if j >= 1:
+                    tile_sent(*order[j - 1])
+                stage[...] = total.astype(bf16)
+                tile_copy(kind, t).start()
+
+        pl.when(i == 8)(lambda: tile_sent(*order[7]))
 
     lag = ring.units() // seqs + 2
 
@@ -698,35 +1001,37 @@
         weight_tile(u - ring.units() - 1)
         return carry
 
-    count = max(line.units() + lag, ring.units() + 1 + down_tiles + up_tiles)
+    count = max(line.units() + lag, ring.units() + 2 + len(order))
     lax.fori_loop(0, count, step, 0)
     ring.finish()
     line.finish()
-    for t in range(max(down_tiles - 2, 0), down_tiles):
-        down_copy(t).wait()
-    for t in range(max(up_tiles - 2, 0), up_tiles):
-        up_copy(t).wait()
+    for kind, t in order:
+        tile_half(kind, t).wait()
     out_copy(0, 0).wait()
 
 
-def mlp_block(n, normed, grad_all, up_weight, up_bias, down_weight):
+def mlp_block(n, normed, grad_all, up_weight, up_bias, down_weight, hidden, gain):
     seqs, rows, width = normed.shape
     slots = n * rows
     units = up_weight.shape[1]
     hbm = pl.BlockSpec(memory_space=pl.ANY)
     vmem = pl.BlockSpec(memory_space=VMEM)
-    down_size, up_size = min(256, units), 512
+    down_size, up_size = units // 4, width // 4
     return pl.pallas_call(
         functools.partial(mlp_kernel, n),
         out_shape=(
             jax.ShapeDtypeStruct((seqs, slots, width), bf16),
             jax.ShapeDtypeStruct((seqs, rows, width), f32),
-            jax.ShapeDtypeStruct((width, units), bf16),
+            jax.ShapeDtypeStruct((seqs, rows, width), bf16),
+            jax.ShapeDtypeStruct((4, width), f32),
+            jax.ShapeDtypeStruct((4, up_size, units), bf16),
             jax.ShapeDtypeStruct((1, units), f32),
-            jax.ShapeDtypeStruct((units, width), bf16),
+            jax.ShapeDtypeStruct((4, down_size, width), bf16),
+            jax.ShapeDtypeStruct((4, up_size // 2, units), bf16),
+            jax.ShapeDtypeStruct((4, down_size // 2, width), bf16),
         ),
-        in_specs=whole(5),
-        out_specs=(hbm, vmem, hbm, vmem, hbm),
+        in_specs=whole(7),
+        out_specs=(hbm, vmem, vmem, vmem, hbm, vmem, hbm, hbm, hbm),
         scratch_shapes=[VMEM((seqs, slots, width), bf16)]
         + Gather.scratch(n, seqs)
         + Scatter.scratch(n, seqs, rows, width)
@@ -735,16 +1040,17 @@
             VMEM((seqs, slots, units), bf16),
             VMEM((2 * rows, width), bf16),
             DMA((1,)),
-            VMEM((2, up_size, units), bf16),
+            VMEM((up_size, units), bf16),
+            VMEM((down_size, width), bf16),
             DMA((2,)),
-            VMEM((2, down_size, width), bf16),
-            DMA((2,)),
+            DMA((2, 4)),
+            DMA((2, 4)),
         ],
         compiler_params=pltpu.CompilerParams(
-            collective_id=3, has_side_effects=True, vmem_limit_bytes=60 * 2**20
+            collective_id=3, has_side_effects=True, vmem_limit_bytes=62 * 2**20
         ),
         name="mlp_block",
-    )(normed, grad_all, up_weight, up_bias, down_weight)
+    )(normed, grad_all, up_weight, up_bias, down_weight, hidden, gain)
 
 
 def attn_grad_kernel(
@@ -755,9 +1061,19 @@
     bias,
     weight,
     mixed,
+    sums,
+    up_bias_part,
+    up_part,
+    down_part,
+    up_box,
+    down_box,
     output,
     grad_heads,
     weight_grad,
+    sums_all,
+    up_bias_grad,
+    up_grad,
+    down_grad,
     buf,
     send,
     recv,
@@ -766,8 +1082,34 @@
     at = Place(n)
     seqs, rows, width = grad.shape
     line = Scatter(at, rows, *scratch[:7])
-    load_sem = scratch[7]
+    load_sem, tile_sem, box_sem = scratch[7:10]
     ring = Gather(at, rows, buf, send, recv)
+    up_sum = GroupSum(at, up_part.shape[1], *scratch[10:15], up_grad, turn=1, skip=1)
+    down_sum = GroupSum(at, down_part.shape[1], *scratch[15:20], down_grad, skip=1)
+    small = SmallSum(at, *scratch[20:24], True)
+    small_bias = SmallSum(at, *scratch[24:28], False)
+    pairs = ((up_sum, up_part, up_box), (down_sum, down_part, down_box))
+
+    def tile_load(i, t):
+        group, part, box = pairs[i]
+        half = box.shape[1]
+        return (
+            pltpu.make_async_copy(
+                part.at[t, group.span(group.base(t, 1), half)], group.tiles.at[t], tile_sem.at[i, t]
+            ),
+            pltpu.make_async_copy(box.at[t], group.box(t, 0), box_sem.at[i, t]),
+        )
+
+    def tile_loaded(i, t):
+        for copy in tile_load(i, t):
+            copy.wait()
+
+    for t in range(4):
+        for i in range(2):
+            for copy in tile_load(i, t):
+                copy.start()
+    small.rows[0] = sums[...]
+    small_bias.rows[0] = up_bias_part[...]
 
     def load(s, o):
         return pltpu.make_async_copy(
@@ -780,10 +1122,10 @@
         return carry
 
     lax.fori_loop(0, line.units(), load_unit, 0)
-    at.greet()
+    at.greet(groups=True, cube=True)
     for s in range(seqs):
         buf[s, rows_of(at.me, rows)] = grad[s]
-        ring.start(s)
+    ring.start(0)
 
     def final(s, there, total):
         output[s, there] = (hidden[s, there] + total + bias[...]).astype(bf16)
@@ -808,9 +1150,19 @@
                 buf[s, here], weight[...], NT, preferred_element_type=f32
             ).astype(bf16)
 
+        for i in range(2):
+            group = pairs[i][0]
+            pl.when(u < group.events())(
+                functools.partial(group.event, u, functools.partial(tile_loaded, i))
+            )
+        small.event(u)
+        small_bias.event(u)
         return carry
 
-    lax.fori_loop(0, max(line.units(), ring.units()) + 1, step, 0)
+    count = max(line.units() + 1, ring.units() + 1, up_sum.events(), down_sum.events())
+    lax.fori_loop(0, count, step, 0)
+    sums_all[...] = small.rows[small.phases]
+    up_bias_grad[...] = small_bias.rows[small_bias.phases]
     for j in range(width // 512):
         cols = pl.ds(j * 512, 512)
         total = 0.0
@@ -819,31 +1171,73 @@
         weight_grad[:, cols] = total.astype(bf16)
     ring.finish()
     line.finish()
-
-
-def attn_grad(n, grad, mlp_part, hidden, bias, weight, mixed):
+    small.finish()
+    small_bias.finish()
+    up_sum.finish()
+    down_sum.finish()
+
+
+def attn_grad(
+    n,
+    grad,
+    mlp_part,
+    hidden,
+    bias,
+    weight,
+    mixed,
+    sums,
+    up_bias_part,
+    up_part,
+    down_part,
+    up_box,
+    down_box,
+):
     seqs, rows, width = grad.shape
     slots = n * rows
     part = weight.shape[0]
+    units = up_part.shape[2]
+    dp = lax.axis_size("dp")
     vmem = pl.BlockSpec(memory_space=VMEM)
+    hbm = pl.BlockSpec(memory_space=pl.ANY)
     return pl.pallas_call(
         functools.partial(attn_grad_kernel, n),
         out_shape=(
             jax.ShapeDtypeStruct((seqs, rows, width), bf16),
             jax.ShapeDtypeStruct((seqs, slots, part), bf16),
             jax.ShapeDtypeStruct((part, width), bf16),
+            jax.ShapeDtypeStruct(sums.shape, f32),
+            jax.ShapeDtypeStruct((1, units), f32),
+            jax.ShapeDtypeStruct(up_part.shape, bf16),
+            jax.ShapeDtypeStruct(down_part.shape, bf16),
         ),
-        in_specs=[vmem, pl.BlockSpec(memory_space=pl.ANY), vmem, vmem, vmem, vmem],
-        out_specs=tuple(whole(3)),
+        in_specs=[vmem, hbm] + [vmem] * 6 + [hbm] * 4,
+        out_specs=(vmem,) * 5 + (hbm, hbm),
         scratch_shapes=[VMEM((seqs, slots, width), bf16)]
         + Gather.scratch(n, seqs)
         + Scatter.scratch(n, seqs, rows, width)
-        + [DMA((seqs, n // 2))],
+        + [DMA((seqs, n // 2)), DMA((2, 4)), DMA((2, 4))]
+        + GroupSum.scratch(dp, 4, width // 4, units, 1)
+        + GroupSum.scratch(dp, 4, units // 4, width, 1)
+        + SmallSum.scratch(dp, n, sums.shape[0], width, True)
+        + SmallSum.scratch(dp, n, 1, units, False),
         compiler_params=pltpu.CompilerParams(
-            collective_id=4, has_side_effects=True, vmem_limit_bytes=48 * 2**20
+            collective_id=4, has_side_effects=True, vmem_limit_bytes=62 * 2**20
         ),
         name="attn_grad",
-    )(grad, mlp_part, hidden, bias, weight, mixed)
+    )(
+        grad,
+        mlp_part,
+        hidden,
+        bias,
+        weight,
+        mixed,
+        sums,
+        up_bias_part,
+        up_part,
+        down_part,
+        up_box,
+        down_box,
+    )
 
 
 def body(
@@ -867,7 +1261,6 @@
     part_width = qkv_weight.shape[2]
     head_count = part_width // HD
     score_scale = HD ** (-0.5)
-    inputs = tokens.astype(jnp.float32)
     n = lax.axis_size("tensor")
     gathered_one, heads = gather_project(
         n, tokens, ln1_gain[None], ln1_shift[None], qkv_weight, qkv_bias
@@ -888,26 +1281,40 @@
     )
     valid_rows = (slot_ids < lengths[:, None]).astype(jnp.float32)
     grad_out = cotangent.astype(jnp.float32) * valid_rows[:, :, None]
-    down_bias_grad = jnp.sum(grad_out, axis=(0, 1))
-    grad_mlp = lax.all_gather(grad_out.astype(jnp.bfloat16), "tensor", axis=1, tiled=True)
-    mlp_part, norm_two_grad, up_weight_grad, up_bias_grad, down_weight_grad = mlp_block(
-        n, normed_two, grad_mlp, up_weight, up_bias[None], down_weight
+    grad_low, heads = lax.optimization_barrier((grad_out.astype(jnp.bfloat16), heads))
+    grad_mlp = lax.all_gather(grad_low, "tensor", axis=1, tiled=True)
+    (
+        mlp_part,
+        hidden_grad,
+        grad_attn,
+        sums,
+        up_part,
+        up_bias_part,
+        down_part,
+        up_box,
+        down_box,
+    ) = mlp_block(
+        n, normed_two, grad_mlp, up_weight, up_bias[None], down_weight, hidden_state, ln2_gain[None]
     )
-    up_bias_grad = up_bias_grad[0]
-    up_weight_grad, down_weight_grad = sum_groups((up_weight_grad, down_weight_grad))
-    unused_two, norm_two_back = jax.vjp(layer_norm, hidden_state, ln2_gain, ln2_shift)
-    hidden_ln_grad, ln2_gain_grad, ln2_shift_grad = norm_two_back(norm_two_grad)
-    hidden_grad = grad_out + hidden_ln_grad
-    out_bias_grad = jnp.sum(hidden_grad, axis=(0, 1))
-    output, grad_heads, out_weight_grad = attn_grad(
+    output, grad_heads, out_part, sums, up_bias_grad, up_weight_grad, down_weight_grad = attn_grad(
         n,
-        hidden_grad.astype(jnp.bfloat16),
+        grad_attn,
         mlp_part,
         hidden_state,
         down_bias[None],
         out_weight,
         mixed_heads,
+        sums,
+        up_bias_part,
+        up_part,
+        down_part,
+        up_box,
+        down_box,
     )
+    ln2_gain_grad, ln2_shift_grad, out_bias_grad, down_bias_grad = [sums[i] for i in range(4)]
+    up_bias_grad = up_bias_grad[0]
+    up_weight_grad = up_weight_grad.astype(jnp.float32).reshape(up_weight.shape)
+    down_weight_grad = down_weight_grad.astype(jnp.float32).reshape(down_weight.shape)
     grad_heads = grad_heads.reshape(head_shape)
     grad_query, grad_key, grad_value = lax.map(
         lambda item: attend_backward(item[0], item[1], item[2], item[3], item[4], item[5]),
@@ -917,41 +1324,28 @@
     grad_query = grad_query.reshape(flat_shape).astype(jnp.bfloat16)
     grad_key = grad_key.reshape(flat_shape).astype(jnp.bfloat16)
     grad_value = grad_value.reshape(flat_shape).astype(jnp.bfloat16)
-    qkv_weight_grad = jnp.stack(
-        [
-            score_scale * rows_product(gathered_one, grad_query),
-            rows_product(gathered_one, grad_key),
-            rows_product(gathered_one, grad_value),
-        ]
-    )
-    qkv_weight_grad, out_weight_grad, up_weight_grad, down_weight_grad = lax.optimization_barrier(
-        (qkv_weight_grad, out_weight_grad, up_weight_grad, down_weight_grad)
-    )
-    qkv_weight_grad, out_weight_grad = sum_groups((qkv_weight_grad, out_weight_grad))
     qkv_bias_grad = jnp.stack(
         [
             score_scale * jnp.sum(grad_query.astype(jnp.float32), axis=(0, 1)),
             jnp.sum(grad_value.astype(jnp.float32), axis=(0, 1)),
         ]
     )
-    norm_one_grad = heads_scatter(n, grad_query, grad_key, grad_value, qkv_weight)
-    unused_one, norm_one_back = jax.vjp(layer_norm, inputs, ln1_gain, ln1_shift)
-    input_ln_grad, ln1_gain_grad, ln1_shift_grad = norm_one_back(norm_one_grad)
-    input_grad = hidden_grad + input_ln_grad
-    qkv_bias_grad, up_bias_grad = lax.psum((qkv_bias_grad, up_bias_grad), "dp")
-    ln1_gain_grad, ln1_shift_grad, out_bias_grad, ln2_gain_grad, ln2_shift_grad, down_bias_grad = (
-        lax.psum(
-            (
-                ln1_gain_grad,
-                ln1_shift_grad,
-                out_bias_grad,
-                ln2_gain_grad,
-                ln2_shift_grad,
-                down_bias_grad,
-            ),
-            ("dp", "tensor"),
-        )
+    input_grad, sums_one, qkv_weight_grad, out_weight_grad, qkv_bias_grad = heads_scatter(
+        n,
+        grad_query,
+        grad_key,
+        grad_value,
+        qkv_weight,
+        gathered_one,
+        out_part,
+        tokens,
+        ln1_gain[None],
+        hidden_grad,
+        qkv_bias_grad,
     )
+    ln1_gain_grad, ln1_shift_grad = sums_one[0], sums_one[1]
+    qkv_weight_grad = qkv_weight_grad.astype(jnp.float32)
+    out_weight_grad = out_weight_grad[0].astype(jnp.float32)
     return (
         output,
         input_grad,

time: 1020 us -> 888 us (0.87)
  waiting for transfers between devices: 121 us -> 0.02 us
  Pallas kernels: 672 us -> 729 us
  blocking collectives: 50.6 us -> 0 us
  other arithmetic: 49.3 us -> 37.7 us
    psum x2 -> x0, waiting for transfers between devices: 121 us -> none  [sum_groups(): return [total.astype(jnp.float32) for total in lax.psum(parts, 'dp')]]
    pallas_call x1, Pallas kernels: 95.4 us -> 169 us  [heads_scatter(): pl.pallas_call(functools.partial(heads_scatter_kernel, n), out_shape=(jax...]
    pallas_call x1, Pallas kernels: 145 us -> 79.7 us  [gather_project(): pl.pallas_call(functools.partial(gather_project_kernel, n), out_shape=(ja...]
    psum x2 -> x0, blocking collectives: 50.6 us -> none  [the longest x1 40 us: body(): lax.psum((ln1_gain_grad, ln1_shift_grad, out_bias_grad, ln2_gain_grad, ln...]
    pallas_call x1, Pallas kernels: 152 us -> 182 us  [attn_grad(): pl.pallas_call(functools.partial(attn_grad_kernel, n), out_shape=(jax.Sha...]
    pallas_call x1, Pallas kernels: 92.2 us -> 118 us  [project_scatter(): pl.pallas_call(functools.partial(project_scatter_kernel, n), out_shape=(j...]
    dot_general x3 -> x0, matrix products: 13.1 us -> none  [rows_product(): lax.dot_general(left_flat, right_flat, (((0,), (0,)), ((), ())), preferre...]
    convert_element_type x5 -> x2, other arithmetic: 17.8 us -> 6.84 us  [the longest x1 5.28 us: body(): qkv_weight_grad = qkv_weight_grad.astype(jnp.float32)]
  transfers between devices with their start and end apart: 3 -> 1, of which waited for: 1 -> 0; matrix products, arithmetic and copies ran while one was open for 10% -> 5% of each run, Pallas kernels for 33% -> 13%
where the time goes in v4:
time: 888 us; the launch traced here: 880 us
  Pallas kernels  729 us (82%)
  matrix products  49.2 us (6%)
  local copies, waits for them, and re-layouts  48.3 us (5%)
  other arithmetic  37.7 us (4%)
  between operations  14.7 us (2%)
    pallas_call x1, Pallas kernels, attn_grad(): pl.pallas_call(functools.partial(attn_grad_kernel, n), out_shape=(jax.Sha...  182 us
    pallas_call x1, Pallas kernels, mlp_block(): pl.pallas_call(functools.partial(mlp_kernel, n), out_shape=(jax.ShapeDtyp...  181 us
    pallas_call x1, Pallas kernels, heads_scatter(): pl.pallas_call(functools.partial(heads_scatter_kernel, n), out_shape=(jax...  169 us
    pallas_call x1, Pallas kernels, project_scatter(): pl.pallas_call(functools.partial(project_scatter_kernel, n), out_shape=(j...  118 us
    pallas_call x1, Pallas kernels, gather_project(): pl.pallas_call(functools.partial(gather_project_kernel, n), out_shape=(ja...  79.7 us
  transfers between devices with their start and end apart: 1, of which 0 were waited for; matrix products, arithmetic and copies ran while one was open for 5% of the time, Pallas kernels for 13%

profile of v4, /device:TPU:0, one launch (start us, length us, event | category | flops | bytes accessed | tf_op | source)
XLA Modules:
  0.0 879.9 jit_solution(7414875714007336307)
XLA Ops:
  8.0 2.5 multiply_convert_fusion.2
  10.4 1.9 copy-done
  12.3 1.2 copy-done.2
  15.6 79.7 %gather_project.1 = (bf16[2,1024,2048]{2,1,0:T(8,128)(2,1)}, bf16[3,2,1024,256]{3,2,1,0:T(8,128)(2,1)S(1)}) custom-call(bf16[2,128,2048]{2,1,0:T(8,128)(2,1)S(1)} %copy-done.2, f32[1,2048]{1,0:T(1,128)S(1)} %bitcast.223, f32[1,2048]{1,0:T(1,128)S(1)} %bitcast.224, bf16[3,2048,256]{2,1,0:T(8,128)(2,1)S(1)} %copy-done, f32[2,256]{1,0:T(2,128)S(1)} %copy-done.12), custom_call_target="tpu_custom_call" | custom-call | tf_op jit(solution)/shard_map/gather_project/pallas_call | solution.py:657
  95.4 1.7 fusion.73
  97.1 1.5 reshape_squeeze.10
  98.6 1.1 copy.36
  100.2 1.1 reshape_squeeze.9
  101.3 1.1 broadcast.129.clone
  102.4 34.6 %while.26 = (s32[]{:T(128)}, bf16[2,1024,2,128]{1,3,2,0:T(8,128)(2,1)}, f32[2,2,1024,1]{2,1,3,0:T(2,128)S(1)}, bf16[2,1024,2,128]{3,2,1,0:T(2,128)(2,1)}, s32[2]...) while((s32[]{:T(128)}, ...), condition=%wide.region_5.6_spmd, body=%wide.region_0.5_spmd.sunk | while | flops 1093666304 | bytes 92357400 | solution.py:1271
  104.2 1.9 select_reduce_fusion.4
  106.1 2.1 select_reduce_fusion.5
  108.2 2.2 exponential_reduce_fusion.3
  110.5 1.2 constant_dynamic-slice_fusion.7
  111.7 2.0 copy.85
  113.7 3.8 fusion.109
  117.6 1.3 fusion.108
  121.6 1.9 select_reduce_fusion.4
  123.4 2.1 select_reduce_fusion.5
  125.5 2.2 exponential_reduce_fusion.3
  127.8 1.2 constant_dynamic-slice_fusion.7
  129.0 2.0 copy.85
  131.0 3.8 fusion.109
  134.9 1.3 fusion.108
  137.0 1.0 copy-done.17
  138.0 1.5 copy.52.mixed
  139.6 1.6 copy-done.5
  141.1 118.1 %project_scatter.1 = (f32[2,128,2048]{2,1,0:T(8,128)S(1)}, bf16[2,128,2048]{2,1,0:T(8,128)(2,1)S(1)}) custom-call(bf16[2,1024,256]{2,1,0:T(8,128)(2,1)S(1)} %copy.52.mixed, bf16[256,2048]{1,0:T(8,128)(2,1)S(1)} %copy-done.5, bf16[2,128,2048]{2,1,0:T(8,128)(2,1)S(1)} %copy-done.3, f32[1,2048]{1,0:T(1,128)S(1)} %bitcast.225, f32[1,2048]{1,0:T(1,128)S(1)} %bitcast.221, ...), custom_call_target="tpu_custom_call" | custom-call | tf_op jit(solution)/shard_map/project_scatter/pallas_call | solution.py:709
  259.2 1.3 copy-done.4
  260.6 1.0 copy-done.6
  261.5 180.6 %mlp_block.1 = (bf16[2,1024,2048]{2,1,0:T(8,128)(2,1)}, f32[2,128,2048]{2,1,0:T(8,128)}, bf16[2,128,2048]{2,1,0:T(8,128)(2,1)}, f32[4,2048]{1,0:T(4,128)}, bf16[...) custom-call(bf16[2,128,2048]{2,1,0:T(8,128)(2,1)} %copy-done.6, ...), custom_call_target="tpu_custom_call" | custom-call | tf_op jit(solution)/shard_map/mlp_block/pallas_call | solution.py:1020
  442.2 182.2 %attn_grad.1 = (bf16[2,128,2048]{2,1,0:T(8,128)(2,1)}, bf16[2,1024,256]{2,1,0:T(8,128)(2,1)}, bf16[256,2048]{1,0:T(8,128)(2,1)}, f32[4,2048]{1,0:T(4,128)}, f32[...) custom-call(bf16[2,128,2048]{2,1,0:T(8,128)(2,1)} %get-tuple-element.137.grad, ...), custom_call_target="tpu_custom_call" | custom-call | tf_op jit(solution)/shard_map/attn_grad/pallas_call | solution.py:1202
  624.4 2.3 reshape.253
  626.8 1.1 broadcast.129
  627.9 1.1 broadcast.129.clone.1
  629.0 1.1 broadcast.129.clone.2
  630.1 44.5 %while.27 = (s32[]{:T(128)}, bf16[2,1024,2,128]{1,3,2,0:T(8,128)(2,1)}, bf16[2,1024,2,128]{1,3,2,0:T(8,128)(2,1)}, bf16[2,1024,2,128]{1,3,2,0:T(8,128)(2,1)}, bf...) while((s32[]{:T(128)}, ...), condition=%wide.region_9.10_spmd, body=%wide.region_6.9_spmd.sunk | while | flops 2713189888 | bytes 107562752 | solution.py:1319
  630.1 2.7 fusion.124
  632.8 1.4 constant_dynamic-slice_fusion.9
  636.4 3.7 multiply_reduce_fusion.5
  640.8 1.5 multiply_reduce_fusion.4
  643.0 2.3 multiply_convert_fusion.4
  645.8 1.3 fusion.127
  648.9 1.3 fusion.128
  650.2 2.1 fusion.129
  652.3 2.7 fusion.124
  655.0 1.4 constant_dynamic-slice_fusion.9
  658.6 3.7 multiply_reduce_fusion.5
  663.1 1.5 multiply_reduce_fusion.4
  665.3 2.3 multiply_convert_fusion.4
  668.0 1.3 fusion.127
  671.1 1.3 fusion.128
  672.4 2.1 fusion.129
  674.6 2.0 convert_reduce_fusion
  676.5 2.3 copy.53.query
  678.8 1.3 copy.54.key
  680.1 2.3 copy.55.value
  683.0 168.6 %heads_scatter.1 = (f32[2,128,2048]{2,1,0:T(8,128)}, f32[2,2048]{1,0:T(2,128)}, bf16[3,2048,256]{2,1,0:T(8,128)(2,1)}, bf16[1,256,2048]{2,1,0:T(8,128)(2,1)}, f32[2,256]{1,0:T(2,128)}) custom-call(bf16[2,1024,256]{2,1,0:T(8,128)(2,1)} %copy.53.query, bf16[2,1024,256]{2,1,0:T(8,128)(2,1)} %copy.54.key, bf16[2,1024,256]{2,1,0:T(8,128)(2,1)} %copy.55.value, ...), custom_call_target="tpu_custom_call" | custom-call | tf_op jit(solution)/shard_map/heads_scatter/pallas_call | solution.py:822
  851.6 5.3 convert_element_type.83
  856.9 1.6 bitcast_convert_fusion.2
  859.1 4.7 bitcast_convert_fusion
  863.8 4.7 bitcast_convert_fusion.1
  869.2 1.0 copy.122
  870.2 1.3 copy.123
  (140 shorter events, 23.4 us)
Async XLA Ops:
  7.2 254.4 %all-gather.2.cloned.1.call-start = ((), (), s32[]{:S(2)}) async-start(), calls=%async_computation | async-start | bytes 9437184 | tf_op jit(solution)/shard_map/all_gather | solution.py:1285
  10.4 1.9 copy-start
  12.3 1.2 copy-start.2
  13.6 0.7 copy-start.8
  14.2 0.7 copy-start.9
  14.9 0.7 copy-start.12
  97.1 2.6 copy-start.29
  97.1 3.0 copy-start.28
  99.7 2.7 copy-start.37
  102.4 37.1 %copy-start.3 = (bf16[2,128,2048]{2,1,0:T(8,128)(2,1)S(1)}, bf16[2,128,2048]{2,1,0:T(8,128)(2,1)}, u32[]{:S(2)}) copy-start(bf16[2,128,2048]{2,1,0:T(8,128)(2,1)} %tokens.5) | copy-start | bytes 3145732
  102.4 37.1 %copy-start.7 = (f32[2048]{0:T(1024)S(1)}, f32[2048]{0:T(1024)}, u32[]{:S(2)}) copy-start(f32[2048]{0:T(1024)} %param.28) | copy-start | bytes 24580
  102.4 37.1 %copy-start.10 = (f32[2048]{0:T(1024)S(1)}, f32[2048]{0:T(1024)}, u32[]{:S(2)}) copy-start(f32[2048]{0:T(1024)} %param.27) | copy-start | bytes 24580
  102.4 37.1 %copy-start.11 = (f32[2048]{0:T(1024)S(1)}, f32[2048]{0:T(1024)}, u32[]{:S(2)}) copy-start(f32[2048]{0:T(1024)} %param.29) | copy-start | bytes 24580
  106.1 4.3 copy-start.14
  108.2 2.3 copy-start.16
  108.2 2.3 copy-start.20
  113.7 3.8 copy-start.15
  113.7 3.9 copy-start.22
  123.4 4.3 copy-start.14
  125.5 2.3 copy-start.16
  125.5 2.3 copy-start.20
  131.0 3.8 copy-start.15
  131.0 3.8 copy-start.22
  137.0 1.0 copy-start.17
  139.5 302.7 %copy-start.1 = (bf16[2,1024,256]{2,1,0:T(8,128)(2,1)}, bf16[2,1024,256]{2,1,0:T(8,128)(2,1)S(1)}, u32[]{:S(2)}) copy-start(bf16[2,1024,256]{2,1,0:T(8,128)(2,1)S(1)} %copy.52.mixed) | copy-start | bytes 3145732
  139.5 1.6 copy-start.5
  259.2 1.3 copy-start.4
  260.6 1.0 copy-start.6
  624.4 5.7 copy-start.18
  624.4 5.7 copy-start.19
  624.4 5.6 copy-start.21
  640.8 2.2 copy-start.13
  645.8 3.0 copy-start.23
  648.9 1.3 copy-start.24
  663.1 2.2 copy-start.13
  668.0 3.0 copy-start.23
  671.1 1.3 copy-start.24
  674.6 4.3 copy-start.27
  851.6 5.3 copy-start.31
  851.6 6.9 copy-start.34
  851.6 7.5 copy-start.26
  859.1 4.8 copy-start.25
  863.8 4.7 copy-start.33
  863.8 5.4 copy-start.32
  863.8 6.3 copy-start.30
  868.5 2.9 copy-start.36
  868.5 3.5 copy-start.35
Sparse Core Ops, SparseCore 0:
  95.5 102.2 all-gather.1

commit v5 on v4

--- a/solution.py
+++ b/solution.py
@@ -1,4 +1,5 @@
 import functools
+import heapq
 
 import jax
 import jax.numpy as jnp
@@ -122,6 +123,168 @@
 bf16 = jnp.bfloat16
 NT = (((1,), (1,)), ((), ()))
 TN = (((0,), (0,)), ((), ()))
+
+
+def order_of(chips, ops_of, backlog=8.0, hop=1.5):
+    todo = [sorted(ops_of(c)) for c in range(chips)]
+    order = [[] for _ in range(chips)]
+    free, busy, have, queue = {}, [False] * chips, set(), []
+
+    def push(time, what):
+        heapq.heappush(queue, (time, len(pushed), what))
+        pushed.append(0)
+
+    pushed = []
+    for c in range(chips):
+        push(0.0, (c, None, ()))
+    now = 0.0
+    while queue:
+        now, _, (c, signal, after) = heapq.heappop(queue)
+        if signal is not None:
+            have.add(signal)
+        for part in after:
+            if part[0] == "free":
+                busy[c] = False
+            elif part[0] == "send":
+                _, link, to, sig, span = part
+                start = max(now, free.get((c, link), 0.0))
+                free[c, link] = start + span
+                push(start + span + hop, (to, sig, ()))
+            else:
+                push(now + part[1], (c, part[2], ()))
+        if busy[c]:
+            continue
+        for op in todo[c]:
+            rank, code, needs, time, sends, gives = op
+            if any(need not in have for need in needs):
+                continue
+            late = max([free.get((c, send[0]), 0.0) - now for send in sends], default=0.0)
+            if late > backlog:
+                push(now + late - backlog, (c, None, ()))
+                continue
+            todo[c].remove(op)
+            order[c].append(code)
+            busy[c] = True
+            ends = [("free",)] + [("send",) + send for send in sends]
+            push(now + time, (c, None, ends + [("give",) + give for give in gives]))
+            break
+    assert not any(todo)
+    return order, now
+
+
+PIECE = 12.0
+
+
+def gather_ops(c, chips, seqs, kind, name, rank=0, time=0.5):
+    ops = []
+    for s in range(seqs):
+        for o in range(chips):
+            sends = []
+            if o <= c < chips - 1:
+                sends.append((c + 1, c + 1, (name, c + 1, s, o), PIECE))
+            if o >= c > 0:
+                sends.append((c - 1, c - 1, (name, c - 1, s, o), PIECE))
+            needs = [] if o == c else [(name, c, s, o)]
+            both = [(3.0, (name, c, s, o, "both"))]
+            ops.append(((rank, s, abs(o - c)), (kind, s, o), needs, time, sends, both))
+    return ops
+
+
+def scatter_ops(c, chips, seqs, kind, name, part, rank=1, time=1.3, last=2.0):
+    ops = []
+    for s in range(seqs):
+        for o in range(chips):
+            needs = [(part, c, s, o)]
+            if o >= c > 0:
+                needs.append((name, c, s, o, "below"))
+            if o <= c < chips - 1:
+                needs.append((name, c, s, o, "above"))
+            sends = []
+            if o > c:
+                sends = [(c + 1, c + 1, (name, c + 1, s, o, "below"), PIECE)]
+            if o < c:
+                sends = [(c - 1, c - 1, (name, c - 1, s, o, "above"), PIECE)]
+            order = (rank, s, -abs(o - c)) if o != c else (8, s, 0)
+            ops.append((order, (kind, s, o), needs, last if o == c else time, sends, []))
+    return ops
+
+
+def work_ops(c, chips, seqs, kind, needs_of, gives, time, rank=2, far=False):
+    return [
+        (
+            (rank, s, -abs(o - c) if far else abs(o - c)),
+            (kind, s, o),
+            needs_of(s, o),
+            time,
+            [],
+            [(3.0, (gives, c, s, o))],
+        )
+        for s in range(seqs)
+        for o in range(chips)
+    ]
+
+
+def group_ops(c, bits, count, span, code_of, skip, turn, first_time, rank=3, name="group"):
+    ops = []
+    for t in range(count):
+        for stage in range(skip, 2 * bits + 1):
+            needs = []
+            if stage > skip:
+                needs = [(name, c, t, stage)]
+            sends = []
+            if stage < 2 * bits:
+                i = stage if stage < bits else 2 * bits - 1 - stage
+                axis = "axis%d" % ((t + turn + i) % bits)
+                sends = [(axis, c, (name, c, t, stage + 1), span / 2**i)]
+            time = first_time if stage == 0 else 0.7
+            code = code_of((stage - skip) * count + t)
+            ops.append(((rank, stage, t), code, needs, time, sends, []))
+    return ops
+
+
+class Plan:
+    def __init__(self, at, seqs, ops_of):
+        chips = at.chips
+        order, self.length = order_of(chips, ops_of)
+        self.per, self.chips, self.seqs = 128, chips, seqs
+        self.count = max(len(codes) for codes in order)
+        assert 8 * seqs * chips <= self.per
+        rows = []
+        for codes in order:
+            flat = [(kind * seqs + s) * chips + o for kind, s, o in codes]
+            flat += [7 * seqs * chips] * (self.count - len(flat) + 4)
+            rows.append(
+                [sum(flat[i + j] * self.per**j for j in range(4)) for i in range(0, self.count, 4)]
+            )
+        self.words = []
+        for w in range(len(rows[0])):
+            word = jnp.int32(rows[0][w])
+            for c in range(1, chips):
+                word = jnp.where(at.chip == c, jnp.int32(rows[c][w]), word)
+            self.words.append(word)
+
+    def step(self, k):
+        which, slot = k // 4, lax.rem(k, 4)
+        word = jnp.int32(0)
+        for w, value in enumerate(self.words):
+            word = jnp.where(which == w, value, word)
+        code = word
+        for j in range(1, 4):
+            code = jnp.where(slot == j, word // self.per**j, code)
+        code = lax.rem(code, self.per)
+        each = self.seqs * self.chips
+        return code // each, lax.rem(code, each) // self.chips, lax.rem(code, self.chips)
+
+    def run(self, actions, beside=None):
+        def step(k, carry):
+            kind, s, o = self.step(k)
+            for which, action in actions.items():
+                pl.when(kind == which)(functools.partial(action, s, o))
+            if beside is not None:
+                beside(k)
+            return carry
+
+        lax.fori_loop(0, self.count, step, 0)
 
 
 class Place:
@@ -210,35 +373,12 @@
             device_id_type=MESH,
         ).wait_recv()
 
-    def start(self, s):
+    def relay(self, s, o):
         at = self.at
-        pl.when(at.above)(lambda: self.copy(s, at.chip, UP).start())
-        pl.when(at.below)(lambda: self.copy(s, at.chip, DOWN).start())
-        self.copy(s, at.chip, SIDE).start()
-
-    def units(self):
-        return self.seqs * (1 + 2 * (self.at.chips - 1))
-
-    def unit(self, u):
-        at = self.at
-        per = 1 + 2 * (at.chips - 1)
-        s, v = u // per, lax.rem(u, per)
-        d = (v + 1) // 2
-        o = at.chip + (2 * lax.rem(v, 2) - 1) * d
-        return s, o, (o >= 0) & (o < at.chips) & (u >= 0) & (u < self.units()), v == 0
-
-    def forward(self, u):
-        at = self.at
-        s, o, there, own = self.unit(u)
-
-        pl.when(there & own & (s > 0))(lambda: self.start(s))
-
-        @pl.when(there & jnp.logical_not(own))
-        def _():
-            self.arrived(s, o, at.core)
-            pl.when((o < at.chip) & at.above)(lambda: self.copy(s, o, UP).start())
-            pl.when((o > at.chip) & at.below)(lambda: self.copy(s, o, DOWN).start())
-            self.copy(s, o, SIDE).start()
+        pl.when(o != at.chip)(lambda: self.arrived(s, o, at.core))
+        pl.when((o <= at.chip) & at.above)(lambda: self.copy(s, o, UP).start())
+        pl.when((o >= at.chip) & at.below)(lambda: self.copy(s, o, DOWN).start())
+        self.copy(s, o, SIDE).start()
 
     def finish(self):
         at = self.at
@@ -273,21 +413,6 @@
             DMA((seqs, chips + 1)),
         ]
 
-    def units(self):
-        return self.seqs * (2 * self.at.chips - 1)
-
-    def unit(self, u):
-        at = self.at
-        per = 2 * (at.chips - 1)
-        v = lax.rem(u, per)
-        last = u >= self.seqs * per
-        s = jnp.where(last, u - self.seqs * per, u // per)
-        up = lax.rem(v, 2) == 0
-        away = jnp.where(up, at.chips - 1 - v // 2, v // 2)
-        o = jnp.where(last, at.chip, away)
-        there = last | jnp.where(up, away > at.chip, away < at.chip)
-        return s, o, there & (u >= 0) & (u < self.units())
-
     def side_copy(self, s, o):
         at = self.at
         return pltpu.make_async_remote_copy(
@@ -329,59 +454,55 @@
 
         self.blocks(body)
 
-    def pass_on(self, u, final):
+    def pass_on(self, final, s, o):
         at = self.at
-        s, o, there = self.unit(u)
-
-        @pl.when(there)
+        self.side_copy(s, o).wait_recv()
+
+        @pl.when(o > at.chip)
         def _():
-            self.side_copy(s, o).wait_recv()
-
-            @pl.when(o > at.chip)
+            @pl.when(at.below)
             def _():
-                @pl.when(at.below)
+                self.link_copy(s, o, o, at.me).wait_recv()
+                self.add_up(s, o, [o])
+
+            pl.when(jnp.logical_not(at.below))(lambda: self.add_up(s, o, []))
+            self.link_copy(s, o, o, at.me + 2).start()
+
+        @pl.when(o < at.chip)
+        def _():
+            @pl.when(at.above)
+            def _():
+                self.link_copy(s, o, o, at.me).wait_recv()
+                self.add_up(s, o, [o])
+
+            pl.when(jnp.logical_not(at.above))(lambda: self.add_up(s, o, []))
+            slot = jnp.where(o == at.chip - 1, at.chips, o)
+            self.link_copy(s, o, slot, at.me - 2).start()
+
+        @pl.when(o == at.chip)
+        def _():
+            pl.when(at.below)(lambda: self.link_copy(s, o, o, at.me).wait_recv())
+            pl.when(at.above)(lambda: self.link_copy(s, o, at.chips, at.me).wait_recv())
+            for slot, used in ((o, at.below), (at.chips, at.above)):
+                @pl.when(jnp.logical_not(used))
                 def _():
-                    self.link_copy(s, o, o, at.me).wait_recv()
-                    self.add_up(s, o, [o])
-
-                pl.when(jnp.logical_not(at.below))(lambda: self.add_up(s, o, []))
-                self.link_copy(s, o, o, at.me + 2).start()
-
-            @pl.when(o < at.chip)
-            def _():
-                @pl.when(at.above)
-                def _():
-                    self.link_copy(s, o, o, at.me).wait_recv()
-                    self.add_up(s, o, [o])
-
-                pl.when(jnp.logical_not(at.above))(lambda: self.add_up(s, o, []))
-                slot = jnp.where(o == at.chip - 1, at.chips, o)
-                self.link_copy(s, o, slot, at.me - 2).start()
-
-            @pl.when(o == at.chip)
-            def _():
-                pl.when(at.below)(lambda: self.link_copy(s, o, o, at.me).wait_recv())
-                pl.when(at.above)(lambda: self.link_copy(s, o, at.chips, at.me).wait_recv())
-                for slot, used in ((o, at.below), (at.chips, at.above)):
-                    @pl.when(jnp.logical_not(used))
-                    def _():
-                        def clear(first, step):
-                            self.link[s, slot, pl.ds(first, step)] = jnp.zeros(
-                                (step, self.link.shape[-1]), bf16
-                            )
-
-                        self.blocks(clear)
-                base = at.core * self.rows
-
-                def body(first, step):
-                    here = pl.ds(pl.multiple_of(base + first, step), step)
-                    there = pl.ds(first, step)
-                    total = self.part[s, o, here].astype(f32) + self.side[s, o, there].astype(f32)
-                    total += self.link[s, o, there].astype(f32)
-                    total += self.link[s, at.chips, there].astype(f32)
-                    final(s, there, total)
-
-                self.blocks(body)
+                    def clear(first, step):
+                        self.link[s, slot, pl.ds(first, step)] = jnp.zeros(
+                            (step, self.link.shape[-1]), bf16
+                        )
+
+                    self.blocks(clear)
+            base = at.core * self.rows
+
+            def body(first, step):
+                here = pl.ds(pl.multiple_of(base + first, step), step)
+                there = pl.ds(first, step)
+                total = self.part[s, o, here].astype(f32) + self.side[s, o, there].astype(f32)
+                total += self.link[s, o, there].astype(f32)
+                total += self.link[s, at.chips, there].astype(f32)
+                final(s, there, total)
+
+            self.blocks(body)
 
     def finish(self):
         at = self.at
@@ -611,33 +732,29 @@
             return carry
 
         lax.fori_loop(0, rows // 16, block, 0)
-        if s == 0:
-            ring.start(s)
 
     def keep(s, o):
         here = rows_of(o, 2 * rows)
         return pltpu.make_async_copy(buf.at[s, here], gathered.at[s, here], out_sem.at[s, o])
 
-    def step(u, carry):
-        ring.forward(u)
-        s, o, there, own = ring.unit(u - 2)
-
-        @pl.when(there)
-        def _():
-            ring.arrived(s, o, 1 - at.core)
-            keep(s, o).start()
-            here = rows_of(o, 2 * rows)
-            for j in range(3):
-                total = jnp.dot(buf[s, here], weight[j], preferred_element_type=f32)
-                if j == 0:
-                    total = (total + bias[0:1]) * HD ** (-0.5)
-                if j == 2:
-                    total = total + bias[1:2]
-                heads[j, s, here] = total.astype(bf16)
-
-        return carry
-
-    lax.fori_loop(0, ring.units() + 2, step, 0)
+    def work(s, o):
+        ring.arrived(s, o, 1 - at.core)
+        keep(s, o).start()
+        here = rows_of(o, 2 * rows)
+        for j in range(3):
+            total = jnp.dot(buf[s, here], weight[j], preferred_element_type=f32)
+            if j == 0:
+                total = (total + bias[0:1]) * HD ** (-0.5)
+            if j == 2:
+                total = total + bias[1:2]
+            heads[j, s, here] = total.astype(bf16)
+
+    def ops_of(c):
+        return gather_ops(c, at.chips, seqs, 0, "in") + work_ops(
+            c, at.chips, seqs, 1, lambda s, o: [("in", c, s, o, "both")], "done", 1.0
+        )
+
+    Plan(at, seqs, ops_of).run({0: ring.relay, 1: work})
     ring.finish()
 
     def close(i, carry):
@@ -685,22 +802,20 @@
         hidden[s, there] = values
         normed[s, there] = norm_rows(values, gain[...], shift[...]).astype(bf16)
 
-    def step(u, carry):
-        s, o, there = line.unit(u)
-
-        @pl.when(there)
-        def _():
-            here = rows_of(o, 2 * rows)
-            for j in range(width // 512):
-                cols = pl.ds(j * 512, 512)
-                total = jnp.dot(mixed[s, here], weight[:, cols], preferred_element_type=f32)
-                line.part[s, o, :, cols] = total.astype(bf16)
-            line.share(s, o)
-
-        line.pass_on(u - 2, final)
-        return carry
-
-    lax.fori_loop(0, line.units() + 2, step, 0)
+    def work(s, o):
+        here = rows_of(o, 2 * rows)
+        for j in range(width // 512):
+            cols = pl.ds(j * 512, 512)
+            total = jnp.dot(mixed[s, here], weight[:, cols], preferred_element_type=f32)
+            line.part[s, o, :, cols] = total.astype(bf16)
+        line.share(s, o)
+
+    def ops_of(c):
+        return work_ops(
+            c, at.chips, seqs, 0, lambda s, o: [], "part", 1.0, rank=0, far=True
+        ) + scatter_ops(c, at.chips, seqs, 1, "out", "part", last=4.0)
+
+    Plan(at, seqs, ops_of).run({0: work, 1: functools.partial(line.pass_on, final)})
     line.finish()
 
 
@@ -773,32 +888,49 @@
                 )
             weight_sum.tiles[j, pl.ds(first, 512)] = (parts[j][1] * total).astype(bf16)
 
-    def step(u, carry):
-        s, o, there = line.unit(u)
-
-        @pl.when(there)
-        def _():
-            here = rows_of(o, 2 * rows)
-            for j in range(width // 512):
-                cols = pl.ds(j * 512, 512)
-                total = 0.0
-                for i in range(3):
-                    total += parts[i][1] * lax.dot_general(
-                        parts[i][0][s, here], weight[i, cols], NT, preferred_element_type=f32
-                    )
-                line.part[s, o, :, cols] = total.astype(bf16)
-            line.share(s, o)
-
-        line.pass_on(u - 2, final)
+    def work(s, o):
+        here = rows_of(o, 2 * rows)
+        for j in range(width // 512):
+            cols = pl.ds(j * 512, 512)
+            total = 0.0
+            for i in range(3):
+                total += parts[i][1] * lax.dot_general(
+                    parts[i][0][s, here], weight[i, cols], NT, preferred_element_type=f32
+                )
+            line.part[s, o, :, cols] = total.astype(bf16)
+        line.share(s, o)
+
+    each = seqs * at.chips
+
+    def weight_event(first, s, o):
+        e = first + s * at.chips + o
         for j in range(3):
-            pl.when(u == j)(functools.partial(weight_tile, j))
-        pl.when(u < weight_sum.events())(lambda: weight_sum.event(u))
-        pl.when(lax.rem(u, 3) == 0)(lambda: out_sum.event(u // 3))
-        small_bias.event(u)
-        return carry
-
-    count = max(line.units() + 2, weight_sum.events(), 3 * out_sum.events())
-    lax.fori_loop(0, count, step, 0)
+            pl.when(e == j)(functools.partial(weight_tile, j))
+        weight_sum.event(e)
+
+    def out_event(s, o):
+        out_sum.event(s * at.chips + o)
+
+    def code_of(kind, e):
+        return (kind + e // each, e % each // at.chips, e % at.chips)
+
+    def ops_of(c):
+        chips = at.chips
+        return (
+            work_ops(c, chips, seqs, 0, lambda s, o: [], "part", 1.5, rank=0, far=True)
+            + scatter_ops(c, chips, seqs, 1, "out", "part", last=4.0)
+            + group_ops(
+                c, at.group_bits, 3, PIECE, lambda e: code_of(2, e), 0, 0, 2.7, name="qkv"
+            )
+            + group_ops(
+                c, at.group_bits, 1, PIECE, lambda e: code_of(5, e), 0, 1, 0.7, name="out_sum"
+            )
+        )
+
+    actions = {0: work, 1: functools.partial(line.pass_on, final), 5: out_event}
+    for i in range(3):
+        actions[2 + i] = functools.partial(weight_event, i * each)
+    Plan(at, seqs, ops_of).run(actions, small_bias.event)
     for e in range(small.phases + 1):
         small.event(e)
     sums_all[...] = small.rows[small.phases]
@@ -893,7 +1025,6 @@
     at.greet(groups=True)
     for s in range(seqs):
         buf[s, rows_of(at.me, rows)] = normed[s]
-    ring.start(0)
     up_bias_grad[...] = jnp.zeros_like(up_bias_grad)
     sums[...] = jnp.zeros_like(sums)
     ft = min(512, units_wide)
@@ -903,7 +1034,7 @@
             out_stage, mlp_part.at[s, rows_of(o, 2 * rows)], out_sem.at[0]
         )
 
-    def work(s, o, first):
+    def work(s, o):
         ring.arrived(s, o, 1 - at.core)
         here = rows_of(o, 2 * rows)
         for j in range(units_wide // ft):
@@ -925,7 +1056,7 @@
                 pre[s, here], up_weight[cols], NT, preferred_element_type=f32
             ).astype(bf16)
         line.share(s, o)
-        pl.when(jnp.logical_not(first))(lambda: out_copy(s, o).wait())
+        pl.when((s > 0) | (o != at.chip))(lambda: out_copy(s, o).wait())
         for j in range(width // 512):
             cols = pl.ds(j * 512, 512)
             out_stage[:, cols] = jnp.dot(
@@ -989,20 +1120,37 @@
                 stage[...] = total.astype(bf16)
                 tile_copy(kind, t).start()
 
-        pl.when(i == 8)(lambda: tile_sent(*order[7]))
-
-    lag = ring.units() // seqs + 2
-
-    def step(u, carry):
-        ring.forward(u)
-        line.pass_on(u - lag, final)
-        s, o, there, own = ring.unit(u - 1)
-        pl.when(there)(lambda: work(s, o, u == 1))
-        weight_tile(u - ring.units() - 1)
-        return carry
-
-    count = max(line.units() + lag, ring.units() + 2 + len(order))
-    lax.fori_loop(0, count, step, 0)
+    def tile_work(s, o):
+        weight_tile(s * at.chips + o)
+
+    def ops_of(c):
+        chips = at.chips
+        units = [(s, o) for s in range(seqs) for o in range(chips)]
+        ops = (
+            gather_ops(c, chips, seqs, 0, "in")
+            + scatter_ops(c, chips, seqs, 1, "back", "part", last=4.0)
+            + work_ops(
+                c, chips, seqs, 2, lambda s, o: [("in", c, s, o, "both")], "part", 5.7
+            )
+        )
+        for i in range(len(ops)):
+            rank, code, needs, time, sends, gives = ops[i]
+            if code[0] == 2 and code[1:] != (0, c):
+                ops[i] = (rank, code, needs + [("first", c)], time, sends, gives)
+            if code == (2, 0, c):
+                ops[i] = (rank, code, needs, time, sends, gives + [(0.0, ("first", c))])
+        for e in range(len(order)):
+            needs = [("part", c, s, o) for s, o in units]
+            needs += [("tile", c, e - 1)] if e else []
+            sends = [("axis%d" % (e % 2), c, ("half", c, e), PIECE)]
+            code = (3, e // chips, e % chips)
+            ops.append(((4, e, 0), code, needs, 2.7, sends, [(0.0, ("tile", c, e))]))
+        return ops
+
+    Plan(at, seqs, ops_of).run(
+        {0: ring.relay, 1: functools.partial(line.pass_on, final), 2: work, 3: tile_work}
+    )
+    tile_sent(*order[7])
     ring.finish()
     line.finish()
     for kind, t in order:
@@ -1116,51 +1264,56 @@
             mlp_part.at[s, rows_of(o, 2 * rows)], line.part.at[s, o], load_sem.at[s, o]
         )
 
-    def load_unit(u, carry):
-        s, o, there = line.unit(u)
-        pl.when(there)(lambda: load(s, o).start())
+    def load_one(i, carry):
+        load(i // at.chips, lax.rem(i, at.chips)).start()
         return carry
 
-    lax.fori_loop(0, line.units(), load_unit, 0)
-    at.greet(groups=True, cube=True)
+    each = seqs * at.chips
+    lax.fori_loop(0, each, load_one, 0)
     for s in range(seqs):
         buf[s, rows_of(at.me, rows)] = grad[s]
-    ring.start(0)
+    at.greet(groups=True, cube=True)
 
     def final(s, there, total):
         output[s, there] = (hidden[s, there] + total + bias[...]).astype(bf16)
 
-    def step(u, carry):
-        ring.forward(u)
-        s, o, there = line.unit(u)
-
-        @pl.when(there)
-        def _():
-            load(s, o).wait()
-            line.share(s, o)
-
-        line.pass_on(u - 1, final)
-        s, o, there, own = ring.unit(u - 1)
-
-        @pl.when(there)
-        def _():
-            ring.arrived(s, o, 1 - at.core)
-            here = rows_of(o, 2 * rows)
-            grad_heads[s, here] = lax.dot_general(
-                buf[s, here], weight[...], NT, preferred_element_type=f32
-            ).astype(bf16)
-
-        for i in range(2):
-            group = pairs[i][0]
-            pl.when(u < group.events())(
-                functools.partial(group.event, u, functools.partial(tile_loaded, i))
-            )
-        small.event(u)
-        small_bias.event(u)
-        return carry
-
-    count = max(line.units() + 1, ring.units() + 1, up_sum.events(), down_sum.events())
-    lax.fori_loop(0, count, step, 0)
+    def share(s, o):
+        load(s, o).wait()
+        line.share(s, o)
+
+    def work(s, o):
+        ring.arrived(s, o, 1 - at.core)
+        here = rows_of(o, 2 * rows)
+        grad_heads[s, here] = lax.dot_general(
+            buf[s, here], weight[...], NT, preferred_element_type=f32
+        ).astype(bf16)
+
+    def event(i, s, o):
+        e = s * at.chips + o
+        for j in range(2):
+            group = pairs[j][0]
+            group.event(e + i * each, functools.partial(tile_loaded, j))
+
+    def ops_of(c):
+        chips = at.chips
+        code_of = lambda e: (4 + e // each, e % each // chips, e % chips)
+        return (
+            gather_ops(c, chips, seqs, 0, "in")
+            + scatter_ops(c, chips, seqs, 1, "out", "part", last=4.0)
+            + work_ops(c, chips, seqs, 2, lambda s, o: [("in", c, s, o, "both")], "done", 1.0)
+            + work_ops(c, chips, seqs, 3, lambda s, o: [], "part", 0.3, rank=0, far=True)
+            + group_ops(c, at.group_bits, 4, PIECE, code_of, 1, 0, 0.7)
+        )
+
+    actions = {0: ring.relay, 1: functools.partial(line.pass_on, final), 2: work, 3: share}
+    for i in range(3):
+        actions[4 + i] = functools.partial(event, i)
+
+    def beside(k):
+        pl.when(lax.rem(k, 3) == 0)(lambda: small.event(k // 3))
+        small_bias.event(k)
+
+    Plan(at, seqs, ops_of).run(actions, beside)
     sums_all[...] = small.rows[small.phases]
     up_bias_grad[...] = small_bias.rows[small_bias.phases]
     for j in range(width // 512):

time: 888 us -> 746 us (0.84)
  Pallas kernels: 729 us -> 575 us
    pallas_call x1, Pallas kernels: 169 us -> 107 us  [heads_scatter(): pl.pallas_call(functools.partial(heads_scatter_kernel, n), out_shape=(jax...]
    pallas_call x1, Pallas kernels: 182 us -> 136 us  [attn_grad(): pl.pallas_call(functools.partial(attn_grad_kernel, n), out_shape=(jax.Sha...]
    pallas_call x1, Pallas kernels: 181 us -> 147 us  [mlp_block(): pl.pallas_call(functools.partial(mlp_kernel, n), out_shape=(jax.ShapeDtyp...]
    pallas_call x1, Pallas kernels: 118 us -> 108 us  [project_scatter(): pl.pallas_call(functools.partial(project_scatter_kernel, n), out_shape=(j...]
  transfers between devices with their start and end apart: 1 -> 1, of which waited for: 0 -> 0; matrix products, arithmetic and copies ran while one was open for 5% -> 6% of each run, Pallas kernels for 13% -> 15%
where the time goes in v5:
time: 746 us; the launch traced here: 735 us
  Pallas kernels  575 us (77%)
  matrix products  49.1 us (7%)
  local copies, waits for them, and re-layouts  48.4 us (6%)
  other arithmetic  37.7 us (5%)
  between operations  14.5 us (2%)
  loops' own time  9.35 us (1%)
    pallas_call x1, Pallas kernels, mlp_block(): pl.pallas_call(functools.partial(mlp_kernel, n), out_shape=(jax.ShapeDtyp...  147 us
    pallas_call x1, Pallas kernels, attn_grad(): pl.pallas_call(functools.partial(attn_grad_kernel, n), out_shape=(jax.Sha...  136 us
    pallas_call x1, Pallas kernels, project_scatter(): pl.pallas_call(functools.partial(project_scatter_kernel, n), out_shape=(j...  108 us
    pallas_call x1, Pallas kernels, heads_scatter(): pl.pallas_call(functools.partial(heads_scatter_kernel, n), out_shape=(jax...  107 us
    pallas_call x1, Pallas kernels, gather_project(): pl.pallas_call(functools.partial(gather_project_kernel, n), out_shape=(ja...  77.9 us
  transfers between devices with their start and end apart: 1, of which 0 were waited for; matrix products, arithmetic and copies ran while one was open for 6% of the time, Pallas kernels for 15%

profile of v5, /device:TPU:0, one launch (start us, length us, event | category | flops | bytes accessed | tf_op | source)
XLA Modules:
  0.0 734.6 jit_solution(8268043573516730539)
XLA Ops:
  8.0 2.5 multiply_convert_fusion.2
  10.4 1.9 copy-done
  12.3 1.2 copy-done.2
  15.6 77.9 %gather_project.1 = (bf16[2,1024,2048]{2,1,0:T(8,128)(2,1)}, bf16[3,2,1024,256]{3,2,1,0:T(8,128)(2,1)S(1)}) custom-call(bf16[2,128,2048]{2,1,0:T(8,128)(2,1)S(1)} %copy-done.2, f32[1,2048]{1,0:T(1,128)S(1)} %bitcast.223, f32[1,2048]{1,0:T(1,128)S(1)} %bitcast.224, bf16[3,2048,256]{2,1,0:T(8,128)(2,1)S(1)} %copy-done, f32[2,256]{1,0:T(2,128)S(1)} %copy-done.12), custom_call_target="tpu_custom_call" | custom-call | tf_op jit(solution)/shard_map/gather_project/pallas_call | solution.py:774
  93.5 1.7 fusion.73
  95.3 1.5 reshape_squeeze.10
  96.8 1.1 copy.36
  98.3 1.1 reshape_squeeze.9
  99.4 1.1 broadcast.129.clone
  100.5 34.6 %while.26 = (s32[]{:T(128)}, bf16[2,1024,2,128]{1,3,2,0:T(8,128)(2,1)}, f32[2,2,1024,1]{2,1,3,0:T(2,128)S(1)}, bf16[2,1024,2,128]{3,2,1,0:T(2,128)(2,1)}, s32[2]...) while((s32[]{:T(128)}, ...), condition=%wide.region_5.6_spmd, body=%wide.region_0.5_spmd.sunk | while | flops 1093666304 | bytes 92357400 | solution.py:1424
  102.4 1.9 select_reduce_fusion.4
  104.3 2.1 select_reduce_fusion.5
  106.4 2.2 exponential_reduce_fusion.3
  108.7 1.2 constant_dynamic-slice_fusion.7
  109.9 2.0 copy.85
  111.9 3.7 fusion.109
  115.7 1.3 fusion.108
  119.7 1.9 select_reduce_fusion.4
  121.6 2.1 select_reduce_fusion.5
  123.7 2.2 exponential_reduce_fusion.3
  126.0 1.2 constant_dynamic-slice_fusion.7
  127.1 2.0 copy.85
  129.2 3.7 fusion.109
  133.0 1.3 fusion.108
  135.1 1.0 copy-done.17
  136.1 1.5 copy.52.mixed
  137.7 1.6 copy-done.5
  139.2 108.4 %project_scatter.1 = (f32[2,128,2048]{2,1,0:T(8,128)S(1)}, bf16[2,128,2048]{2,1,0:T(8,128)(2,1)S(1)}) custom-call(bf16[2,1024,256]{2,1,0:T(8,128)(2,1)S(1)} %copy.52.mixed, bf16[256,2048]{1,0:T(8,128)(2,1)S(1)} %copy-done.5, bf16[2,128,2048]{2,1,0:T(8,128)(2,1)S(1)} %copy-done.3, f32[1,2048]{1,0:T(1,128)S(1)} %bitcast.225, f32[1,2048]{1,0:T(1,128)S(1)} %bitcast.221, ...), custom_call_target="tpu_custom_call" | custom-call | tf_op jit(solution)/shard_map/project_scatter/pallas_call | solution.py:824
  247.7 1.3 copy-done.4
  249.0 1.0 copy-done.6
  250.0 146.9 %mlp_block.1 = (bf16[2,1024,2048]{2,1,0:T(8,128)(2,1)}, f32[2,128,2048]{2,1,0:T(8,128)}, bf16[2,128,2048]{2,1,0:T(8,128)(2,1)}, f32[4,2048]{1,0:T(4,128)}, bf16[...) custom-call(bf16[2,128,2048]{2,1,0:T(8,128)(2,1)} %copy-done.6, ...), custom_call_target="tpu_custom_call" | custom-call | tf_op jit(solution)/shard_map/mlp_block/pallas_call | solution.py:1168
  396.9 135.6 %attn_grad.1 = (bf16[2,128,2048]{2,1,0:T(8,128)(2,1)}, bf16[2,1024,256]{2,1,0:T(8,128)(2,1)}, bf16[256,2048]{1,0:T(8,128)(2,1)}, f32[4,2048]{1,0:T(4,128)}, f32[...) custom-call(bf16[2,128,2048]{2,1,0:T(8,128)(2,1)} %get-tuple-element.137.grad, ...), custom_call_target="tpu_custom_call" | custom-call | tf_op jit(solution)/shard_map/attn_grad/pallas_call | solution.py:1355
  532.5 2.3 reshape.253
  534.9 1.1 broadcast.129
  536.0 1.1 broadcast.129.clone.1
  537.1 1.1 broadcast.129.clone.2
  538.2 53.3 %while.27 = (s32[]{:T(128)}, bf16[2,1024,2,128]{1,3,2,0:T(8,128)(2,1)}, bf16[2,1024,2,128]{1,3,2,0:T(8,128)(2,1)}, bf16[2,1024,2,128]{1,3,2,0:T(8,128)(2,1)}, bf...) while((s32[]{:T(128)}, ...), condition=%wide.region_9.10_spmd, body=%wide.region_6.9_spmd.sunk | while | flops 2713189888 | bytes 107562752 | solution.py:1472
  547.0 2.7 fusion.124
  549.7 1.4 constant_dynamic-slice_fusion.9
  553.3 3.7 multiply_reduce_fusion.5
  557.7 1.5 multiply_reduce_fusion.4
  559.9 2.3 multiply_convert_fusion.4
  562.7 1.3 fusion.127
  565.8 1.3 fusion.128
  567.1 2.1 fusion.129
  569.2 2.7 fusion.124
  571.9 1.4 constant_dynamic-slice_fusion.9
  575.5 3.7 multiply_reduce_fusion.5
  580.0 1.5 multiply_reduce_fusion.4
  582.1 2.3 multiply_convert_fusion.4
  584.9 1.3 fusion.127
  588.0 1.3 fusion.128
  589.3 2.1 fusion.129
  591.4 2.0 convert_reduce_fusion
  593.4 2.3 copy.53.query
  595.7 1.3 copy.54.key
  597.0 2.3 copy.55.value
  599.8 106.7 %heads_scatter.1 = (f32[2,128,2048]{2,1,0:T(8,128)}, f32[2,2048]{1,0:T(2,128)}, bf16[3,2048,256]{2,1,0:T(8,128)(2,1)}, bf16[1,256,2048]{2,1,0:T(8,128)(2,1)}, f32[2,256]{1,0:T(2,128)}) custom-call(bf16[2,1024,256]{2,1,0:T(8,128)(2,1)} %copy.53.query, bf16[2,1024,256]{2,1,0:T(8,128)(2,1)} %copy.54.key, bf16[2,1024,256]{2,1,0:T(8,128)(2,1)} %copy.55.value, ...), custom_call_target="tpu_custom_call" | custom-call | tf_op jit(solution)/shard_map/heads_scatter/pallas_call | solution.py:954
  706.5 5.3 convert_element_type.83
  711.8 1.6 bitcast_convert_fusion.2
  714.0 4.7 bitcast_convert_fusion
  718.8 4.7 bitcast_convert_fusion.1
  724.1 1.0 copy.122
  725.1 1.3 copy.123
  (140 shorter events, 23.5 us)
Async XLA Ops:
  7.2 242.8 %all-gather.2.cloned.1.call-start = ((), (), s32[]{:S(2)}) async-start(), calls=%async_computation | async-start | bytes 9437184 | tf_op jit(solution)/shard_map/all_gather | solution.py:1438
  10.4 1.9 copy-start
  12.3 1.2 copy-start.2
  13.6 0.7 copy-start.8
  14.2 0.7 copy-start.9
  14.9 0.7 copy-start.12
  95.3 2.6 copy-start.29
  95.3 3.0 copy-start.28
  97.9 2.7 copy-start.37
  100.5 37.1 %copy-start.3 = (bf16[2,128,2048]{2,1,0:T(8,128)(2,1)S(1)}, bf16[2,128,2048]{2,1,0:T(8,128)(2,1)}, u32[]{:S(2)}) copy-start(bf16[2,128,2048]{2,1,0:T(8,128)(2,1)} %tokens.5) | copy-start | bytes 3145732
  100.5 37.1 %copy-start.7 = (f32[2048]{0:T(1024)S(1)}, f32[2048]{0:T(1024)}, u32[]{:S(2)}) copy-start(f32[2048]{0:T(1024)} %param.28) | copy-start | bytes 24580
  100.5 37.1 %copy-start.10 = (f32[2048]{0:T(1024)S(1)}, f32[2048]{0:T(1024)}, u32[]{:S(2)}) copy-start(f32[2048]{0:T(1024)} %param.27) | copy-start | bytes 24580
  100.5 37.1 %copy-start.11 = (f32[2048]{0:T(1024)S(1)}, f32[2048]{0:T(1024)}, u32[]{:S(2)}) copy-start(f32[2048]{0:T(1024)} %param.29) | copy-start | bytes 24580
  104.3 4.4 copy-start.14
  106.4 2.3 copy-start.16
  106.4 2.3 copy-start.20
  111.9 3.7 copy-start.15
  111.9 3.8 copy-start.22
  121.6 4.3 copy-start.14
  123.6 2.3 copy-start.16
  123.7 2.3 copy-start.20
  129.2 3.7 copy-start.15
  129.2 3.8 copy-start.22
  135.1 1.0 copy-start.17
  137.6 259.3 %copy-start.1 = (bf16[2,1024,256]{2,1,0:T(8,128)(2,1)}, bf16[2,1024,256]{2,1,0:T(8,128)(2,1)S(1)}, u32[]{:S(2)}) copy-start(bf16[2,1024,256]{2,1,0:T(8,128)(2,1)S(1)} %copy.52.mixed) | copy-start | bytes 3145732
  137.6 1.6 copy-start.5
  247.7 1.3 copy-start.4
  249.0 1.0 copy-start.6
  532.5 5.7 copy-start.18
  532.5 5.7 copy-start.19
  532.5 5.6 copy-start.21
  557.7 2.2 copy-start.13
  562.7 3.0 copy-start.23
  565.8 1.3 copy-start.24
  579.9 2.2 copy-start.13
  584.9 3.0 copy-start.23
  588.0 1.3 copy-start.24
  591.4 4.3 copy-start.27
  706.5 5.3 copy-start.31
  706.5 6.9 copy-start.34
  706.5 7.5 %copy-start.26 = (bf16[4,256,2048]{2,1,0:T(8,128)(2,1)S(1)}, bf16[4,256,2048]{2,1,0:T(8,128)(2,1)}, u32[]{:S(2)}) copy-start(bf16[4,256,2048]{2,1,0:T(8,128)(2,1)} %get-tuple-element.162) | copy-start | bytes 12582916
  714.0 4.8 copy-start.25
  718.8 4.7 copy-start.33
  718.8 5.4 copy-start.32
  718.8 6.3 copy-start.30
  723.5 2.9 copy-start.36
  723.5 3.5 copy-start.35
Sparse Core Ops, SparseCore 0:
  93.6 104.1 all-gather.1

commit v6 on v5

--- a/solution.py
+++ b/solution.py
@@ -12,108 +12,6 @@
 
 
 norm_epsilon = 1e-05
-block_rows = 512
-
-
-def layer_norm(values, norm_gain, norm_shift):
-    centre = values - jnp.mean(values, axis=-1, keepdims=True)
-    spread = jnp.mean(centre * centre, axis=-1, keepdims=True)
-    return centre * lax.rsqrt(spread + norm_epsilon) * norm_gain + norm_shift
-
-
-def gelu_exact(values):
-    return jax.nn.gelu(values, approximate=False)
-
-
-def flat_product(left_rows, right_rows):
-    flat = left_rows.reshape(-1, left_rows.shape[-1])
-    result = jnp.dot(flat, right_rows, preferred_element_type=jnp.float32)
-    return result.reshape(left_rows.shape[:-1] + (right_rows.shape[-1],))
-
-
-def product_back(left_rows, right_rows):
-    flat = left_rows.reshape(-1, left_rows.shape[-1])
-    result = lax.dot_general(
-        flat, right_rows, (((1,), (1,)), ((), ())), preferred_element_type=jnp.float32
-    )
-    return result.reshape(left_rows.shape[:-1] + (right_rows.shape[0],))
-
-
-def rows_product(left_rows, right_rows):
-    left_flat = left_rows.reshape(-1, left_rows.shape[-1])
-    right_flat = right_rows.reshape(-1, right_rows.shape[-1])
-    return lax.dot_general(
-        left_flat, right_flat, (((0,), (0,)), ((), ())), preferred_element_type=jnp.float32
-    )
-
-
-def sum_groups(parts):
-    parts = [part.astype(jnp.bfloat16) for part in parts]
-    return [total.astype(jnp.float32) for total in lax.psum(parts, "dp")]
-
-
-def allowed_mask(first_row, row_count, slot_count, length):
-    row_ids = first_row + lax.broadcasted_iota(jnp.int32, (row_count, slot_count), 0)
-    col_ids = lax.broadcasted_iota(jnp.int32, (row_count, slot_count), 1)
-    return (col_ids <= row_ids) & (col_ids < length)
-
-
-def block_scores(query_block, key_rows, first_row, length):
-    scores = jnp.einsum("qhd,khd->hqk", query_block, key_rows, preferred_element_type=jnp.float32)
-    allowed = allowed_mask(first_row, query_block.shape[0], key_rows.shape[0], length)
-    return jnp.where(allowed[None], scores, -1e30)
-
-
-def attend_forward(query_rows, key_rows, value_rows, length):
-    slot_count = query_rows.shape[0]
-    step_rows = min(block_rows, slot_count)
-    outputs = []
-    totals = []
-    for block_index in range(slot_count // step_rows):
-        first_row = block_index * step_rows
-        query_block = query_rows[first_row : first_row + step_rows]
-        scores = block_scores(query_block, key_rows, first_row, length)
-        row_peak = jnp.max(scores, axis=-1, keepdims=True)
-        log_total = row_peak + jnp.log(jnp.sum(jnp.exp(scores - row_peak), axis=-1, keepdims=True))
-        weights = jnp.exp(scores - log_total).astype(jnp.bfloat16)
-        outputs.append(
-            jnp.einsum("hqk,khd->qhd", weights, value_rows, preferred_element_type=jnp.float32)
-        )
-        totals.append(log_total)
-    return (jnp.concatenate(outputs, axis=0), jnp.concatenate(totals, axis=1))
-
-
-def attend_backward(query_rows, key_rows, value_rows, grad_rows, log_totals, length):
-    slot_count = query_rows.shape[0]
-    step_rows = min(block_rows, slot_count)
-    grad_keys = jnp.zeros(key_rows.shape, jnp.float32)
-    grad_values = jnp.zeros(value_rows.shape, jnp.float32)
-    grad_queries = []
-    for block_index in range(slot_count // step_rows):
-        first_row = block_index * step_rows
-        query_block = query_rows[first_row : first_row + step_rows]
-        grad_block = grad_rows[first_row : first_row + step_rows]
-        scores = block_scores(query_block, key_rows, first_row, length)
-        probs = jnp.exp(scores - log_totals[:, first_row : first_row + step_rows])
-        grad_probs = jnp.einsum(
-            "qhd,khd->hqk", grad_block, value_rows, preferred_element_type=jnp.float32
-        )
-        centre = jnp.sum(probs * grad_probs, axis=-1, keepdims=True)
-        grad_scores = (probs * (grad_probs - centre)).astype(jnp.bfloat16)
-        grad_queries.append(
-            jnp.einsum("hqk,khd->qhd", grad_scores, key_rows, preferred_element_type=jnp.float32)
-        )
-        grad_keys = grad_keys + jnp.einsum(
-            "hqk,qhd->khd", grad_scores, query_block, preferred_element_type=jnp.float32
-        )
-        grad_values = grad_values + jnp.einsum(
-            "hqk,qhd->khd",
-            probs.astype(jnp.bfloat16),
-            grad_block,
-            preferred_element_type=jnp.float32,
-        )
-    return (jnp.concatenate(grad_queries, axis=0), grad_keys, grad_values)
-
 
 MESH = pl.DeviceIdType.MESH
 UP, DOWN, SIDE = 0, 1, 2
@@ -175,7 +73,7 @@
 PIECE = 12.0
 
 
-def gather_ops(c, chips, seqs, kind, name, rank=0, time=0.5):
+def gather_ops(c, chips, seqs, kind, name, rank=0, time=0.5, gate=False):
     ops = []
     for s in range(seqs):
         for o in range(chips):
@@ -185,6 +83,10 @@
             if o >= c > 0:
                 sends.append((c - 1, c - 1, (name, c - 1, s, o), PIECE))
             needs = [] if o == c else [(name, c, s, o)]
+            if gate and o == c and s > 0:
+                for other in range(chips):
+                    if other < c < chips - 1 or other > c > 0:
+                        needs.append((name, c, s - 1, other))
             both = [(3.0, (name, c, s, o, "both"))]
             ops.append(((rank, s, abs(o - c)), (kind, s, o), needs, time, sends, both))
     return ops
@@ -717,27 +619,125 @@
     ref[row : row + 1] += jnp.sum(values, axis=0, keepdims=True)
 
 
-def gather_project_kernel(
-    n, tokens, gain, shift, weight, bias, gathered, heads, buf, send, recv, out_sem
+def head_probs(query, keys, first, length):
+    rows, cols = query.shape[0], keys.shape[0]
+    scores = lax.dot_general(query, keys, NT, preferred_element_type=f32)
+    row_ids = first + lax.broadcasted_iota(jnp.int32, (rows, cols), 0)
+    col_ids = lax.broadcasted_iota(jnp.int32, (rows, cols), 1)
+    scores = jnp.where((col_ids <= row_ids) & (col_ids < length), scores, -1e30)
+    probs = jnp.exp(scores - jnp.max(scores, axis=-1, keepdims=True))
+    return probs * (1.0 / jnp.sum(probs, axis=-1, keepdims=True))
+
+
+def attend(heads, lengths, mixed, block, s):
+    slots, part = mixed.shape[1:]
+
+    def one(h, carry):
+        cols = pl.ds(pl.multiple_of(h * HD, HD), HD)
+        for first in range(0, slots, block):
+            rows, seen = pl.ds(first, block), pl.ds(0, first + block)
+            probs = head_probs(heads[0, s, rows, cols], heads[1, s, seen, cols], first, lengths[s])
+            mixed[s, rows, cols] = jnp.dot(
+                probs.astype(bf16), heads[2, s, seen, cols], preferred_element_type=f32
+            ).astype(bf16)
+        return carry
+
+    lax.fori_loop(0, part // HD, one, 0)
+
+
+def attend_back(heads, grad_heads, lengths, grads, grad_key, grad_value, block, s):
+    slots, part = grad_heads.shape[1:]
+
+    def one(h, carry):
+        cols = pl.ds(pl.multiple_of(h * HD, HD), HD)
+        grad_key[...] = jnp.zeros_like(grad_key)
+        grad_value[...] = jnp.zeros_like(grad_value)
+        for first in range(0, slots, block):
+            rows, seen = pl.ds(first, block), pl.ds(0, first + block)
+            query, grad = heads[0, s, rows, cols], grad_heads[s, rows, cols]
+            keys = heads[1, s, seen, cols]
+            probs = head_probs(query, keys, first, lengths[s])
+            grad_value[seen] += lax.dot_general(
+                probs.astype(bf16), grad, TN, preferred_element_type=f32
+            )
+            back = lax.dot_general(
+                grad, heads[2, s, seen, cols], NT, preferred_element_type=f32
+            )
+            centre = jnp.sum(probs * back, axis=-1, keepdims=True)
+            scores = (probs * (back - centre)).astype(bf16)
+            grads[0, s, rows, cols] = jnp.dot(
+                scores, keys, preferred_element_type=f32
+            ).astype(bf16)
+            grad_key[seen] += lax.dot_general(scores, query, TN, preferred_element_type=f32)
+        grads[1, s, :, cols] = grad_key[...].astype(bf16)
+        grads[2, s, :, cols] = grad_value[...].astype(bf16)
+        return carry
+
+    lax.fori_loop(0, part // HD, one, 0)
+
+
+def attention_block_kernel(
+    n,
+    tokens,
+    cotangent,
+    lengths,
+    gain,
+    shift,
+    weight,
+    bias,
+    out_weight,
+    out_bias,
+    gain_two,
+    shift_two,
+    gathered,
+    heads,
+    mixed,
+    hidden,
+    normed,
+    grad_all,
+    buf,
+    send,
+    recv,
+    keep_sem,
+    grad_send,
+    grad_recv,
+    masked,
+    mask_sem,
+    *scratch,
 ):
     at = Place(n)
     seqs, rows, width = tokens.shape
     ring = Gather(at, rows, buf, send, recv)
-    at.greet()
+    grad_ring = Gather(at, rows, grad_all, grad_send, grad_recv)
+    line = Scatter(at, rows, *scratch)
+
+    def mask_copy(s):
+        return pltpu.make_async_copy(
+            masked.at[s], grad_all.at[s, rows_of(at.me, rows)], mask_sem.at[s]
+        )
+
     for s in range(seqs):
         def block(i, carry):
             first = pl.multiple_of(i * 16, 16)
-            values = norm_rows(tokens[s, pl.ds(first, 16)].astype(f32), gain[...], shift[...])
+            here = pl.ds(first, 16)
+            values = norm_rows(tokens[s, here].astype(f32), gain[...], shift[...])
             buf[s, pl.ds(pl.multiple_of(at.me * rows + first, 16), 16)] = values.astype(bf16)
+            slot = at.me * rows + first + lax.broadcasted_iota(jnp.int32, (16, width), 0)
+            grad = jnp.where(slot < lengths[s], cotangent[s, here].astype(f32), 0.0)
+            masked[s, here] = grad.astype(bf16)
             return carry
 
         lax.fori_loop(0, rows // 16, block, 0)
+        mask_copy(s).start()
+    at.greet()
+    for s in range(seqs):
+        mask_copy(s).wait()
 
     def keep(s, o):
         here = rows_of(o, 2 * rows)
-        return pltpu.make_async_copy(buf.at[s, here], gathered.at[s, here], out_sem.at[s, o])
-
-    def work(s, o):
+        return pltpu.make_async_copy(buf.at[s, here], gathered.at[s, here], keep_sem.at[s, o])
+
+    def project(s, o):
         ring.arrived(s, o, 1 - at.core)
         keep(s, o).start()
         here = rows_of(o, 2 * rows)
@@ -749,16 +749,59 @@
                 total = total + bias[1:2]
             heads[j, s, here] = total.astype(bf16)
 
+    def final(s, there, total):
+        values = tokens[s, there].astype(f32) + total + out_bias[...]
+        hidden[s, there] = values
+        normed[s, there] = norm_rows(values, gain_two[...], shift_two[...]).astype(bf16)
+
+    def mix(s, o):
+        attend(heads, lengths, mixed, min(512, n * rows), s)
+
+    def project_out(s, o):
+        here = rows_of(o, 2 * rows)
+        for j in range(width // 512):
+            cols = pl.ds(j * 512, 512)
+            total = jnp.dot(mixed[s, here], out_weight[:, cols], preferred_element_type=f32)
+            line.part[s, o, :, cols] = total.astype(bf16)
+        line.share(s, o)
+
     def ops_of(c):
-        return gather_ops(c, at.chips, seqs, 0, "in") + work_ops(
-            c, at.chips, seqs, 1, lambda s, o: [("in", c, s, o, "both")], "done", 1.0
+        chips = at.chips
+        mixing = []
+        for s in range(seqs):
+            needs = [("heads", c, s, o) for o in range(chips)]
+            mixing.append(((2, s, 0), (2, s, 0), needs, 6.0, [], [(0.0, ("mixed", c, s))]))
+        return (
+            gather_ops(c, chips, seqs, 0, "in", gate=True)
+            + work_ops(
+                c, chips, seqs, 1, lambda s, o: [("in", c, s, o, "both")], "heads", 1.0
+            )
+            + mixing
+            + work_ops(
+                c, chips, seqs, 3, lambda s, o: [("mixed", c, s)], "part", 1.0, far=True
+            )
+            + scatter_ops(c, chips, seqs, 4, "out", "part", last=4.0)
+            + gather_ops(c, chips, seqs, 5, "grad", rank=6)
         )
 
-    Plan(at, seqs, ops_of).run({0: ring.relay, 1: work})
+    Plan(at, seqs, ops_of).run(
+        {
+            0: ring.relay,
+            1: project,
+            2: mix,
+            3: project_out,
+            4: functools.partial(line.pass_on, final),
+            5: grad_ring.relay,
+        }
+    )
     ring.finish()
+    line.finish()
+    grad_ring.finish()
 
     def close(i, carry):
-        keep(i // at.chips, lax.rem(i, at.chips)).wait()
+        s, o = i // at.chips, lax.rem(i, at.chips)
+        grad_ring.arrived(s, o, 1 - at.core)
+        keep(s, o).wait()
         return carry
 
     lax.fori_loop(0, seqs * at.chips, close, 0)
@@ -768,87 +811,71 @@
     return [pl.BlockSpec(memory_space=VMEM)] * count
 
 
-def gather_project(n, tokens, gain, shift, weight, bias):
+def attention_block(
+    n,
+    tokens,
+    cotangent,
+    lengths,
+    gain,
+    shift,
+    weight,
+    bias,
+    out_weight,
+    out_bias,
+    gain_two,
+    shift_two,
+):
     seqs, rows, width = tokens.shape
     part = weight.shape[2]
+    vmem = pl.BlockSpec(memory_space=VMEM)
+    hbm = pl.BlockSpec(memory_space=pl.ANY)
+    smem = pl.BlockSpec(memory_space=pltpu.SMEM)
     return pl.pallas_call(
-        functools.partial(gather_project_kernel, n),
+        functools.partial(attention_block_kernel, n),
         out_shape=(
             jax.ShapeDtypeStruct((seqs, n * rows, width), bf16),
             jax.ShapeDtypeStruct((3, seqs, n * rows, part), bf16),
+            jax.ShapeDtypeStruct((seqs, n * rows, part), bf16),
+            jax.ShapeDtypeStruct((seqs, rows, width), f32),
+            jax.ShapeDtypeStruct((seqs, rows, width), bf16),
+            jax.ShapeDtypeStruct((seqs, n * rows, width), bf16),
         ),
-        in_specs=whole(5),
-        out_specs=(pl.BlockSpec(memory_space=pl.ANY), pl.BlockSpec(memory_space=VMEM)),
+        in_specs=[vmem, vmem, smem] + [vmem] * 8,
+        out_specs=(hbm, vmem, vmem, vmem, vmem, hbm),
         scratch_shapes=[VMEM((seqs, n * rows, width), bf16)]
         + Gather.scratch(n, seqs)
-        + [DMA((seqs, n // 2))],
+        + [DMA((seqs, n // 2))]
+        + Gather.scratch(n, seqs)
+        + [VMEM((seqs, rows, width), bf16), DMA((seqs,))]
+        + Scatter.scratch(n, seqs, rows, width),
         compiler_params=pltpu.CompilerParams(
-            collective_id=0, has_side_effects=True, vmem_limit_bytes=40 * 2**20
+            collective_id=0, has_side_effects=True, vmem_limit_bytes=60 * 2**20
         ),
-        name="gather_project",
-    )(tokens, gain, shift, weight, bias)
-
-
-def project_scatter_kernel(
-    n, mixed, weight, tokens, bias, gain, shift, hidden, normed, *scratch
-):
-    at = Place(n)
-    seqs, rows, width = tokens.shape
-    line = Scatter(at, rows, *scratch)
-    at.greet()
-
-    def final(s, there, total):
-        values = tokens[s, there].astype(f32) + total + bias[...]
-        hidden[s, there] = values
-        normed[s, there] = norm_rows(values, gain[...], shift[...]).astype(bf16)
-
-    def work(s, o):
-        here = rows_of(o, 2 * rows)
-        for j in range(width // 512):
-            cols = pl.ds(j * 512, 512)
-            total = jnp.dot(mixed[s, here], weight[:, cols], preferred_element_type=f32)
-            line.part[s, o, :, cols] = total.astype(bf16)
-        line.share(s, o)
-
-    def ops_of(c):
-        return work_ops(
-            c, at.chips, seqs, 0, lambda s, o: [], "part", 1.0, rank=0, far=True
-        ) + scatter_ops(c, at.chips, seqs, 1, "out", "part", last=4.0)
-
-    Plan(at, seqs, ops_of).run({0: work, 1: functools.partial(line.pass_on, final)})
-    line.finish()
-
-
-def project_scatter(n, mixed, weight, tokens, bias, gain, shift):
-    seqs, rows, width = tokens.shape
-    return pl.pallas_call(
-        functools.partial(project_scatter_kernel, n),
-        out_shape=(
-            jax.ShapeDtypeStruct((seqs, rows, width), f32),
-            jax.ShapeDtypeStruct((seqs, rows, width), bf16),
-        ),
-        in_specs=whole(6),
-        out_specs=tuple(whole(2)),
-        scratch_shapes=Scatter.scratch(n, seqs, rows, width),
-        compiler_params=pltpu.CompilerParams(
-            collective_id=1, has_side_effects=True, vmem_limit_bytes=40 * 2**20
-        ),
-        name="project_scatter",
-    )(mixed, weight, tokens, bias, gain, shift)
+        name="attention_block",
+    )(
+        tokens,
+        cotangent,
+        lengths,
+        gain,
+        shift,
+        weight,
+        bias,
+        out_weight,
+        out_bias,
+        gain_two,
+        shift_two,
+    )
 
 
 def heads_scatter_kernel(
     n,
-    query,
-    key,
-    value,
+    grads,
     weight,
     gathered,
     out_part,
     tokens,
     gain,
     hidden_grad,
-    bias_part,
     grad,
     sums_all,
     weight_grad,
@@ -865,7 +892,11 @@
     small_bias = SmallSum(at, *scratch[21:25], False)
     out_sum.tiles[0] = out_part[...]
     small.rows[0] = jnp.zeros(small.rows.shape[1:], f32)
-    small_bias.rows[0] = bias_part[...]
+    for row, j, scale in ((0, 0, HD ** (-0.5)), (1, 2, 1.0)):
+        total = 0.0
+        for s in range(seqs):
+            total += jnp.sum(grads[j, s].astype(f32), axis=0, keepdims=True)
+        small_bias.rows[0, row : row + 1] = scale * total
     at.greet(groups=True, cube=True)
 
     def final(s, there, total):
@@ -874,7 +905,7 @@
         small.rows[0, 0:1] += jnp.sum(terms, axis=0, keepdims=True)
         small.rows[0, 1:2] += jnp.sum(total, axis=0, keepdims=True)
 
-    parts = ((query, HD ** (-0.5)), (key, 1.0), (value, 1.0))
+    scales = (HD ** (-0.5), 1.0, 1.0)
 
     def weight_tile(j):
         for first in range(0, width, 512):
@@ -882,11 +913,11 @@
             for s in range(seqs):
                 total += lax.dot_general(
                     gathered[s, :, pl.ds(first, 512)],
-                    parts[j][0][s],
+                    grads[j, s],
                     TN,
                     preferred_element_type=f32,
                 )
-            weight_sum.tiles[j, pl.ds(first, 512)] = (parts[j][1] * total).astype(bf16)
+            weight_sum.tiles[j, pl.ds(first, 512)] = (scales[j] * total).astype(bf16)
 
     def work(s, o):
         here = rows_of(o, 2 * rows)
@@ -894,8 +925,8 @@
             cols = pl.ds(j * 512, 512)
             total = 0.0
             for i in range(3):
-                total += parts[i][1] * lax.dot_general(
-                    parts[i][0][s, here], weight[i, cols], NT, preferred_element_type=f32
+                total += scales[i] * lax.dot_general(
+                    grads[i, s, here], weight[i, cols], NT, preferred_element_type=f32
                 )
             line.part[s, o, :, cols] = total.astype(bf16)
         line.share(s, o)
@@ -942,10 +973,8 @@
     small_bias.finish()
 
 
-def heads_scatter(
-    n, query, key, value, weight, gathered, out_part, tokens, gain, hidden_grad, bias_part
-):
-    seqs, slots, part = query.shape
+def heads_scatter(n, grads, weight, gathered, out_part, tokens, gain, hidden_grad):
+    seqs, slots, part = grads.shape[1:]
     width = weight.shape[1]
     rows = slots // n
     dp = lax.axis_size("dp")
@@ -960,7 +989,7 @@
             jax.ShapeDtypeStruct((1, part, width), bf16),
             jax.ShapeDtypeStruct((2, part), f32),
         ),
-        in_specs=whole(10),
+        in_specs=whole(7),
         out_specs=(vmem, vmem, hbm, hbm, vmem),
         scratch_shapes=Scatter.scratch(n, seqs, rows, width)
         + GroupSum.scratch(dp, 3, width, part)
@@ -971,7 +1000,7 @@
             collective_id=2, has_side_effects=True, vmem_limit_bytes=62 * 2**20
         ),
         name="heads_scatter",
-    )(query, key, value, weight, gathered, out_part, tokens, gain, hidden_grad, bias_part)
+    )(grads, weight, gathered, out_part, tokens, gain, hidden_grad)
 
 
 def normal_cdf(values):
@@ -1215,8 +1244,10 @@
     down_part,
     up_box,
     down_box,
+    lengths,
+    heads,
     output,
-    grad_heads,
+    grads,
     weight_grad,
     sums_all,
     up_bias_grad,
@@ -1236,6 +1267,7 @@
     down_sum = GroupSum(at, down_part.shape[1], *scratch[15:20], down_grad, skip=1)
     small = SmallSum(at, *scratch[20:24], True)
     small_bias = SmallSum(at, *scratch[24:28], False)
+    grad_heads, grad_key, grad_value = scratch[28:]
     pairs = ((up_sum, up_part, up_box), (down_sum, down_part, down_box))
 
     def tile_load(i, t):
@@ -1288,6 +1320,10 @@
             buf[s, here], weight[...], NT, preferred_element_type=f32
         ).astype(bf16)
 
+    def back(s, o):
+        block = min(512, n * rows)
+        attend_back(heads, grad_heads, lengths, grads, grad_key, grad_value, block, s)
+
     def event(i, s, o):
         e = s * at.chips + o
         for j in range(2):
@@ -1297,7 +1333,11 @@
     def ops_of(c):
         chips = at.chips
         code_of = lambda e: (4 + e // each, e % each // chips, e % chips)
-        return (
+        backs = []
+        for s in range(seqs):
+            needs = [("done", c, s, o) for o in range(chips)]
+            backs.append(((4, s, 0), (6, s, 0), needs, 8.0, [], []))
+        return backs + (
             gather_ops(c, chips, seqs, 0, "in")
             + scatter_ops(c, chips, seqs, 1, "out", "part", last=4.0)
             + work_ops(c, chips, seqs, 2, lambda s, o: [("in", c, s, o, "both")], "done", 1.0)
@@ -1306,8 +1346,9 @@
         )
 
     actions = {0: ring.relay, 1: functools.partial(line.pass_on, final), 2: work, 3: share}
-    for i in range(3):
+    for i in range(2):
         actions[4 + i] = functools.partial(event, i)
+    actions[6] = back
 
     def beside(k):
         pl.when(lax.rem(k, 3) == 0)(lambda: small.event(k // 3))
@@ -1344,6 +1385,8 @@
     down_part,
     up_box,
     down_box,
+    lengths,
+    heads,
 ):
     seqs, rows, width = grad.shape
     slots = n * rows
@@ -1356,14 +1399,17 @@
         functools.partial(attn_grad_kernel, n),
         out_shape=(
             jax.ShapeDtypeStruct((seqs, rows, width), bf16),
-            jax.ShapeDtypeStruct((seqs, slots, part), bf16),
+            jax.ShapeDtypeStruct(heads.shape, bf16),
             jax.ShapeDtypeStruct((part, width), bf16),
             jax.ShapeDtypeStruct(sums.shape, f32),
             jax.ShapeDtypeStruct((1, units), f32),
             jax.ShapeDtypeStruct(up_part.shape, bf16),
             jax.ShapeDtypeStruct(down_part.shape, bf16),
         ),
-        in_specs=[vmem, hbm] + [vmem] * 6 + [hbm] * 4,
+        in_specs=[vmem, hbm]
+        + [vmem] * 6
+        + [hbm] * 4
+        + [pl.BlockSpec(memory_space=pltpu.SMEM), vmem],
         out_specs=(vmem,) * 5 + (hbm, hbm),
         scratch_shapes=[VMEM((seqs, slots, width), bf16)]
         + Gather.scratch(n, seqs)
@@ -1372,7 +1418,8 @@
         + GroupSum.scratch(dp, 4, width // 4, units, 1)
         + GroupSum.scratch(dp, 4, units // 4, width, 1)
         + SmallSum.scratch(dp, n, sums.shape[0], width, True)
-        + SmallSum.scratch(dp, n, 1, units, False),
+        + SmallSum.scratch(dp, n, 1, units, False)
+        + [VMEM((seqs, slots, part), bf16), VMEM((slots, HD), f32), VMEM((slots, HD), f32)],
         compiler_params=pltpu.CompilerParams(
             collective_id=4, has_side_effects=True, vmem_limit_bytes=62 * 2**20
         ),
@@ -1390,6 +1437,8 @@
         down_part,
         up_box,
         down_box,
+        lengths,
+        heads,
     )
 
 
@@ -1410,32 +1459,21 @@
     down_weight,
     down_bias,
 ):
-    seq_count, local_rows, model_width = tokens.shape
-    part_width = qkv_weight.shape[2]
-    head_count = part_width // HD
-    score_scale = HD ** (-0.5)
     n = lax.axis_size("tensor")
-    gathered_one, heads = gather_project(
-        n, tokens, ln1_gain[None], ln1_shift[None], qkv_weight, qkv_bias
+    gathered_one, heads, mixed_heads, hidden_state, normed_two, grad_mlp = attention_block(
+        n,
+        tokens,
+        cotangent,
+        lengths,
+        ln1_gain[None],
+        ln1_shift[None],
+        qkv_weight,
+        qkv_bias,
+        out_weight,
+        out_bias[None],
+        ln2_gain[None],
+        ln2_shift[None],
     )
-    slot_count = gathered_one.shape[1]
-    head_shape = (seq_count, slot_count, head_count, HD)
-    query_rows, key_rows, value_rows = [heads[j].reshape(head_shape) for j in range(3)]
-    attended, log_totals = lax.map(
-        lambda item: attend_forward(item[0], item[1], item[2], item[3]),
-        (query_rows, key_rows, value_rows, lengths),
-    )
-    mixed_heads = attended.reshape(seq_count, slot_count, part_width).astype(jnp.bfloat16)
-    hidden_state, normed_two = project_scatter(
-        n, mixed_heads, out_weight, tokens, out_bias[None], ln2_gain[None], ln2_shift[None]
-    )
-    slot_ids = lax.axis_index("tensor") * local_rows + lax.broadcasted_iota(
-        jnp.int32, (seq_count, local_rows), 1
-    )
-    valid_rows = (slot_ids < lengths[:, None]).astype(jnp.float32)
-    grad_out = cotangent.astype(jnp.float32) * valid_rows[:, :, None]
-    grad_low, heads = lax.optimization_barrier((grad_out.astype(jnp.bfloat16), heads))
-    grad_mlp = lax.all_gather(grad_low, "tensor", axis=1, tiled=True)
     (
         mlp_part,
         hidden_grad,
@@ -1449,7 +1487,7 @@
     ) = mlp_block(
         n, normed_two, grad_mlp, up_weight, up_bias[None], down_weight, hidden_state, ln2_gain[None]
     )
-    output, grad_heads, out_part, sums, up_bias_grad, up_weight_grad, down_weight_grad = attn_grad(
+    output, grads, out_part, sums, up_bias_grad, up_weight_grad, down_weight_grad = attn_grad(
         n,
         grad_attn,
         mlp_part,
@@ -1463,55 +1501,28 @@
         down_part,
         up_box,
         down_box,
+        lengths,
+        heads,
     )
     ln2_gain_grad, ln2_shift_grad, out_bias_grad, down_bias_grad = [sums[i] for i in range(4)]
-    up_bias_grad = up_bias_grad[0]
+    input_grad, sums_one, qkv_weight_grad, out_weight_grad, qkv_bias_grad = heads_scatter(
+        n, grads, qkv_weight, gathered_one, out_part, tokens, ln1_gain[None], hidden_grad
+    )
     up_weight_grad = up_weight_grad.astype(jnp.float32).reshape(up_weight.shape)
     down_weight_grad = down_weight_grad.astype(jnp.float32).reshape(down_weight.shape)
-    grad_heads = grad_heads.reshape(head_shape)
-    grad_query, grad_key, grad_value = lax.map(
-        lambda item: attend_backward(item[0], item[1], item[2], item[3], item[4], item[5]),
-        (query_rows, key_rows, value_rows, grad_heads, log_totals, lengths),
-    )
-    flat_shape = (seq_count, slot_count, part_width)
-    grad_query = grad_query.reshape(flat_shape).astype(jnp.bfloat16)
-    grad_key = grad_key.reshape(flat_shape).astype(jnp.bfloat16)
-    grad_value = grad_value.reshape(flat_shape).astype(jnp.bfloat16)
-    qkv_bias_grad = jnp.stack(
-        [
-            score_scale * jnp.sum(grad_query.astype(jnp.float32), axis=(0, 1)),
-            jnp.sum(grad_value.astype(jnp.float32), axis=(0, 1)),
-        ]
-    )
-    input_grad, sums_one, qkv_weight_grad, out_weight_grad, qkv_bias_grad = heads_scatter(
-        n,
-        grad_query,
-        grad_key,
-        grad_value,
-        qkv_weight,
-        gathered_one,
-        out_part,
-        tokens,
-        ln1_gain[None],
-        hidden_grad,
-        qkv_bias_grad,
-    )
-    ln1_gain_grad, ln1_shift_grad = sums_one[0], sums_one[1]
-    qkv_weight_grad = qkv_weight_grad.astype(jnp.float32)
-    out_weight_grad = out_weight_grad[0].astype(jnp.float32)
     return (
         output,
         input_grad,
-        ln1_gain_grad,
-        ln1_shift_grad,
-        qkv_weight_grad,
+        sums_one[0],
+        sums_one[1],
+        qkv_weight_grad.astype(jnp.float32),
         qkv_bias_grad,
-        out_weight_grad,
+        out_weight_grad[0].astype(jnp.float32),
         out_bias_grad,
         ln2_gain_grad,
         ln2_shift_grad,
         up_weight_grad,
-        up_bias_grad,
+        up_bias_grad[0],
         down_weight_grad,
         down_bias_grad,
     )

time: 746 us -> 598 us (0.80); the launches traced: 735 us -> 595 us
  matrix products: 49.1 us -> 0 us
  local copies, waits for them, and re-layouts: 48.4 us -> 6.06 us
  other arithmetic: 37.7 us -> 15.8 us
  between operations: 14.5 us -> 0.93 us
  loops' own time: 9.35 us -> 0 us
    dot_general x28 -> x0, matrix products: 49.1 us -> none  [the longest x8 14.8 us: block_scores(): jnp.einsum('qhd,khd->hqk', query_block, key_rows, preferred_element_type=...]
    pallas_call x2 -> x1, Pallas kernels: 186 us -> 176 us  [attention_block(): pl.pallas_call(functools.partial(attention_block_kernel, n), out_shape=(j...]
    unnamed x64 -> x20, local copies, waits for them, and re-layouts: 13.6 us -> 3.94 us
    dynamic_slice x10 -> x0, local copies, waits for them, and re-layouts: 9.44 us -> none  [body(): lax.map(lambda item: attend_forward(item[0], item[1], item[2], item[3]),...]
    another operation x2 -> x0, loops' own time: 9.35 us -> none  [the longest x1 9.1 us: body(): lax.map(lambda item: attend_backward(item[0], item[1], item[2], item[3],...]
    convert_element_type x6 -> x2, other arithmetic: 14.5 us -> 6.28 us  [the longest x1 3.49 us: body(): qkv_weight_grad.astype(jnp.float32)]
  transfers between devices with their start and end apart: 1 -> 0, of which waited for: 0 -> 0; matrix products, arithmetic and copies ran while one was open for 6% -> 0% of each run, Pallas kernels for 15% -> 0%
where the time goes in v6:
time: 598 us; the launch traced here: 595 us
  Pallas kernels  572 us (96%)
  other arithmetic  15.8 us (3%)
  local copies, waits for them, and re-layouts  6.06 us (1%)
    pallas_call x1, Pallas kernels, attention_block(): pl.pallas_call(functools.partial(attention_block_kernel, n), out_shape=(j...  176 us
    pallas_call x1, Pallas kernels, mlp_block(): pl.pallas_call(functools.partial(mlp_kernel, n), out_shape=(jax.ShapeDtyp...  147 us
    pallas_call x1, Pallas kernels, attn_grad(): pl.pallas_call(functools.partial(attn_grad_kernel, n), out_shape=(jax.Sha...  143 us
    pallas_call x1, Pallas kernels, heads_scatter(): pl.pallas_call(functools.partial(heads_scatter_kernel, n), out_shape=(jax...  107 us

profile of v6, /device:TPU:0, one launch (start us, length us, event | category | flops | bytes accessed | tf_op | source)
XLA Modules:
  0.0 594.8 jit_solution(12251371876191672547)
XLA Ops:
  0.6 175.5 %attention_block.1 = (bf16[2,1024,2048]{2,1,0:T(8,128)(2,1)}, bf16[3,2,1024,256]{3,2,1,0:T(8,128)(2,1)}, bf16[2,1024,256]{2,1,0:T(8,128)(2,1)}, f32[2,128,2048]{...) custom-call(bf16[2,128,2048]{2,1,0:T(8,128)(2,1)} %tokens.3, ...), custom_call_target="tpu_custom_call" | custom-call | tf_op jit(solution)/shard_map/attention_block/pallas_call | solution.py:833
  176.2 146.7 %mlp_block.1 = (bf16[2,1024,2048]{2,1,0:T(8,128)(2,1)}, f32[2,128,2048]{2,1,0:T(8,128)}, bf16[2,128,2048]{2,1,0:T(8,128)(2,1)}, f32[4,2048]{1,0:T(4,128)}, bf16[...) custom-call(bf16[2,128,2048]{2,1,0:T(8,128)(2,1)} %get-tuple-element, ...), custom_call_target="tpu_custom_call" | custom-call | tf_op jit(solution)/shard_map/mlp_block/pallas_call | solution.py:1197
  322.8 142.9 %attn_grad.1 = (bf16[2,128,2048]{2,1,0:T(8,128)(2,1)}, bf16[3,2,1024,256]{3,2,1,0:T(8,128)(2,1)}, bf16[256,2048]{1,0:T(8,128)(2,1)}, f32[4,2048]{1,0:T(4,128)}, ...) custom-call(bf16[2,128,2048]{2,1,0:T(8,128)(2,1)} %get-tuple-element.44.grad, ...), custom_call_target="tpu_custom_call" | custom-call | tf_op jit(solution)/shard_map/attn_grad/pallas_call | solution.py:1398
  465.7 0.0 copy-start.5
  465.7 106.9 %heads_scatter.1 = (f32[2,128,2048]{2,1,0:T(8,128)}, f32[2,2048]{1,0:T(2,128)}, bf16[3,2048,256]{2,1,0:T(8,128)(2,1)}, bf16[1,256,2048]{2,1,0:T(8,128)(2,1)}, f32[2,256]{1,0:T(2,128)}) custom-call(bf16[3,2,1024,256]{3,2,1,0:T(8,128)(2,1)} %get-tuple-element.55.grads, bf16[3,2048,256]{2,1,0:T(8,128)(2,1)} %weight.5, ...), custom_call_target="tpu_custom_call" | custom-call | tf_op jit(solution)/shard_map/heads_scatter/pallas_call | solution.py:983
  572.7 0.0 copy-start.2
  572.7 1.5 fusion.1
  574.2 0.0 copy-done.5
  574.2 0.6 fusion
  574.8 2.8 bitcast_convert_fusion.2
  577.6 0.0 copy-done.2
  577.6 0.0 copy-start.1
  577.6 3.5 convert_element_type.11
  581.1 0.5 copy-done.1
  581.6 0.0 copy-start
  581.6 4.7 bitcast_convert_fusion.1
  586.3 0.0 copy-done
  586.3 0.0 copy-start.4
  586.3 0.0 copy-start.3
  586.3 4.7 bitcast_convert_fusion
  591.0 0.0 copy-done.4
  591.0 0.0 copy-start.7
  591.1 0.0 copy-start.6
  591.1 1.0 copy.33
  592.0 0.0 copy-done.3
  592.0 1.3 copy.34
  593.3 0.0 copy-done.7
  593.3 0.6 copy.35
  593.9 0.0 copy-done.6
  593.9 0.6 copy.36
Async XLA Ops:
  465.7 108.5 %copy-start.5 = (f32[4,2048]{1,0:T(4,128)S(1)}, f32[4,2048]{1,0:T(4,128)}, u32[]{:S(2)}) copy-start(f32[4,2048]{1,0:T(4,128)} %get-tuple-element.64) | copy-start | bytes 98308
  572.7 4.9 copy-start.2
  577.6 3.9 copy-start.1
  581.6 4.7 copy-start
  586.3 4.8 copy-start.4
  586.3 5.7 copy-start.3
  591.0 2.3 copy-start.7
  591.1 2.9 copy-start.6

commit v7 on v6

--- a/solution.py
+++ b/solution.py
@@ -73,22 +73,29 @@
 PIECE = 12.0
 
 
-def gather_ops(c, chips, seqs, kind, name, rank=0, time=0.5, gate=False):
+def gather_ops(c, chips, seqs, kind, name, rank=0, time=0.5, gate=False, own=None):
     ops = []
     for s in range(seqs):
         for o in range(chips):
-            sends = []
+            up, down = [], []
             if o <= c < chips - 1:
-                sends.append((c + 1, c + 1, (name, c + 1, s, o), PIECE))
+                up.append((c + 1, c + 1, (name, c + 1, s, o), PIECE))
             if o >= c > 0:
-                sends.append((c - 1, c - 1, (name, c - 1, s, o), PIECE))
+                down.append((c - 1, c - 1, (name, c - 1, s, o), PIECE))
+            both = [(3.0, (name, c, s, o, "both"))]
+            if own is not None and o == c and s > 0:
+                ops.append(((rank, s, -1), (own[0], s, o), [], time, [], both))
+                for sends, which, others in ((up, own[1], range(c)), (down, own[2], range(c + 1, chips))):
+                    needs = [(name, c, t, other) for t in (s - 1, s) for other in others]
+                    if sends:
+                        ops.append(((rank, s, chips), (which, s, o), needs, time, sends, []))
+                continue
             needs = [] if o == c else [(name, c, s, o)]
             if gate and o == c and s > 0:
                 for other in range(chips):
                     if other < c < chips - 1 or other > c > 0:
                         needs.append((name, c, s - 1, other))
-            both = [(3.0, (name, c, s, o, "both"))]
-            ops.append(((rank, s, abs(o - c)), (kind, s, o), needs, time, sends, both))
+            ops.append(((rank, s, abs(o - c)), (kind, s, o), needs, time, up + down, both))
     return ops
 
 
@@ -126,19 +133,19 @@
     ]
 
 
-def group_ops(c, bits, count, span, code_of, skip, turn, first_time, rank=3, name="group"):
+def group_ops(c, bits, count, span, code_of, skip, turns, first_time, rank=3, name="group"):
     ops = []
     for t in range(count):
         for stage in range(skip, 2 * bits + 1):
-            needs = []
-            if stage > skip:
-                needs = [(name, c, t, stage)]
-            sends = []
-            if stage < 2 * bits:
-                i = stage if stage < bits else 2 * bits - 1 - stage
-                axis = "axis%d" % ((t + turn + i) % bits)
-                sends = [(axis, c, (name, c, t, stage + 1), span / 2**i)]
-            time = first_time if stage == 0 else 0.7
+            needs, sends = [], []
+            for turn in turns:
+                if stage > skip:
+                    needs.append((name, c, turn, t, stage))
+                if stage < 2 * bits:
+                    i = stage if stage < bits else 2 * bits - 1 - stage
+                    axis = "axis%d" % ((t + turn + i) % bits)
+                    sends.append((axis, c, (name, c, turn, t, stage + 1), span / 2**i))
+            time = first_time if stage == 0 else 0.8 * len(turns)
             code = code_of((stage - skip) * count + t)
             ops.append(((rank, stage, t), code, needs, time, sends, []))
     return ops
@@ -148,15 +155,19 @@
     def __init__(self, at, seqs, ops_of):
         chips = at.chips
         order, self.length = order_of(chips, ops_of)
-        self.per, self.chips, self.seqs = 128, chips, seqs
+        self.per, self.each, self.chips, self.seqs = 1024, 3, chips, seqs
         self.count = max(len(codes) for codes in order)
-        assert 8 * seqs * chips <= self.per
+        idle = self.per // (seqs * chips) - 1
         rows = []
         for codes in order:
+            assert all(kind < idle for kind, s, o in codes)
             flat = [(kind * seqs + s) * chips + o for kind, s, o in codes]
-            flat += [7 * seqs * chips] * (self.count - len(flat) + 4)
+            flat += [idle * seqs * chips] * (self.count - len(flat) + self.each)
             rows.append(
-                [sum(flat[i + j] * self.per**j for j in range(4)) for i in range(0, self.count, 4)]
+                [
+                    sum(flat[i + j] * self.per**j for j in range(self.each))
+                    for i in range(0, self.count, self.each)
+                ]
             )
         self.words = []
         for w in range(len(rows[0])):
@@ -166,12 +177,12 @@
             self.words.append(word)
 
     def step(self, k):
-        which, slot = k // 4, lax.rem(k, 4)
+        which, slot = k // self.each, lax.rem(k, self.each)
         word = jnp.int32(0)
         for w, value in enumerate(self.words):
             word = jnp.where(which == w, value, word)
         code = word
-        for j in range(1, 4):
+        for j in range(1, self.each):
             code = jnp.where(slot == j, word // self.per**j, code)
         code = lax.rem(code, self.per)
         each = self.seqs * self.chips
@@ -209,7 +220,7 @@
         mine = lax.rem(self.me // 2**q, 2)
         return self.me + (1 - 2 * mine) * 2**q
 
-    def greet(self, groups=False, cube=False):
+    def greet(self, groups=False, cube=False, everyone=False):
         barrier = pltpu.get_barrier_semaphore()
 
         def tell(target):
@@ -227,6 +238,13 @@
                     barrier, inc=1, device_id={"dp": self.group_peer(q)[0]}, device_id_type=MESH
                 )
             peers = peers + self.group_bits
+        if everyone:
+            for other in range(1, self.n):
+                tell(lax.rem(self.me + other, self.n))
+            for other in range(1, 2**self.group_bits):
+                peer = lax.rem(self.group + other, 2**self.group_bits)
+                pl.semaphore_signal(barrier, inc=1, device_id={"dp": peer}, device_id_type=MESH)
+            peers = peers + (self.n - 1 + 2**self.group_bits - 1)
         if cube:
             for q in range(self.bits):
                 tell(self.peer(q))
@@ -281,6 +299,15 @@
         pl.when((o <= at.chip) & at.above)(lambda: self.copy(s, o, UP).start())
         pl.when((o >= at.chip) & at.below)(lambda: self.copy(s, o, DOWN).start())
         self.copy(s, o, SIDE).start()
+
+    def own(self, kind, s, o):
+        self.copy(s, o, kind).start()
+
+    def owns(self, kinds):
+        return {
+            which: functools.partial(self.own, kind)
+            for which, kind in zip(kinds, (SIDE, UP, DOWN))
+        }
 
     def finish(self):
         at = self.at
@@ -514,13 +541,13 @@
         bits = self.bits
 
         def at_stage(stage):
+            if stage == self.skip and loaded is not None:
+                loaded(t)
             if stage == 0:
                 self.halve(t, 0).start()
             elif stage <= bits:
                 if stage > self.skip:
                     self.halve(t, stage - 1).wait_recv()
-                else:
-                    loaded(t)
                 self.add(t, stage - 1)
                 if stage < bits:
                     self.halve(t, stage).start()
@@ -597,6 +624,53 @@
     def finish(self):
         for i in range(self.phases):
             self.copy(i).wait_send()
+
+
+class DirectSum:
+    def __init__(self, at, rows, group_box, line_box, send, recv):
+        self.at, self.rows, self.send, self.recv = at, rows, send, recv
+        self.boxes = (group_box, line_box)
+
+    @staticmethod
+    def scratch(dp, n, count, width):
+        most = max(dp, n)
+        return [
+            VMEM((count, width), f32),
+            VMEM((dp, count, width), f32),
+            VMEM((n, count, width), f32),
+            DMA((2, most)),
+            DMA((2, most)),
+        ]
+
+    def copy(self, step, other, back=False):
+        at, box = self.at, self.boxes[step]
+        size, axis = box.shape[0], ("dp", "tensor")[step]
+        mine = (at.group, at.me)[step]
+        peer = lax.rem(mine + other, size)
+        slot = peer if back else mine
+        return pltpu.make_async_remote_copy(
+            src_ref=box.at[mine],
+            dst_ref=box.at[slot],
+            send_sem=self.send.at[step, other],
+            recv_sem=self.recv.at[step, slot],
+            device_id={axis: peer},
+            device_id_type=MESH,
+        )
+
+    def run(self):
+        for step, box in enumerate(self.boxes):
+            box[(self.at.group, self.at.me)[step]] = self.rows[...]
+            for other in range(1, box.shape[0]):
+                self.copy(step, other).start()
+            for other in range(1, box.shape[0]):
+                self.copy(step, other, back=True).wait_recv()
+            total = box[0]
+            for i in range(1, box.shape[0]):
+                total = total + box[i]
+            self.rows[...] = total
+        for step, box in enumerate(self.boxes):
+            for other in range(1, box.shape[0]):
+                self.copy(step, other).wait_send()
 
 
 def norm_rows(values, gain, shift):
@@ -871,11 +945,11 @@
     n,
     grads,
     weight,
-    gathered,
+    gathered_hbm,
     out_part,
-    tokens,
+    tokens_hbm,
     gain,
-    hidden_grad,
+    hidden_hbm,
     grad,
     sums_all,
     weight_grad,
@@ -884,26 +958,34 @@
     *scratch,
 ):
     at = Place(n)
-    seqs, rows, width = hidden_grad.shape
+    seqs, rows, width = hidden_hbm.shape
     line = Scatter(at, rows, *scratch[:7])
     weight_sum = GroupSum(at, width, *scratch[7:12], weight_grad)
     out_sum = GroupSum(at, out_part.shape[0], *scratch[12:17], out_grad, turn=1)
-    small = SmallSum(at, *scratch[17:21], True)
-    small_bias = SmallSum(at, *scratch[21:25], False)
+    small = DirectSum(at, *scratch[17:22])
+    small_bias = SmallSum(at, *scratch[22:26], False)
+    gathered, tokens, hidden_grad, in_sem = scratch[26:]
+    sources = ((gathered_hbm, gathered), (tokens_hbm, tokens), (hidden_hbm, hidden_grad))
+    loads = [
+        pltpu.make_async_copy(source, target, in_sem.at[i])
+        for i, (source, target) in enumerate(sources)
+    ]
+    for copy in loads:
+        copy.start()
     out_sum.tiles[0] = out_part[...]
-    small.rows[0] = jnp.zeros(small.rows.shape[1:], f32)
+    small.rows[...] = jnp.zeros_like(small.rows)
     for row, j, scale in ((0, 0, HD ** (-0.5)), (1, 2, 1.0)):
         total = 0.0
         for s in range(seqs):
             total += jnp.sum(grads[j, s].astype(f32), axis=0, keepdims=True)
         small_bias.rows[0, row : row + 1] = scale * total
-    at.greet(groups=True, cube=True)
+    at.greet(groups=True, everyone=True)
 
     def final(s, there, total):
         back, terms = norm_rows_back(tokens[s, there].astype(f32), total, gain[...])
         grad[s, there] = hidden_grad[s, there] + back
-        small.rows[0, 0:1] += jnp.sum(terms, axis=0, keepdims=True)
-        small.rows[0, 1:2] += jnp.sum(total, axis=0, keepdims=True)
+        add_row(small.rows, 0, terms)
+        add_row(small.rows, 1, total)
 
     scales = (HD ** (-0.5), 1.0, 1.0)
 
@@ -935,6 +1017,12 @@
 
     def weight_event(first, s, o):
         e = first + s * at.chips + o
+
+        @pl.when(e == 0)
+        def _():
+            for copy in loads:
+                copy.wait()
+
         for j in range(3):
             pl.when(e == j)(functools.partial(weight_tile, j))
         weight_sum.event(e)
@@ -947,14 +1035,19 @@
 
     def ops_of(c):
         chips = at.chips
+        finals = scatter_ops(c, chips, seqs, 1, "out", "part", last=4.0)
+        loaded = ("qkv", c, 0, 0, 1)
+        for i, (rank, code, needs, time, sends, gives) in enumerate(finals):
+            if code[2] == c:
+                finals[i] = (rank, code, needs + [loaded], time, sends, gives)
         return (
             work_ops(c, chips, seqs, 0, lambda s, o: [], "part", 1.5, rank=0, far=True)
-            + scatter_ops(c, chips, seqs, 1, "out", "part", last=4.0)
+            + finals
             + group_ops(
-                c, at.group_bits, 3, PIECE, lambda e: code_of(2, e), 0, 0, 2.7, name="qkv"
+                c, at.group_bits, 3, PIECE, lambda e: code_of(2, e), 0, (0,), 2.7, name="qkv"
             )
             + group_ops(
-                c, at.group_bits, 1, PIECE, lambda e: code_of(5, e), 0, 1, 0.7, name="out_sum"
+                c, at.group_bits, 1, PIECE, lambda e: code_of(5, e), 0, (1,), 0.7, name="out_sum"
             )
         )
 
@@ -962,14 +1055,12 @@
     for i in range(3):
         actions[2 + i] = functools.partial(weight_event, i * each)
     Plan(at, seqs, ops_of).run(actions, small_bias.event)
-    for e in range(small.phases + 1):
-        small.event(e)
-    sums_all[...] = small.rows[small.phases]
+    small.run()
+    sums_all[...] = small.rows[...]
     bias_grad[...] = small_bias.rows[small_bias.phases]
     line.finish()
     weight_sum.finish()
     out_sum.finish()
-    small.finish()
     small_bias.finish()
 
 
@@ -989,13 +1080,19 @@
             jax.ShapeDtypeStruct((1, part, width), bf16),
             jax.ShapeDtypeStruct((2, part), f32),
         ),
-        in_specs=whole(7),
+        in_specs=[vmem, vmem, hbm, vmem, hbm, vmem, hbm],
         out_specs=(vmem, vmem, hbm, hbm, vmem),
         scratch_shapes=Scatter.scratch(n, seqs, rows, width)
         + GroupSum.scratch(dp, 3, width, part)
         + GroupSum.scratch(dp, 1, part, width)
-        + SmallSum.scratch(dp, n, 2, width, True)
-        + SmallSum.scratch(dp, n, 2, part, False),
+        + DirectSum.scratch(dp, n, 2, width)
+        + SmallSum.scratch(dp, n, 2, part, False)
+        + [
+            VMEM(gathered.shape, bf16),
+            VMEM(tokens.shape, bf16),
+            VMEM(hidden_grad.shape, f32),
+            DMA((3,)),
+        ],
         compiler_params=pltpu.CompilerParams(
             collective_id=2, has_side_effects=True, vmem_limit_bytes=62 * 2**20
         ),
@@ -1025,11 +1122,11 @@
 def mlp_kernel(
     n,
     normed,
-    grad_all,
-    up_weight,
+    grad_hbm,
+    up_hbm,
     up_bias,
-    down_weight,
-    hidden,
+    down_hbm,
+    hidden_hbm,
     gain,
     mlp_part,
     hidden_grad,
@@ -1038,11 +1135,15 @@
     up_grad,
     up_bias_grad,
     down_grad,
-    up_box,
     down_box,
     buf,
     send,
     recv,
+    grad_all,
+    up_weight,
+    down_weight,
+    hidden,
+    in_sem,
     *scratch,
 ):
     at = Place(n)
@@ -1051,6 +1152,19 @@
     line = Scatter(at, rows, *scratch[:7])
     act, pre, out_stage, out_sem, up_stage, down_stage, tile_sem, half_send, half_recv = scratch[7:]
     ring = Gather(at, rows, buf, send, recv)
+    loads = [
+        pltpu.make_async_copy(source, target, in_sem.at[i])
+        for i, (source, target) in enumerate(
+            (
+                (up_hbm, up_weight),
+                (grad_hbm, grad_all),
+                (down_hbm, down_weight),
+                (hidden_hbm, hidden),
+            )
+        )
+    ]
+    for copy in loads:
+        copy.start()
     at.greet(groups=True)
     for s in range(seqs):
         buf[s, rows_of(at.me, rows)] = normed[s]
@@ -1065,6 +1179,12 @@
 
     def work(s, o):
         ring.arrived(s, o, 1 - at.core)
+
+        @pl.when((s == 0) & (o == at.chip))
+        def _():
+            for copy in loads:
+                copy.wait()
+
         here = rows_of(o, 2 * rows)
         for j in range(units_wide // ft):
             cols = pl.ds(j * ft, ft)
@@ -1105,31 +1225,30 @@
         add_row(sums, 2, grad)
         add_row(sums, 3, grad_out)
 
-    kinds = ((down_stage, down_grad, down_box, 0), (up_stage, up_grad, up_box, 1))
+    kinds = ((down_stage, down_grad), (up_stage, up_grad))
 
     def tile_copy(kind, t):
-        stage, grad, box, turn = kinds[kind]
+        stage, grad = kinds[kind]
         return pltpu.make_async_copy(stage, grad.at[t], tile_sem.at[kind])
 
-    def tile_half(kind, t):
-        stage, grad, box, turn = kinds[kind]
-        half = box.shape[1]
-        which = (t + turn) % at.group_bits
-        peer, mine = at.group_peer(which)
+    def down_half(t):
+        half = down_box.shape[1]
+        peer, mine = at.group_peer(t % at.group_bits)
         return pltpu.make_async_remote_copy(
-            src_ref=grad.at[t, rows_of(1 - mine, half)],
-            dst_ref=box.at[t],
-            send_sem=half_send.at[kind, t],
-            recv_sem=half_recv.at[kind, t],
+            src_ref=down_grad.at[t, rows_of(1 - mine, half)],
+            dst_ref=down_box.at[t],
+            send_sem=half_send.at[t],
+            recv_sem=half_recv.at[t],
             device_id={"dp": peer},
             device_id_type=MESH,
         )
 
     def tile_sent(kind, t):
         tile_copy(kind, t).wait()
-        tile_half(kind, t).start()
-
-    order = [(i % 2, i // 2) for i in range(8)]
+        if kind == 0:
+            down_half(t).start()
+
+    order = [(i // 4, i % 4) for i in range(8)]
 
     def weight_tile(i):
         for j, (kind, t) in enumerate(order):
@@ -1152,11 +1271,13 @@
     def tile_work(s, o):
         weight_tile(s * at.chips + o)
 
+    own = (4, 5, 6)
+
     def ops_of(c):
         chips = at.chips
         units = [(s, o) for s in range(seqs) for o in range(chips)]
         ops = (
-            gather_ops(c, chips, seqs, 0, "in")
+            gather_ops(c, chips, seqs, 0, "in", own=own)
             + scatter_ops(c, chips, seqs, 1, "back", "part", last=4.0)
             + work_ops(
                 c, chips, seqs, 2, lambda s, o: [("in", c, s, o, "both")], "part", 5.7
@@ -1171,19 +1292,19 @@
         for e in range(len(order)):
             needs = [("part", c, s, o) for s, o in units]
             needs += [("tile", c, e - 1)] if e else []
-            sends = [("axis%d" % (e % 2), c, ("half", c, e), PIECE)]
+            sends = [("axis%d" % (e % 2), c, ("half", c, e), PIECE)] if e < 4 else []
             code = (3, e // chips, e % chips)
             ops.append(((4, e, 0), code, needs, 2.7, sends, [(0.0, ("tile", c, e))]))
         return ops
 
-    Plan(at, seqs, ops_of).run(
-        {0: ring.relay, 1: functools.partial(line.pass_on, final), 2: work, 3: tile_work}
-    )
+    actions = {0: ring.relay, 1: functools.partial(line.pass_on, final), 2: work, 3: tile_work}
+    actions.update(ring.owns(own))
+    Plan(at, seqs, ops_of).run(actions)
     tile_sent(*order[7])
     ring.finish()
     line.finish()
-    for kind, t in order:
-        tile_half(kind, t).wait()
+    for t in range(4):
+        down_half(t).wait()
     out_copy(0, 0).wait()
 
 
@@ -1204,13 +1325,19 @@
             jax.ShapeDtypeStruct((4, up_size, units), bf16),
             jax.ShapeDtypeStruct((1, units), f32),
             jax.ShapeDtypeStruct((4, down_size, width), bf16),
-            jax.ShapeDtypeStruct((4, up_size // 2, units), bf16),
             jax.ShapeDtypeStruct((4, down_size // 2, width), bf16),
         ),
-        in_specs=whole(7),
-        out_specs=(hbm, vmem, vmem, vmem, hbm, vmem, hbm, hbm, hbm),
+        in_specs=[vmem, hbm, hbm, vmem, hbm, hbm, vmem],
+        out_specs=(hbm, vmem, vmem, vmem, hbm, vmem, hbm, hbm),
         scratch_shapes=[VMEM((seqs, slots, width), bf16)]
         + Gather.scratch(n, seqs)
+        + [
+            VMEM((seqs, slots, width), bf16),
+            VMEM(up_weight.shape, bf16),
+            VMEM(down_weight.shape, bf16),
+            VMEM(hidden.shape, f32),
+            DMA((4,)),
+        ]
         + Scatter.scratch(n, seqs, rows, width)
         + [
             VMEM((seqs, slots, units), bf16),
@@ -1220,8 +1347,8 @@
             VMEM((up_size, units), bf16),
             VMEM((down_size, width), bf16),
             DMA((2,)),
-            DMA((2, 4)),
-            DMA((2, 4)),
+            DMA((4,)),
+            DMA((4,)),
         ],
         compiler_params=pltpu.CompilerParams(
             collective_id=3, has_side_effects=True, vmem_limit_bytes=62 * 2**20
@@ -1242,7 +1369,6 @@
     up_bias_part,
     up_part,
     down_part,
-    up_box,
     down_box,
     lengths,
     heads,
@@ -1263,31 +1389,33 @@
     line = Scatter(at, rows, *scratch[:7])
     load_sem, tile_sem, box_sem = scratch[7:10]
     ring = Gather(at, rows, buf, send, recv)
-    up_sum = GroupSum(at, up_part.shape[1], *scratch[10:15], up_grad, turn=1, skip=1)
+    up_sum = GroupSum(at, up_part.shape[1], *scratch[10:15], up_grad, turn=1)
     down_sum = GroupSum(at, down_part.shape[1], *scratch[15:20], down_grad, skip=1)
     small = SmallSum(at, *scratch[20:24], True)
     small_bias = SmallSum(at, *scratch[24:28], False)
     grad_heads, grad_key, grad_value = scratch[28:]
-    pairs = ((up_sum, up_part, up_box), (down_sum, down_part, down_box))
-
-    def tile_load(i, t):
-        group, part, box = pairs[i]
-        half = box.shape[1]
+    def up_load(t):
+        return pltpu.make_async_copy(up_part.at[t], up_sum.tiles.at[t], tile_sem.at[0, t])
+
+    def down_load(t):
+        half = down_box.shape[1]
+        kept = down_part.at[t, down_sum.span(down_sum.base(t, 1), half)]
         return (
-            pltpu.make_async_copy(
-                part.at[t, group.span(group.base(t, 1), half)], group.tiles.at[t], tile_sem.at[i, t]
-            ),
-            pltpu.make_async_copy(box.at[t], group.box(t, 0), box_sem.at[i, t]),
-        )
-
-    def tile_loaded(i, t):
-        for copy in tile_load(i, t):
+            pltpu.make_async_copy(kept, down_sum.tiles.at[t], tile_sem.at[1, t]),
+            pltpu.make_async_copy(down_box.at[t], down_sum.box(t, 0), box_sem.at[t]),
+        )
+
+    def up_loaded(t):
+        up_load(t).wait()
+
+    def down_loaded(t):
+        for copy in down_load(t):
             copy.wait()
 
     for t in range(4):
-        for i in range(2):
-            for copy in tile_load(i, t):
-                copy.start()
+        up_load(t).start()
+        for copy in down_load(t):
+            copy.start()
     small.rows[0] = sums[...]
     small_bias.rows[0] = up_bias_part[...]
 
@@ -1324,34 +1452,41 @@
         block = min(512, n * rows)
         attend_back(heads, grad_heads, lengths, grads, grad_key, grad_value, block, s)
 
-    def event(i, s, o):
-        e = s * at.chips + o
-        for j in range(2):
-            group = pairs[j][0]
-            group.event(e + i * each, functools.partial(tile_loaded, j))
+    def up_event(first, s, o):
+        up_sum.event(first + s * at.chips + o, up_loaded)
+
+    def down_event(first, s, o):
+        down_sum.event(first + s * at.chips + o, down_loaded)
 
     def ops_of(c):
         chips = at.chips
-        code_of = lambda e: (4 + e // each, e % each // chips, e % chips)
+        code_of = lambda kind, e: (kind + e // each, e % each // chips, e % chips)
         backs = []
         for s in range(seqs):
             needs = [("done", c, s, o) for o in range(chips)]
-            backs.append(((4, s, 0), (6, s, 0), needs, 8.0, [], []))
+            backs.append(((4, s, 0), (4, s, 0), needs, 8.0, [], []))
         return backs + (
             gather_ops(c, chips, seqs, 0, "in")
             + scatter_ops(c, chips, seqs, 1, "out", "part", last=4.0)
             + work_ops(c, chips, seqs, 2, lambda s, o: [("in", c, s, o, "both")], "done", 1.0)
             + work_ops(c, chips, seqs, 3, lambda s, o: [], "part", 0.3, rank=0, far=True)
-            + group_ops(c, at.group_bits, 4, PIECE, code_of, 1, 0, 0.7)
+            + group_ops(
+                c, at.group_bits, 4, PIECE, lambda e: code_of(8, e), 0, (1,), 0.7, name="up"
+            )
+            + group_ops(
+                c, at.group_bits, 4, PIECE, lambda e: code_of(16, e), 1, (0,), 0.7, name="down"
+            )
         )
 
     actions = {0: ring.relay, 1: functools.partial(line.pass_on, final), 2: work, 3: share}
-    for i in range(2):
-        actions[4 + i] = functools.partial(event, i)
-    actions[6] = back
+    actions[4] = back
+    for i in range(-(-up_sum.events() // each)):
+        actions[8 + i] = functools.partial(up_event, i * each)
+    for i in range(-(-down_sum.events() // each)):
+        actions[16 + i] = functools.partial(down_event, i * each)
 
     def beside(k):
-        pl.when(lax.rem(k, 3) == 0)(lambda: small.event(k // 3))
+        pl.when(lax.rem(k, 8) == 0)(lambda: small.event(k // 8))
         small_bias.event(k)
 
     Plan(at, seqs, ops_of).run(actions, beside)
@@ -1383,7 +1518,6 @@
     up_bias_part,
     up_part,
     down_part,
-    up_box,
     down_box,
     lengths,
     heads,
@@ -1408,14 +1542,14 @@
         ),
         in_specs=[vmem, hbm]
         + [vmem] * 6
-        + [hbm] * 4
+        + [hbm] * 3
         + [pl.BlockSpec(memory_space=pltpu.SMEM), vmem],
         out_specs=(vmem,) * 5 + (hbm, hbm),
         scratch_shapes=[VMEM((seqs, slots, width), bf16)]
         + Gather.scratch(n, seqs)
         + Scatter.scratch(n, seqs, rows, width)
-        + [DMA((seqs, n // 2)), DMA((2, 4)), DMA((2, 4))]
-        + GroupSum.scratch(dp, 4, width // 4, units, 1)
+        + [DMA((seqs, n // 2)), DMA((2, 4)), DMA((4,))]
+        + GroupSum.scratch(dp, 4, width // 4, units)
         + GroupSum.scratch(dp, 4, units // 4, width, 1)
         + SmallSum.scratch(dp, n, sums.shape[0], width, True)
         + SmallSum.scratch(dp, n, 1, units, False)
@@ -1435,7 +1569,6 @@
         up_bias_part,
         up_part,
         down_part,
-        up_box,
         down_box,
         lengths,
         heads,
@@ -1482,7 +1615,6 @@
         up_part,
         up_bias_part,
         down_part,
-        up_box,
         down_box,
     ) = mlp_block(
         n, normed_two, grad_mlp, up_weight, up_bias[None], down_weight, hidden_state, ln2_gain[None]
@@ -1499,7 +1631,6 @@
         up_bias_part,
         up_part,
         down_part,
-        up_box,
         down_box,
         lengths,
         heads,

time: 598 us -> 566 us (0.946)
  Pallas kernels: 572 us -> 540 us
    pallas_call x1, Pallas kernels: 147 us -> 124 us  [mlp_block(): pl.pallas_call(functools.partial(mlp_kernel, n), out_shape=(jax.ShapeDtyp...]
    pallas_call x1, Pallas kernels: 143 us -> 134 us  [attn_grad(): pl.pallas_call(functools.partial(attn_grad_kernel, n), out_shape=(jax.Sha...]
where the time goes in v7:
time: 566 us; the launch traced here: 563 us
  Pallas kernels  540 us (95%)
  other arithmetic  15.8 us (3%)
  local copies, waits for them, and re-layouts  6.06 us (1%)
    pallas_call x1, Pallas kernels, attention_block(): pl.pallas_call(functools.partial(attention_block_kernel, n), out_shape=(j...  175 us
    pallas_call x1, Pallas kernels, attn_grad(): pl.pallas_call(functools.partial(attn_grad_kernel, n), out_shape=(jax.Sha...  134 us
    pallas_call x1, Pallas kernels, mlp_block(): pl.pallas_call(functools.partial(mlp_kernel, n), out_shape=(jax.ShapeDtyp...  124 us
    pallas_call x1, Pallas kernels, heads_scatter(): pl.pallas_call(functools.partial(heads_scatter_kernel, n), out_shape=(jax...  106 us

profile of v7, /device:TPU:0, one launch (start us, length us, event | category | flops | bytes accessed | tf_op | source)
XLA Modules:
  0.0 562.7 jit_solution(1208447957384416678)
XLA Ops:
  0.6 175.5 %attention_block.1 = (bf16[2,1024,2048]{2,1,0:T(8,128)(2,1)}, bf16[3,2,1024,256]{3,2,1,0:T(8,128)(2,1)}, bf16[2,1024,256]{2,1,0:T(8,128)(2,1)}, f32[2,128,2048]{...) custom-call(bf16[2,128,2048]{2,1,0:T(8,128)(2,1)} %tokens_hbm.1, ...), custom_call_target="tpu_custom_call" | custom-call | tf_op jit(solution)/shard_map/attention_block/pallas_call | solution.py:907
  176.1 124.4 %mlp_block.1 = (bf16[2,1024,2048]{2,1,0:T(8,128)(2,1)}, f32[2,128,2048]{2,1,0:T(8,128)}, bf16[2,128,2048]{2,1,0:T(8,128)(2,1)}, f32[4,2048]{1,0:T(4,128)}, bf16[...) custom-call(bf16[2,128,2048]{2,1,0:T(8,128)(2,1)} %get-tuple-element, ...), custom_call_target="tpu_custom_call" | custom-call | tf_op jit(solution)/shard_map/mlp_block/pallas_call | solution.py:1318
  300.5 133.7 %attn_grad.1 = (bf16[2,128,2048]{2,1,0:T(8,128)(2,1)}, bf16[3,2,1024,256]{3,2,1,0:T(8,128)(2,1)}, bf16[256,2048]{1,0:T(8,128)(2,1)}, f32[4,2048]{1,0:T(4,128)}, ...) custom-call(bf16[2,128,2048]{2,1,0:T(8,128)(2,1)} %get-tuple-element.43.grad, ...), custom_call_target="tpu_custom_call" | custom-call | tf_op jit(solution)/shard_map/attn_grad/pallas_call | solution.py:1532
  434.2 0.0 copy-start.5
  434.2 106.4 %heads_scatter.1 = (f32[2,128,2048]{2,1,0:T(8,128)}, f32[2,2048]{1,0:T(2,128)}, bf16[3,2048,256]{2,1,0:T(8,128)(2,1)}, bf16[1,256,2048]{2,1,0:T(8,128)(2,1)}, f32[2,256]{1,0:T(2,128)}) custom-call(bf16[3,2,1024,256]{3,2,1,0:T(8,128)(2,1)} %get-tuple-element.53.grads, bf16[3,2048,256]{2,1,0:T(8,128)(2,1)} %weight.5, ...), custom_call_target="tpu_custom_call" | custom-call | tf_op jit(solution)/shard_map/heads_scatter/pallas_call | solution.py:1074
  540.6 0.0 copy-start.2
  540.6 1.5 fusion.1
  542.1 0.0 copy-done.5
  542.1 0.6 fusion
  542.7 2.8 bitcast_convert_fusion.2
  545.5 0.0 copy-done.2
  545.5 0.0 copy-start.1
  545.5 3.5 convert_element_type.11
  549.0 0.5 copy-done.1
  549.5 0.0 copy-start
  549.5 4.7 bitcast_convert_fusion.1
  554.2 0.0 copy-done
  554.2 0.0 copy-start.4
  554.2 0.0 copy-start.3
  554.2 4.7 bitcast_convert_fusion
  559.0 0.0 copy-done.4
  559.0 0.0 copy-start.7
  559.0 0.0 copy-start.6
  559.0 1.0 copy.33
  559.9 0.0 copy-done.3
  559.9 1.3 copy.34
  561.3 0.0 copy-done.7
  561.3 0.6 copy.35
  561.8 0.0 copy-done.6
  561.8 0.6 copy.36
Async XLA Ops:
  434.2 107.9 %copy-start.5 = (f32[4,2048]{1,0:T(4,128)S(1)}, f32[4,2048]{1,0:T(4,128)}, u32[]{:S(2)}) copy-start(f32[4,2048]{1,0:T(4,128)} %get-tuple-element.62) | copy-start | bytes 98308
  540.6 4.9 copy-start.2
  545.5 3.9 copy-start.1
  549.5 4.7 copy-start
  554.2 4.8 copy-start.4
  554.2 5.7 %copy-start.3 = (f32[2,128,2048]{2,1,0:T(8,128)S(1)}, f32[2,128,2048]{2,1,0:T(8,128)}, u32[]{:S(2)}) copy-start(f32[2,128,2048]{2,1,0:T(8,128)} %get-tuple-element.87) | copy-start | bytes 6291460
  559.0 2.3 copy-start.7
  559.0 2.9 copy-start.6

commit v8 on v7

--- a/solution.py
+++ b/solution.py
@@ -23,7 +23,7 @@
 TN = (((0,), (0,)), ((), ()))
 
 
-def order_of(chips, ops_of, backlog=8.0, hop=1.5):
+def order_of(chips, ops_of, backlog=8.0, hop=2.0):
     todo = [sorted(ops_of(c)) for c in range(chips)]
     order = [[] for _ in range(chips)]
     free, busy, have, queue = {}, [False] * chips, set(), []
@@ -114,7 +114,8 @@
             if o < c:
                 sends = [(c - 1, c - 1, (name, c - 1, s, o, "above"), PIECE)]
             order = (rank, s, -abs(o - c)) if o != c else (8, s, 0)
-            ops.append((order, (kind, s, o), needs, last if o == c else time, sends, []))
+            ends = [(0.0, (name, c, s, "sum"))] if o == c else []
+            ops.append((order, (kind, s, o), needs, last if o == c else time, sends, ends))
     return ops
 
 
@@ -657,17 +658,22 @@
             device_id_type=MESH,
         )
 
-    def run(self):
-        for step, box in enumerate(self.boxes):
-            box[(self.at.group, self.at.me)[step]] = self.rows[...]
+    def event(self, e):
+        if e > 0:
+            box = self.boxes[e - 1]
             for other in range(1, box.shape[0]):
-                self.copy(step, other).start()
-            for other in range(1, box.shape[0]):
-                self.copy(step, other, back=True).wait_recv()
+                self.copy(e - 1, other, back=True).wait_recv()
             total = box[0]
             for i in range(1, box.shape[0]):
                 total = total + box[i]
             self.rows[...] = total
+        if e < 2:
+            box = self.boxes[e]
+            box[(self.at.group, self.at.me)[e]] = self.rows[...]
+            for other in range(1, box.shape[0]):
+                self.copy(e, other).start()
+
+    def finish(self):
         for step, box in enumerate(self.boxes):
             for other in range(1, box.shape[0]):
                 self.copy(step, other).wait_send()
@@ -974,12 +980,20 @@
         copy.start()
     out_sum.tiles[0] = out_part[...]
     small.rows[...] = jnp.zeros_like(small.rows)
-    for row, j, scale in ((0, 0, HD ** (-0.5)), (1, 2, 1.0)):
-        total = 0.0
-        for s in range(seqs):
-            total += jnp.sum(grads[j, s].astype(f32), axis=0, keepdims=True)
-        small_bias.rows[0, row : row + 1] = scale * total
     at.greet(groups=True, everyone=True)
+
+    def bias_sums():
+        for row, j, scale in ((0, 0, HD ** (-0.5)), (1, 2, 1.0)):
+            total = 0.0
+            for s in range(seqs):
+                total += jnp.sum(grads[j, s].astype(f32), axis=0, keepdims=True)
+            small_bias.rows[0, row : row + 1] = scale * total
+
+    def beside(k):
+        pl.when(k == 10)(bias_sums)
+        for e in range(small_bias.phases + 1):
+            pl.when(k == 11 + 6 * e)(functools.partial(small_bias.event, e))
+
 
     def final(s, there, total):
         back, terms = norm_rows_back(tokens[s, there].astype(f32), total, gain[...])
@@ -1040,8 +1054,13 @@
         for i, (rank, code, needs, time, sends, gives) in enumerate(finals):
             if code[2] == c:
                 finals[i] = (rank, code, needs + [loaded], time, sends, gives)
-        return (
-            work_ops(c, chips, seqs, 0, lambda s, o: [], "part", 1.5, rank=0, far=True)
+        smalls = []
+        needs = [("out", c, s, "sum") for s in range(seqs)]
+        for e in range(3):
+            smalls.append(((0, e), (30 + e, 0, 0), needs, 0.5, [], [(4.0, ("small", c, e))]))
+            needs = [("small", c, e)]
+        return smalls + (
+            work_ops(c, chips, seqs, 0, lambda s, o: [], "part", 1.5, far=True)
             + finals
             + group_ops(
                 c, at.group_bits, 3, PIECE, lambda e: code_of(2, e), 0, (0,), 2.7, name="qkv"
@@ -1054,8 +1073,9 @@
     actions = {0: work, 1: functools.partial(line.pass_on, final), 5: out_event}
     for i in range(3):
         actions[2 + i] = functools.partial(weight_event, i * each)
-    Plan(at, seqs, ops_of).run(actions, small_bias.event)
-    small.run()
+        actions[30 + i] = lambda s, o, e=i: small.event(e)
+    Plan(at, seqs, ops_of).run(actions, beside)
+    small.finish()
     sums_all[...] = small.rows[...]
     bias_grad[...] = small_bias.rows[small_bias.phases]
     line.finish()
@@ -1452,6 +1472,14 @@
         block = min(512, n * rows)
         attend_back(heads, grad_heads, lengths, grads, grad_key, grad_value, block, s)
 
+    def weight_work(s, o):
+        for j in range(width // 512):
+            cols = pl.ds(j * 512, 512)
+            total = 0.0
+            for q in range(seqs):
+                total += lax.dot_general(mixed[q], buf[q, :, cols], TN, preferred_element_type=f32)
+            weight_grad[:, cols] = total.astype(bf16)
+
     def up_event(first, s, o):
         up_sum.event(first + s * at.chips + o, up_loaded)
 
@@ -1465,21 +1493,23 @@
         for s in range(seqs):
             needs = [("done", c, s, o) for o in range(chips)]
             backs.append(((4, s, 0), (4, s, 0), needs, 8.0, [], []))
+        needs = [("done", c, s, o) for s in range(seqs) for o in range(chips)]
+        backs.append(((5, 0, 0), (5, 0, 0), needs, 3.0, [], []))
         return backs + (
             gather_ops(c, chips, seqs, 0, "in")
             + scatter_ops(c, chips, seqs, 1, "out", "part", last=4.0)
             + work_ops(c, chips, seqs, 2, lambda s, o: [("in", c, s, o, "both")], "done", 1.0)
             + work_ops(c, chips, seqs, 3, lambda s, o: [], "part", 0.3, rank=0, far=True)
             + group_ops(
-                c, at.group_bits, 4, PIECE, lambda e: code_of(8, e), 0, (1,), 0.7, name="up"
+                c, at.group_bits, 4, PIECE, lambda e: code_of(8, e), 0, (1,), 0.7, -1, "up"
             )
             + group_ops(
-                c, at.group_bits, 4, PIECE, lambda e: code_of(16, e), 1, (0,), 0.7, name="down"
+                c, at.group_bits, 4, PIECE, lambda e: code_of(16, e), 1, (0,), 0.7, -1, "down"
             )
         )
 
     actions = {0: ring.relay, 1: functools.partial(line.pass_on, final), 2: work, 3: share}
-    actions[4] = back
+    actions[4], actions[5] = back, weight_work
     for i in range(-(-up_sum.events() // each)):
         actions[8 + i] = functools.partial(up_event, i * each)
     for i in range(-(-down_sum.events() // each)):
@@ -1492,12 +1522,6 @@
     Plan(at, seqs, ops_of).run(actions, beside)
     sums_all[...] = small.rows[small.phases]
     up_bias_grad[...] = small_bias.rows[small_bias.phases]
-    for j in range(width // 512):
-        cols = pl.ds(j * 512, 512)
-        total = 0.0
-        for s in range(seqs):
-            total += lax.dot_general(mixed[s], buf[s, :, cols], TN, preferred_element_type=f32)
-        weight_grad[:, cols] = total.astype(bf16)
     ring.finish()
     line.finish()
     small.finish()

time: 566 us -> 545 us (0.963)
  Pallas kernels: 540 us -> 519 us
    pallas_call x1, Pallas kernels: 106 us -> 96.2 us  [heads_scatter(): pl.pallas_call(functools.partial(heads_scatter_kernel, n), out_shape=(jax...]
    pallas_call x1, Pallas kernels: 134 us -> 126 us  [attn_grad(): pl.pallas_call(functools.partial(attn_grad_kernel, n), out_shape=(jax.Sha...]
where the time goes in v8:
time: 545 us; the launch traced here: 541 us
  Pallas kernels  519 us (95%)
  other arithmetic  15.8 us (3%)
  local copies, waits for them, and re-layouts  6.06 us (1%)
    pallas_call x1, Pallas kernels, attention_block(): pl.pallas_call(functools.partial(attention_block_kernel, n), out_shape=(j...  175 us
    pallas_call x1, Pallas kernels, attn_grad(): pl.pallas_call(functools.partial(attn_grad_kernel, n), out_shape=(jax.Sha...  126 us
    pallas_call x1, Pallas kernels, mlp_block(): pl.pallas_call(functools.partial(mlp_kernel, n), out_shape=(jax.ShapeDtyp...  121 us
    pallas_call x1, Pallas kernels, heads_scatter(): pl.pallas_call(functools.partial(heads_scatter_kernel, n), out_shape=(jax...  96.2 us

profile of v8, /device:TPU:0, one launch (start us, length us, event | category | flops | bytes accessed | tf_op | source)
XLA Modules:
  0.0 541.4 jit_solution(4812798088039472881)
XLA Ops:
  0.6 175.5 %attention_block.1 = (bf16[2,1024,2048]{2,1,0:T(8,128)(2,1)}, bf16[3,2,1024,256]{3,2,1,0:T(8,128)(2,1)}, bf16[2,1024,256]{2,1,0:T(8,128)(2,1)}, f32[2,128,2048]{...) custom-call(bf16[2,128,2048]{2,1,0:T(8,128)(2,1)} %tokens_hbm.1, ...), custom_call_target="tpu_custom_call" | custom-call | tf_op jit(solution)/shard_map/attention_block/pallas_call | solution.py:913
  176.1 120.6 %mlp_block.1 = (bf16[2,1024,2048]{2,1,0:T(8,128)(2,1)}, f32[2,128,2048]{2,1,0:T(8,128)}, bf16[2,128,2048]{2,1,0:T(8,128)(2,1)}, f32[4,2048]{1,0:T(4,128)}, bf16[...) custom-call(bf16[2,128,2048]{2,1,0:T(8,128)(2,1)} %get-tuple-element, ...), custom_call_target="tpu_custom_call" | custom-call | tf_op jit(solution)/shard_map/mlp_block/pallas_call | solution.py:1338
  296.7 126.4 %attn_grad.1 = (bf16[2,128,2048]{2,1,0:T(8,128)(2,1)}, bf16[3,2,1024,256]{3,2,1,0:T(8,128)(2,1)}, bf16[256,2048]{1,0:T(8,128)(2,1)}, f32[4,2048]{1,0:T(4,128)}, ...) custom-call(bf16[2,128,2048]{2,1,0:T(8,128)(2,1)} %get-tuple-element.43.grad, ...), custom_call_target="tpu_custom_call" | custom-call | tf_op jit(solution)/shard_map/attn_grad/pallas_call | solution.py:1556
  423.1 0.0 copy-start.5
  423.1 96.2 %heads_scatter.1 = (f32[2,128,2048]{2,1,0:T(8,128)}, f32[2,2048]{1,0:T(2,128)}, bf16[3,2048,256]{2,1,0:T(8,128)(2,1)}, bf16[1,256,2048]{2,1,0:T(8,128)(2,1)}, f32[2,256]{1,0:T(2,128)}) custom-call(bf16[3,2,1024,256]{3,2,1,0:T(8,128)(2,1)} %get-tuple-element.53.grads, bf16[3,2048,256]{2,1,0:T(8,128)(2,1)} %weight.5, ...), custom_call_target="tpu_custom_call" | custom-call | tf_op jit(solution)/shard_map/heads_scatter/pallas_call | solution.py:1094
  519.4 0.0 copy-start.2
  519.4 1.5 fusion.1
  520.9 0.0 copy-done.5
  520.9 0.6 fusion
  521.5 2.8 bitcast_convert_fusion.2
  524.3 0.0 copy-done.2
  524.3 0.0 copy-start.1
  524.3 3.5 convert_element_type.11
  527.8 0.5 copy-done.1
  528.2 0.0 copy-start
  528.2 4.7 bitcast_convert_fusion.1
  533.0 0.0 copy-done
  533.0 0.0 copy-start.4
  533.0 0.0 copy-start.3
  533.0 4.7 bitcast_convert_fusion
  537.7 0.0 copy-done.4
  537.7 0.0 copy-start.7
  537.7 0.0 copy-start.6
  537.7 1.0 copy.33
  538.7 0.0 copy-done.3
  538.7 1.3 copy.34
  540.0 0.0 copy-done.7
  540.0 0.6 copy.35
  540.6 0.0 copy-done.6
  540.6 0.6 copy.36
Async XLA Ops:
  423.1 97.8 %copy-start.5 = (f32[4,2048]{1,0:T(4,128)S(1)}, f32[4,2048]{1,0:T(4,128)}, u32[]{:S(2)}) copy-start(f32[4,2048]{1,0:T(4,128)} %get-tuple-element.62) | copy-start | bytes 98308
  519.4 4.9 copy-start.2
  524.3 3.9 copy-start.1
  528.2 4.7 copy-start
  533.0 4.8 copy-start.4
  533.0 5.7 %copy-start.3 = (f32[2,128,2048]{2,1,0:T(8,128)S(1)}, f32[2,128,2048]{2,1,0:T(8,128)}, u32[]{:S(2)}) copy-start(f32[2,128,2048]{2,1,0:T(8,128)} %get-tuple-element.87) | copy-start | bytes 6291460
  537.7 2.3 copy-start.7
  537.7 2.9 copy-start.6

commit v9 on v8

--- a/solution.py
+++ b/solution.py
@@ -1,5 +1,6 @@
 import functools
 import heapq
+import itertools
 
 import jax
 import jax.numpy as jnp
@@ -73,49 +74,57 @@
 PIECE = 12.0
 
 
-def gather_ops(c, chips, seqs, kind, name, rank=0, time=0.5, gate=False, own=None):
+PART = 40
+
+
+def gather_ops(c, chips, seqs, kind, name, rank=0, time=0.5, gate=False, own=None, parts=1):
     ops = []
-    for s in range(seqs):
-        for o in range(chips):
-            up, down = [], []
-            if o <= c < chips - 1:
-                up.append((c + 1, c + 1, (name, c + 1, s, o), PIECE))
-            if o >= c > 0:
-                down.append((c - 1, c - 1, (name, c - 1, s, o), PIECE))
-            both = [(3.0, (name, c, s, o, "both"))]
-            if own is not None and o == c and s > 0:
-                ops.append(((rank, s, -1), (own[0], s, o), [], time, [], both))
-                for sends, which, others in ((up, own[1], range(c)), (down, own[2], range(c + 1, chips))):
-                    needs = [(name, c, t, other) for t in (s - 1, s) for other in others]
-                    if sends:
-                        ops.append(((rank, s, chips), (which, s, o), needs, time, sends, []))
-                continue
-            needs = [] if o == c else [(name, c, s, o)]
-            if gate and o == c and s > 0:
-                for other in range(chips):
-                    if other < c < chips - 1 or other > c > 0:
-                        needs.append((name, c, s - 1, other))
-            ops.append(((rank, s, abs(o - c)), (kind, s, o), needs, time, up + down, both))
+    for s, o, j in itertools.product(range(seqs), range(chips), range(parts)):
+        up, down = [], []
+        if o <= c < chips - 1:
+            up.append((c + 1, c + 1, (name, c + 1, s, o, j), PIECE / parts))
+        if o >= c > 0:
+            down.append((c - 1, c - 1, (name, c - 1, s, o, j), PIECE / parts))
+        both = [(3.0, (name, c, s, o, "both", j))]
+        add = j * PART
+        if own is not None and o == c and s > 0:
+            ops.append(((rank, s, -1, j), (own[0] + add, s, o), [], time, [], both))
+            for sends, which, others in ((up, own[1], range(c)), (down, own[2], range(c + 1, chips))):
+                needs = [(name, c, t, q, parts - 1) for t in (s - 1, s) for q in others]
+                if sends:
+                    code = (which + add, s, o)
+                    ops.append(((rank, s, chips, j), code, needs, time, sends, []))
+            continue
+        needs = [] if o == c else [(name, c, s, o, j)]
+        if gate and o == c and s > 0:
+            for q in range(chips):
+                if q < c < chips - 1 or q > c > 0:
+                    needs.append((name, c, s - 1, q, parts - 1))
+        ops.append(((rank, s, abs(o - c), j), (kind + add, s, o), needs, time, up + down, both))
     return ops
 
 
-def scatter_ops(c, chips, seqs, kind, name, part, rank=1, time=1.3, last=2.0):
+def gathered_here(name, c, s, o, parts=1):
+    return [(name, c, s, o, "both", j) for j in range(parts)]
+
+
+def scatter_ops(c, chips, seqs, kind, name, part, rank=1, time=1.3, last=2.0, parts=1):
     ops = []
-    for s in range(seqs):
-        for o in range(chips):
-            needs = [(part, c, s, o)]
-            if o >= c > 0:
-                needs.append((name, c, s, o, "below"))
-            if o <= c < chips - 1:
-                needs.append((name, c, s, o, "above"))
-            sends = []
-            if o > c:
-                sends = [(c + 1, c + 1, (name, c + 1, s, o, "below"), PIECE)]
-            if o < c:
-                sends = [(c - 1, c - 1, (name, c - 1, s, o, "above"), PIECE)]
-            order = (rank, s, -abs(o - c)) if o != c else (8, s, 0)
-            ends = [(0.0, (name, c, s, "sum"))] if o == c else []
-            ops.append((order, (kind, s, o), needs, last if o == c else time, sends, ends))
+    for s, o, j in itertools.product(range(seqs), range(chips), range(parts)):
+        needs = [(part, c, s, o)]
+        if o >= c > 0:
+            needs.append((name, c, s, o, "below", j))
+        if o <= c < chips - 1:
+            needs.append((name, c, s, o, "above", j))
+        sends = []
+        if o > c:
+            sends = [(c + 1, c + 1, (name, c + 1, s, o, "below", j), PIECE / parts)]
+        if o < c:
+            sends = [(c - 1, c - 1, (name, c - 1, s, o, "above", j), PIECE / parts)]
+        order = (rank, s, -abs(o - c), j) if o != c else (8, s, j)
+        ends = [(0.0, (name, c, s, "sum", j))] if o == c else []
+        span = (last if o == c else time) / parts + 0.2 * (parts - 1)
+        ops.append((order, (kind + j * PART, s, o), needs, span, sends, ends))
     return ops
 
 
@@ -260,64 +269,57 @@
 class Gather:
     def __init__(self, at, rows, buf, send, recv):
         self.at, self.rows, self.buf, self.send, self.recv = at, rows, buf, send, recv
-        self.seqs = buf.shape[0]
+        self.seqs, self.parts = buf.shape[0], recv.shape[2]
 
     @staticmethod
-    def scratch(n, seqs):
-        return [DMA((3, seqs, n // 2)), DMA((seqs, n))]
-
-    def piece(self, s, o, k):
-        return self.buf.at[s, rows_of(2 * o + k, self.rows)]
-
-    def copy(self, s, o, kind):
+    def scratch(n, seqs, parts=1):
+        return [DMA((3, seqs, n // 2, parts)), DMA((seqs, n, parts))]
+
+    def copy(self, s, o, kind, j, owner=None):
         at = self.at
         target = (at.me + 2, at.me - 2, at.side)[kind]
-        piece = self.piece(s, o, at.core)
+        owner = 2 * o + at.core if owner is None else owner
+        piece = self.buf.at[s, rows_of(owner * self.parts + j, self.rows // self.parts)]
         return pltpu.make_async_remote_copy(
             src_ref=piece,
             dst_ref=piece,
-            send_sem=self.send.at[kind, s, o],
-            recv_sem=self.recv.at[s, 2 * o + at.core],
+            send_sem=self.send.at[kind, s, o, j],
+            recv_sem=self.recv.at[s, owner, j],
             device_id={"tensor": target},
             device_id_type=MESH,
         )
 
-    def arrived(self, s, o, k):
+    def arrived(self, s, o):
+        for j in range(self.parts):
+            self.copy(s, o, SIDE, j, 2 * o + 1 - self.at.core).wait_recv()
+
+    def relay(self, j, s, o):
         at = self.at
-        piece = self.piece(s, o, k)
-        pltpu.make_async_remote_copy(
-            src_ref=piece,
-            dst_ref=piece,
-            send_sem=self.send.at[SIDE, s, o],
-            recv_sem=self.recv.at[s, 2 * o + k],
-            device_id={"tensor": at.side},
-            device_id_type=MESH,
-        ).wait_recv()
-
-    def relay(self, s, o):
-        at = self.at
-        pl.when(o != at.chip)(lambda: self.arrived(s, o, at.core))
-        pl.when((o <= at.chip) & at.above)(lambda: self.copy(s, o, UP).start())
-        pl.when((o >= at.chip) & at.below)(lambda: self.copy(s, o, DOWN).start())
-        self.copy(s, o, SIDE).start()
-
-    def own(self, kind, s, o):
-        self.copy(s, o, kind).start()
-
-    def owns(self, kinds):
-        return {
-            which: functools.partial(self.own, kind)
-            for which, kind in zip(kinds, (SIDE, UP, DOWN))
-        }
+        pl.when(o != at.chip)(lambda: self.copy(s, o, SIDE, j).wait_recv())
+        pl.when((o <= at.chip) & at.above)(lambda: self.copy(s, o, UP, j).start())
+        pl.when((o >= at.chip) & at.below)(lambda: self.copy(s, o, DOWN, j).start())
+        self.copy(s, o, SIDE, j).start()
+
+    def own(self, kind, j, s, o):
+        self.copy(s, o, kind, j).start()
+
+    def actions(self, kind, own=()):
+        found = {}
+        for j in range(self.parts):
+            found[kind + j * PART] = functools.partial(self.relay, j)
+            for which, way in zip(own, (SIDE, UP, DOWN)):
+                found[which + j * PART] = functools.partial(self.own, way, j)
+        return found
 
     def finish(self):
         at = self.at
 
         def one(i, carry):
             s, o = i // at.chips, lax.rem(i, at.chips)
-            pl.when((o <= at.chip) & at.above)(lambda: self.copy(s, o, UP).wait_send())
-            pl.when((o >= at.chip) & at.below)(lambda: self.copy(s, o, DOWN).wait_send())
-            self.copy(s, o, SIDE).wait_send()
+            for j in range(self.parts):
+                pl.when((o <= at.chip) & at.above)(lambda: self.copy(s, o, UP, j).wait_send())
+                pl.when((o >= at.chip) & at.below)(lambda: self.copy(s, o, DOWN, j).wait_send())
+                self.copy(s, o, SIDE, j).wait_send()
             return carry
 
         lax.fori_loop(0, self.seqs * at.chips, one, 0)
@@ -328,92 +330,93 @@
         self.at, self.rows = at, rows
         self.part, self.side, self.link = part, side, link
         self.side_send, self.side_recv, self.send, self.recv = side_send, side_recv, send, recv
-        self.seqs = part.shape[0]
+        self.seqs, self.parts = part.shape[0], recv.shape[2]
+        self.size = rows // self.parts
 
     @staticmethod
-    def scratch(n, seqs, rows, width):
+    def scratch(n, seqs, rows, width, parts=1):
         chips = n // 2
         return [
             VMEM((seqs, chips, 2 * rows, width), bf16),
             VMEM((seqs, chips, rows, width), bf16),
             VMEM((seqs, chips + 1, rows, width), bf16),
-            DMA((seqs, chips)),
-            DMA((seqs, chips)),
-            DMA((seqs, chips)),
-            DMA((seqs, chips + 1)),
+            DMA((seqs, chips, parts)),
+            DMA((seqs, chips, parts)),
+            DMA((seqs, chips, parts)),
+            DMA((seqs, chips + 1, parts)),
         ]
 
-    def side_copy(self, s, o):
+    def side_copy(self, s, o, j):
         at = self.at
         return pltpu.make_async_remote_copy(
-            src_ref=self.part.at[s, o, rows_of(1 - at.core, self.rows)],
-            dst_ref=self.side.at[s, o],
-            send_sem=self.side_send.at[s, o],
-            recv_sem=self.side_recv.at[s, o],
+            src_ref=self.part.at[s, o, rows_of((1 - at.core) * self.parts + j, self.size)],
+            dst_ref=self.side.at[s, o, pl.ds(j * self.size, self.size)],
+            send_sem=self.side_send.at[s, o, j],
+            recv_sem=self.side_recv.at[s, o, j],
             device_id={"tensor": at.side},
             device_id_type=MESH,
         )
 
-    def link_copy(self, s, o, slot, target):
+    def link_copy(self, s, o, slot, target, j):
         return pltpu.make_async_remote_copy(
-            src_ref=self.part.at[s, o, rows_of(self.at.core, self.rows)],
-            dst_ref=self.link.at[s, slot],
-            send_sem=self.send.at[s, o],
-            recv_sem=self.recv.at[s, slot],
+            src_ref=self.part.at[s, o, rows_of(self.at.core * self.parts + j, self.size)],
+            dst_ref=self.link.at[s, slot, pl.ds(j * self.size, self.size)],
+            send_sem=self.send.at[s, o, j],
+            recv_sem=self.recv.at[s, slot, j],
             device_id={"tensor": target},
             device_id_type=MESH,
         )
 
     def share(self, s, o):
-        self.side_copy(s, o).start()
-
-    def blocks(self, body):
+        for j in range(self.parts):
+            self.side_copy(s, o, j).start()
+
+    def blocks(self, j, body):
         step = 16
-        lax.fori_loop(0, self.rows // step, lambda i, c: (body(pl.multiple_of(i * step, step), step), c)[1], 0)
-
-    def add_up(self, s, o, slots):
-        base = self.at.core * self.rows
-
+
+        def one(i, carry):
+            body(pl.multiple_of(j * self.size + i * step, step), step)
+            return carry
+
+        lax.fori_loop(0, self.size // step, one, 0)
+
+    def total(self, s, o, first, step, slots):
+        here = pl.ds(pl.multiple_of(self.at.core * self.rows + first, step), step)
+        there = pl.ds(first, step)
+        total = self.part[s, o, here].astype(f32) + self.side[s, o, there].astype(f32)
+        for slot in slots:
+            total += self.link[s, slot, there].astype(f32)
+        return here, total
+
+    def add_up(self, s, o, slots, j):
         def body(first, step):
-            here = pl.ds(pl.multiple_of(base + first, step), step)
-            there = pl.ds(first, step)
-            total = self.part[s, o, here].astype(f32) + self.side[s, o, there].astype(f32)
-            for slot in slots:
-                total += self.link[s, slot, there].astype(f32)
+            here, total = self.total(s, o, first, step, slots)
             self.part[s, o, here] = total.astype(bf16)
 
-        self.blocks(body)
-
-    def pass_on(self, final, s, o):
+        self.blocks(j, body)
+
+    def pass_on(self, final, j, s, o):
         at = self.at
-        self.side_copy(s, o).wait_recv()
-
-        @pl.when(o > at.chip)
-        def _():
-            @pl.when(at.below)
+        self.side_copy(s, o, j).wait_recv()
+
+        def onward(before, slot, target):
+            @pl.when(before)
             def _():
-                self.link_copy(s, o, o, at.me).wait_recv()
-                self.add_up(s, o, [o])
-
-            pl.when(jnp.logical_not(at.below))(lambda: self.add_up(s, o, []))
-            self.link_copy(s, o, o, at.me + 2).start()
-
-        @pl.when(o < at.chip)
-        def _():
-            @pl.when(at.above)
-            def _():
-                self.link_copy(s, o, o, at.me).wait_recv()
-                self.add_up(s, o, [o])
-
-            pl.when(jnp.logical_not(at.above))(lambda: self.add_up(s, o, []))
-            slot = jnp.where(o == at.chip - 1, at.chips, o)
-            self.link_copy(s, o, slot, at.me - 2).start()
+                self.link_copy(s, o, o, at.me, j).wait_recv()
+                self.add_up(s, o, [o], j)
+
+            pl.when(jnp.logical_not(before))(lambda: self.add_up(s, o, [], j))
+            self.link_copy(s, o, slot, target, j).start()
+
+        pl.when(o > at.chip)(lambda: onward(at.below, o, at.me + 2))
+        last = jnp.where(o == at.chip - 1, at.chips, o)
+        pl.when(o < at.chip)(lambda: onward(at.above, last, at.me - 2))
 
         @pl.when(o == at.chip)
         def _():
-            pl.when(at.below)(lambda: self.link_copy(s, o, o, at.me).wait_recv())
-            pl.when(at.above)(lambda: self.link_copy(s, o, at.chips, at.me).wait_recv())
             for slot, used in ((o, at.below), (at.chips, at.above)):
+                pl.when(used)(lambda: self.link_copy(s, o, slot, at.me, j).wait_recv())
+
                 @pl.when(jnp.logical_not(used))
                 def _():
                     def clear(first, step):
@@ -421,26 +424,27 @@
                             (step, self.link.shape[-1]), bf16
                         )
 
-                    self.blocks(clear)
-            base = at.core * self.rows
+                    self.blocks(j, clear)
 
             def body(first, step):
-                here = pl.ds(pl.multiple_of(base + first, step), step)
-                there = pl.ds(first, step)
-                total = self.part[s, o, here].astype(f32) + self.side[s, o, there].astype(f32)
-                total += self.link[s, o, there].astype(f32)
-                total += self.link[s, at.chips, there].astype(f32)
-                final(s, there, total)
-
-            self.blocks(body)
+                total = self.total(s, o, first, step, [o, at.chips])[1]
+                final(s, pl.ds(first, step), total)
+
+            self.blocks(j, body)
+
+    def actions(self, kind, final):
+        return {
+            kind + j * PART: functools.partial(self.pass_on, final, j) for j in range(self.parts)
+        }
 
     def finish(self):
         at = self.at
 
         def one(i, carry):
             s, o = i // at.chips, lax.rem(i, at.chips)
-            self.side_copy(s, o).wait_send()
-            pl.when(o != at.chip)(lambda: self.link_copy(s, o, o, at.side).wait_send())
+            for j in range(self.parts):
+                self.side_copy(s, o, j).wait_send()
+                pl.when(o != at.chip)(lambda: self.link_copy(s, o, o, at.side, j).wait_send())
             return carry
 
         lax.fori_loop(0, self.seqs * at.chips, one, 0)
@@ -818,7 +822,7 @@
         return pltpu.make_async_copy(buf.at[s, here], gathered.at[s, here], keep_sem.at[s, o])
 
     def project(s, o):
-        ring.arrived(s, o, 1 - at.core)
+        ring.arrived(s, o)
         keep(s, o).start()
         here = rows_of(o, 2 * rows)
         for j in range(3):
@@ -854,7 +858,7 @@
         return (
             gather_ops(c, chips, seqs, 0, "in", gate=True)
             + work_ops(
-                c, chips, seqs, 1, lambda s, o: [("in", c, s, o, "both")], "heads", 1.0
+                c, chips, seqs, 1, lambda s, o: gathered_here("in", c, s, o), "heads", 1.0
             )
             + mixing
             + work_ops(
@@ -866,12 +870,12 @@
 
     Plan(at, seqs, ops_of).run(
         {
-            0: ring.relay,
             1: project,
             2: mix,
             3: project_out,
-            4: functools.partial(line.pass_on, final),
-            5: grad_ring.relay,
+            **ring.actions(0),
+            **line.actions(4, final),
+            **grad_ring.actions(5),
         }
     )
     ring.finish()
@@ -880,7 +884,7 @@
 
     def close(i, carry):
         s, o = i // at.chips, lax.rem(i, at.chips)
-        grad_ring.arrived(s, o, 1 - at.core)
+        grad_ring.arrived(s, o)
         keep(s, o).wait()
         return carry
 
@@ -1049,13 +1053,13 @@
 
     def ops_of(c):
         chips = at.chips
-        finals = scatter_ops(c, chips, seqs, 1, "out", "part", last=4.0)
+        finals = scatter_ops(c, chips, seqs, 1, "out", "part", last=4.0, parts=line.parts)
         loaded = ("qkv", c, 0, 0, 1)
         for i, (rank, code, needs, time, sends, gives) in enumerate(finals):
             if code[2] == c:
                 finals[i] = (rank, code, needs + [loaded], time, sends, gives)
         smalls = []
-        needs = [("out", c, s, "sum") for s in range(seqs)]
+        needs = [("out", c, s, "sum", j) for s in range(seqs) for j in range(line.parts)]
         for e in range(3):
             smalls.append(((0, e), (30 + e, 0, 0), needs, 0.5, [], [(4.0, ("small", c, e))]))
             needs = [("small", c, e)]
@@ -1070,7 +1074,7 @@
             )
         )
 
-    actions = {0: work, 1: functools.partial(line.pass_on, final), 5: out_event}
+    actions = {0: work, 5: out_event, **line.actions(1, final)}
     for i in range(3):
         actions[2 + i] = functools.partial(weight_event, i * each)
         actions[30 + i] = lambda s, o, e=i: small.event(e)
@@ -1102,7 +1106,7 @@
         ),
         in_specs=[vmem, vmem, hbm, vmem, hbm, vmem, hbm],
         out_specs=(vmem, vmem, hbm, hbm, vmem),
-        scratch_shapes=Scatter.scratch(n, seqs, rows, width)
+        scratch_shapes=Scatter.scratch(n, seqs, rows, width, 2)
         + GroupSum.scratch(dp, 3, width, part)
         + GroupSum.scratch(dp, 1, part, width)
         + DirectSum.scratch(dp, n, 2, width)
@@ -1198,7 +1202,7 @@
         )
 
     def work(s, o):
-        ring.arrived(s, o, 1 - at.core)
+        ring.arrived(s, o)
 
         @pl.when((s == 0) & (o == at.chip))
         def _():
@@ -1297,10 +1301,10 @@
         chips = at.chips
         units = [(s, o) for s in range(seqs) for o in range(chips)]
         ops = (
-            gather_ops(c, chips, seqs, 0, "in", own=own)
+            gather_ops(c, chips, seqs, 0, "in", own=own, parts=ring.parts)
             + scatter_ops(c, chips, seqs, 1, "back", "part", last=4.0)
             + work_ops(
-                c, chips, seqs, 2, lambda s, o: [("in", c, s, o, "both")], "part", 5.7
+                c, chips, seqs, 2, lambda s, o: gathered_here("in", c, s, o, ring.parts), "part", 5.7
             )
         )
         for i in range(len(ops)):
@@ -1317,8 +1321,7 @@
             ops.append(((4, e, 0), code, needs, 2.7, sends, [(0.0, ("tile", c, e))]))
         return ops
 
-    actions = {0: ring.relay, 1: functools.partial(line.pass_on, final), 2: work, 3: tile_work}
-    actions.update(ring.owns(own))
+    actions = {2: work, 3: tile_work, **ring.actions(0, own), **line.actions(1, final)}
     Plan(at, seqs, ops_of).run(actions)
     tile_sent(*order[7])
     ring.finish()
@@ -1350,7 +1353,7 @@
         in_specs=[vmem, hbm, hbm, vmem, hbm, hbm, vmem],
         out_specs=(hbm, vmem, vmem, vmem, hbm, vmem, hbm, hbm),
         scratch_shapes=[VMEM((seqs, slots, width), bf16)]
-        + Gather.scratch(n, seqs)
+        + Gather.scratch(n, seqs, 2)
         + [
             VMEM((seqs, slots, width), bf16),
             VMEM(up_weight.shape, bf16),
@@ -1462,7 +1465,7 @@
         line.share(s, o)
 
     def work(s, o):
-        ring.arrived(s, o, 1 - at.core)
+        ring.arrived(s, o)
         here = rows_of(o, 2 * rows)
         grad_heads[s, here] = lax.dot_general(
             buf[s, here], weight[...], NT, preferred_element_type=f32
@@ -1498,7 +1501,7 @@
         return backs + (
             gather_ops(c, chips, seqs, 0, "in")
             + scatter_ops(c, chips, seqs, 1, "out", "part", last=4.0)
-            + work_ops(c, chips, seqs, 2, lambda s, o: [("in", c, s, o, "both")], "done", 1.0)
+            + work_ops(c, chips, seqs, 2, lambda s, o: gathered_here("in", c, s, o), "done", 1.0)
             + work_ops(c, chips, seqs, 3, lambda s, o: [], "part", 0.3, rank=0, far=True)
             + group_ops(
                 c, at.group_bits, 4, PIECE, lambda e: code_of(8, e), 0, (1,), 0.7, -1, "up"
@@ -1508,7 +1511,7 @@
             )
         )
 
-    actions = {0: ring.relay, 1: functools.partial(line.pass_on, final), 2: work, 3: share}
+    actions = {2: work, 3: share, **ring.actions(0), **line.actions(1, final)}
     actions[4], actions[5] = back, weight_work
     for i in range(-(-up_sum.events() // each)):
         actions[8 + i] = functools.partial(up_event, i * each)
@@ -1599,6 +1602,34 @@
     )
 
 
+def finish_kernel(*refs):
+    sums_two, sums_one = refs[8:10]
+    targets = refs[10:]
+    for source, target in zip(refs[:8], targets):
+        target[...] = source[...].astype(target.dtype)
+    rows = [sums_one[i : i + 1] for i in range(2)] + [sums_two[i : i + 1] for i in range(4)]
+    for row, target in zip(rows, targets[8:]):
+        target[...] = row
+
+
+def finish(blocks, wholes, sums_two, sums_one, steps=4):
+    width = sums_one.shape[1]
+    specs = [pl.BlockSpec((a.shape[0] // steps, a.shape[1]), lambda i: (i, 0)) for a, t in blocks]
+    specs += [pl.BlockSpec(a.shape, lambda i: (0, 0)) for a in wholes]
+    row = pl.BlockSpec((1, width), lambda i: (0, 0))
+    shapes = [jax.ShapeDtypeStruct(a.shape, t) for a, t in blocks]
+    shapes += [jax.ShapeDtypeStruct(a.shape, f32) for a in wholes]
+    return pl.pallas_call(
+        finish_kernel,
+        grid=(steps,),
+        out_shape=shapes + [jax.ShapeDtypeStruct((1, width), f32)] * 6,
+        in_specs=specs + [pl.BlockSpec(a.shape, lambda i: (0, 0)) for a in (sums_two, sums_one)],
+        out_specs=specs + [row] * 6,
+        compiler_params=pltpu.CompilerParams(vmem_limit_bytes=62 * 2**20),
+        name="finish",
+    )(*[a for a, t in blocks], *wholes, sums_two, sums_one)
+
+
 def body(
     tokens,
     cotangent,
@@ -1659,20 +1690,44 @@
         lengths,
         heads,
     )
-    ln2_gain_grad, ln2_shift_grad, out_bias_grad, down_bias_grad = [sums[i] for i in range(4)]
     input_grad, sums_one, qkv_weight_grad, out_weight_grad, qkv_bias_grad = heads_scatter(
         n, grads, qkv_weight, gathered_one, out_part, tokens, ln1_gain[None], hidden_grad
     )
-    up_weight_grad = up_weight_grad.astype(jnp.float32).reshape(up_weight.shape)
-    down_weight_grad = down_weight_grad.astype(jnp.float32).reshape(down_weight.shape)
-    return (
+    width = tokens.shape[2]
+    (
+        qkv_weight_grad,
+        out_weight_grad,
+        up_weight_grad,
+        down_weight_grad,
         output,
         input_grad,
-        sums_one[0],
-        sums_one[1],
-        qkv_weight_grad.astype(jnp.float32),
         qkv_bias_grad,
-        out_weight_grad[0].astype(jnp.float32),
+        up_bias_grad,
+        *rows,
+    ) = finish(
+        (
+            (qkv_weight_grad.reshape(-1, qkv_weight.shape[2]), f32),
+            (out_weight_grad.reshape(out_weight.shape), f32),
+            (up_weight_grad.reshape(up_weight.shape), f32),
+            (down_weight_grad.reshape(down_weight.shape), f32),
+            (output.reshape(-1, width), bf16),
+            (input_grad.reshape(-1, width), f32),
+        ),
+        (qkv_bias_grad, up_bias_grad),
+        sums,
+        sums_one,
+    )
+    ln1_gain_grad, ln1_shift_grad, ln2_gain_grad, ln2_shift_grad, out_bias_grad, down_bias_grad = [
+        row[0] for row in rows
+    ]
+    return (
+        output.reshape(tokens.shape),
+        input_grad.reshape(tokens.shape),
+        ln1_gain_grad,
+        ln1_shift_grad,
+        qkv_weight_grad.reshape(qkv_weight.shape),
+        qkv_bias_grad,
+        out_weight_grad,
         out_bias_grad,
         ln2_gain_grad,
         ln2_shift_grad,

time: 545 us -> 536 us (0.983)
  other arithmetic: 15.8 us -> 0 us
  Pallas kernels: 519 us -> 531 us
  local copies, waits for them, and re-layouts: 6.06 us -> 0 us
    pallas_call x0 -> x1, Pallas kernels: none -> 15 us  [finish(): pl.pallas_call(finish_kernel, grid=(steps,), out_shape=shapes + [jax.Shap...]
    reshape x2 -> x0, other arithmetic: 9.48 us -> none  [the longest x1 4.75 us: body(): down_weight_grad.astype(jnp.float32).reshape(down_weight.shape)]
    convert_element_type x2 -> x0, other arithmetic: 6.28 us -> none  [the longest x1 3.49 us: body(): qkv_weight_grad.astype(jnp.float32)]
where the time goes in v9:
time: 536 us; the launch traced here: 532 us
  Pallas kernels  531 us (99%)
    pallas_call x1, Pallas kernels, attention_block(): pl.pallas_call(functools.partial(attention_block_kernel, n), out_shape=(j...  175 us
    pallas_call x1, Pallas kernels, attn_grad(): pl.pallas_call(functools.partial(attn_grad_kernel, n), out_shape=(jax.Sha...  127 us
    pallas_call x1, Pallas kernels, mlp_block(): pl.pallas_call(functools.partial(mlp_kernel, n), out_shape=(jax.ShapeDtyp...  116 us
    pallas_call x1, Pallas kernels, heads_scatter(): pl.pallas_call(functools.partial(heads_scatter_kernel, n), out_shape=(jax...  97.8 us
    pallas_call x1, Pallas kernels, finish(): pl.pallas_call(finish_kernel, grid=(steps,), out_shape=shapes + [jax.Shap...  15 us

profile of v9, /device:TPU:0, one launch (start us, length us, event | category | flops | bytes accessed | tf_op | source)
XLA Modules:
  0.0 532.1 jit_solution(6840471583850988835)
XLA Ops:
  0.6 175.3 %attention_block.1 = (bf16[2,1024,2048]{2,1,0:T(8,128)(2,1)}, bf16[3,2,1024,256]{3,2,1,0:T(8,128)(2,1)}, bf16[2,1024,256]{2,1,0:T(8,128)(2,1)}, f32[2,128,2048]{...) custom-call(bf16[2,128,2048]{2,1,0:T(8,128)(2,1)} %tokens_hbm.1, ...), custom_call_target="tpu_custom_call" | custom-call | tf_op jit(solution)/shard_map/attention_block/pallas_call | solution.py:917
  176.0 116.4 %mlp_block.1 = (bf16[2,1024,2048]{2,1,0:T(8,128)(2,1)}, f32[2,128,2048]{2,1,0:T(8,128)}, bf16[2,128,2048]{2,1,0:T(8,128)(2,1)}, f32[4,2048]{1,0:T(4,128)}, bf16[...) custom-call(bf16[2,128,2048]{2,1,0:T(8,128)(2,1)} %get-tuple-element, ...), custom_call_target="tpu_custom_call" | custom-call | tf_op jit(solution)/shard_map/mlp_block/pallas_call | solution.py:1341
  292.4 126.7 %attn_grad.1 = (bf16[2,128,2048]{2,1,0:T(8,128)(2,1)}, bf16[3,2,1024,256]{3,2,1,0:T(8,128)(2,1)}, bf16[256,2048]{1,0:T(8,128)(2,1)}, f32[4,2048]{1,0:T(4,128)}, ...) custom-call(bf16[2,128,2048]{2,1,0:T(8,128)(2,1)} %get-tuple-element.57.grad, ...), custom_call_target="tpu_custom_call" | custom-call | tf_op jit(solution)/shard_map/attn_grad/pallas_call | solution.py:1559
  419.1 97.8 %heads_scatter.1 = (f32[2,128,2048]{2,1,0:T(8,128)}, f32[2,2048]{1,0:T(2,128)}, bf16[3,2048,256]{2,1,0:T(8,128)(2,1)}, bf16[1,256,2048]{2,1,0:T(8,128)(2,1)}, f32[2,256]{1,0:T(2,128)}) custom-call(bf16[3,2,1024,256]{3,2,1,0:T(8,128)(2,1)} %get-tuple-element.66.grads, bf16[3,2048,256]{2,1,0:T(8,128)(2,1)} %weight.5, ...), custom_call_target="tpu_custom_call" | custom-call | tf_op jit(solution)/shard_map/heads_scatter/pallas_call | solution.py:1098
  516.9 15.0 %finish.1 = (f32[6144,256]{1,0:T(8,128)}, f32[256,2048]{1,0:T(8,128)}, f32[2048,1024]{1,0:T(8,128)}, f32[1024,2048]{1,0:T(8,128)}, bf16[256,2048]{1,0:T(8,128)(2...) custom-call(bf16[6144,256]{1,0:T(8,128)(2,1)} %bitcast.25, ...), custom_call_target="tpu_custom_call" | custom-call | tf_op jit(solution)/shard_map/finish/pallas_call | solution.py:1622

commit v10 on v9

--- a/solution.py
+++ b/solution.py
@@ -74,7 +74,7 @@
 PIECE = 12.0
 
 
-PART = 40
+PART = 12
 
 
 def gather_ops(c, chips, seqs, kind, name, rank=0, time=0.5, gate=False, own=None, parts=1):
@@ -774,11 +774,14 @@
     gain_two,
     shift_two,
     gathered,
-    heads,
-    mixed,
+    heads_hbm,
+    mixed_hbm,
     hidden,
     normed,
     grad_all,
+    heads,
+    mixed,
+    result_sem,
     buf,
     send,
     recv,
@@ -838,8 +841,18 @@
         hidden[s, there] = values
         normed[s, there] = norm_rows(values, gain_two[...], shift_two[...]).astype(bf16)
 
+    def results(s):
+        pairs = [(heads.at[j, s], heads_hbm.at[j, s]) for j in range(3)]
+        pairs.append((mixed.at[s], mixed_hbm.at[s]))
+        return [
+            pltpu.make_async_copy(source, target, result_sem.at[s, j])
+            for j, (source, target) in enumerate(pairs)
+        ]
+
     def mix(s, o):
         attend(heads, lengths, mixed, min(512, n * rows), s)
+        for copy in results(s):
+            copy.start()
 
     def project_out(s, o):
         here = rows_of(o, 2 * rows)
@@ -881,6 +894,10 @@
     ring.finish()
     line.finish()
     grad_ring.finish()
+
+    for s in range(seqs):
+        for copy in results(s):
+            copy.wait()
 
     def close(i, carry):
         s, o = i // at.chips, lax.rem(i, at.chips)
@@ -925,8 +942,13 @@
             jax.ShapeDtypeStruct((seqs, n * rows, width), bf16),
         ),
         in_specs=[vmem, vmem, smem] + [vmem] * 8,
-        out_specs=(hbm, vmem, vmem, vmem, vmem, hbm),
-        scratch_shapes=[VMEM((seqs, n * rows, width), bf16)]
+        out_specs=(hbm, hbm, hbm, vmem, vmem, hbm),
+        scratch_shapes=[
+            VMEM((3, seqs, n * rows, part), bf16),
+            VMEM((seqs, n * rows, part), bf16),
+            DMA((seqs, 4)),
+            VMEM((seqs, n * rows, width), bf16),
+        ]
         + Gather.scratch(n, seqs)
         + [DMA((seqs, n // 2))]
         + Gather.scratch(n, seqs)
@@ -960,11 +982,13 @@
     tokens_hbm,
     gain,
     hidden_hbm,
+    up_part,
     grad,
     sums_all,
     weight_grad,
     out_grad,
     bias_grad,
+    up_grad,
     *scratch,
 ):
     at = Place(n)
@@ -974,7 +998,10 @@
     out_sum = GroupSum(at, out_part.shape[0], *scratch[12:17], out_grad, turn=1)
     small = DirectSum(at, *scratch[17:22])
     small_bias = SmallSum(at, *scratch[22:26], False)
-    gathered, tokens, hidden_grad, in_sem = scratch[26:]
+    gathered, tokens, hidden_grad, in_sem = scratch[26:30]
+    up_sum = GroupSum(at, up_part.shape[1], *scratch[30:35], up_grad, turn=1)
+    up_load = pltpu.make_async_copy(up_part.at[3], up_sum.tiles.at[0], in_sem.at[3])
+    up_load.start()
     sources = ((gathered_hbm, gathered), (tokens_hbm, tokens), (hidden_hbm, hidden_grad))
     loads = [
         pltpu.make_async_copy(source, target, in_sem.at[i])
@@ -1047,6 +1074,9 @@
 
     def out_event(s, o):
         out_sum.event(s * at.chips + o)
+
+    def up_event(first, s, o):
+        up_sum.event(first + s * at.chips + o, lambda t: up_load.wait())
 
     def code_of(kind, e):
         return (kind + e // each, e % each // at.chips, e % at.chips)
@@ -1067,14 +1097,19 @@
             work_ops(c, chips, seqs, 0, lambda s, o: [], "part", 1.5, far=True)
             + finals
             + group_ops(
-                c, at.group_bits, 3, PIECE, lambda e: code_of(2, e), 0, (0,), 2.7, name="qkv"
+                c, at.group_bits, 3, PIECE, lambda e: code_of(2, e), 0, (0,), 2.7, -1, "qkv"
             )
             + group_ops(
-                c, at.group_bits, 1, PIECE, lambda e: code_of(5, e), 0, (1,), 0.7, name="out_sum"
+                c, at.group_bits, 1, PIECE, lambda e: code_of(5, e), 0, (1,), 0.7, -1, "out_sum"
+            )
+            + group_ops(
+                c, at.group_bits, 1, PIECE, lambda e: code_of(20, e), 0, (1,), 0.7, -2, "up"
             )
         )
 
     actions = {0: work, 5: out_event, **line.actions(1, final)}
+    for i in range(-(-up_sum.events() // each)):
+        actions[20 + i] = functools.partial(up_event, i * each)
     for i in range(3):
         actions[2 + i] = functools.partial(weight_event, i * each)
         actions[30 + i] = lambda s, o, e=i: small.event(e)
@@ -1085,10 +1120,11 @@
     line.finish()
     weight_sum.finish()
     out_sum.finish()
+    up_sum.finish()
     small_bias.finish()
 
 
-def heads_scatter(n, grads, weight, gathered, out_part, tokens, gain, hidden_grad):
+def heads_scatter(n, grads, weight, gathered, out_part, tokens, gain, hidden_grad, up_part):
     seqs, slots, part = grads.shape[1:]
     width = weight.shape[1]
     rows = slots // n
@@ -1103,9 +1139,10 @@
             jax.ShapeDtypeStruct((3, width, part), bf16),
             jax.ShapeDtypeStruct((1, part, width), bf16),
             jax.ShapeDtypeStruct((2, part), f32),
+            jax.ShapeDtypeStruct((1,) + up_part.shape[1:], bf16),
         ),
-        in_specs=[vmem, vmem, hbm, vmem, hbm, vmem, hbm],
-        out_specs=(vmem, vmem, hbm, hbm, vmem),
+        in_specs=[vmem, vmem, hbm, vmem, hbm, vmem, hbm, hbm],
+        out_specs=(vmem, vmem, hbm, hbm, vmem, hbm),
         scratch_shapes=Scatter.scratch(n, seqs, rows, width, 2)
         + GroupSum.scratch(dp, 3, width, part)
         + GroupSum.scratch(dp, 1, part, width)
@@ -1115,13 +1152,14 @@
             VMEM(gathered.shape, bf16),
             VMEM(tokens.shape, bf16),
             VMEM(hidden_grad.shape, f32),
-            DMA((3,)),
-        ],
+            DMA((4,)),
+        ]
+        + GroupSum.scratch(dp, 1, *up_part.shape[1:]),
         compiler_params=pltpu.CompilerParams(
             collective_id=2, has_side_effects=True, vmem_limit_bytes=62 * 2**20
         ),
         name="heads_scatter",
-    )(grads, weight, gathered, out_part, tokens, gain, hidden_grad)
+    )(grads, weight, gathered, out_part, tokens, gain, hidden_grad, up_part)
 
 
 def normal_cdf(values):
@@ -1229,6 +1267,9 @@
                 pre[s, here], up_weight[cols], NT, preferred_element_type=f32
             ).astype(bf16)
         line.share(s, o)
+
+    def work_down(s, o):
+        here = rows_of(o, 2 * rows)
         pl.when((s > 0) | (o != at.chip))(lambda: out_copy(s, o).wait())
         for j in range(width // 512):
             cols = pl.ds(j * 512, 512)
@@ -1300,19 +1341,21 @@
     def ops_of(c):
         chips = at.chips
         units = [(s, o) for s in range(seqs) for o in range(chips)]
-        ops = (
-            gather_ops(c, chips, seqs, 0, "in", own=own, parts=ring.parts)
-            + scatter_ops(c, chips, seqs, 1, "back", "part", last=4.0)
-            + work_ops(
-                c, chips, seqs, 2, lambda s, o: gathered_here("in", c, s, o, ring.parts), "part", 5.7
-            )
-        )
-        for i in range(len(ops)):
-            rank, code, needs, time, sends, gives = ops[i]
-            if code[0] == 2 and code[1:] != (0, c):
-                ops[i] = (rank, code, needs + [("first", c)], time, sends, gives)
-            if code == (2, 0, c):
-                ops[i] = (rank, code, needs, time, sends, gives + [(0.0, ("first", c))])
+        ops = gather_ops(c, chips, seqs, 0, "in", own=own, parts=ring.parts)
+        ops += scatter_ops(c, chips, seqs, 1, "back", "part", last=4.0)
+        for s, o in units:
+            needs = gathered_here("in", c, s, o, ring.parts)
+            gives = [(3.0, ("part", c, s, o)), (0.0, ("done", c, s, o))]
+            needs_down, gives_down = [("done", c, s, o)], []
+            if (s, o) == (0, c):
+                gives.append((0.0, ("first", c)))
+                gives_down.append((0.0, ("first down", c)))
+            else:
+                needs.append(("first", c))
+                needs_down.append(("first down", c))
+            rank = (s, abs(o - c))
+            ops.append(((2,) + rank, (2, s, o), needs, 4.3, [], gives))
+            ops.append(((3,) + rank, (7, s, o), needs_down, 1.4, [], gives_down))
         for e in range(len(order)):
             needs = [("part", c, s, o) for s, o in units]
             needs += [("tile", c, e - 1)] if e else []
@@ -1321,7 +1364,8 @@
             ops.append(((4, e, 0), code, needs, 2.7, sends, [(0.0, ("tile", c, e))]))
         return ops
 
-    actions = {2: work, 3: tile_work, **ring.actions(0, own), **line.actions(1, final)}
+    actions = {2: work, 3: tile_work, 7: work_down}
+    actions.update({**ring.actions(0, own), **line.actions(1, final)})
     Plan(at, seqs, ops_of).run(actions)
     tile_sent(*order[7])
     ring.finish()
@@ -1353,7 +1397,7 @@
         in_specs=[vmem, hbm, hbm, vmem, hbm, hbm, vmem],
         out_specs=(hbm, vmem, vmem, vmem, hbm, vmem, hbm, hbm),
         scratch_shapes=[VMEM((seqs, slots, width), bf16)]
-        + Gather.scratch(n, seqs, 2)
+        + Gather.scratch(n, seqs, 4)
         + [
             VMEM((seqs, slots, width), bf16),
             VMEM(up_weight.shape, bf16),
@@ -1384,17 +1428,17 @@
     n,
     grad,
     mlp_part,
-    hidden,
+    hidden_hbm,
     bias,
-    weight,
-    mixed,
+    weight_hbm,
+    mixed_hbm,
     sums,
     up_bias_part,
     up_part,
     down_part,
     down_box,
     lengths,
-    heads,
+    heads_hbm,
     output,
     grads,
     weight_grad,
@@ -1416,7 +1460,14 @@
     down_sum = GroupSum(at, down_part.shape[1], *scratch[15:20], down_grad, skip=1)
     small = SmallSum(at, *scratch[20:24], True)
     small_bias = SmallSum(at, *scratch[24:28], False)
-    grad_heads, grad_key, grad_value = scratch[28:]
+    grad_heads, grad_key, grad_value, hidden, weight, mixed, heads, in_sem = scratch[28:]
+    sources = (weight_hbm, weight), (hidden_hbm, hidden), (mixed_hbm, mixed), (heads_hbm, heads)
+    loads = [
+        pltpu.make_async_copy(source, target, in_sem.at[i])
+        for i, (source, target) in enumerate(sources)
+    ]
+    for copy in loads:
+        copy.start()
     def up_load(t):
         return pltpu.make_async_copy(up_part.at[t], up_sum.tiles.at[t], tile_sem.at[0, t])
 
@@ -1436,7 +1487,8 @@
             copy.wait()
 
     for t in range(4):
-        up_load(t).start()
+        if t < up_sum.count:
+            up_load(t).start()
         for copy in down_load(t):
             copy.start()
     small.rows[0] = sums[...]
@@ -1470,6 +1522,10 @@
         grad_heads[s, here] = lax.dot_general(
             buf[s, here], weight[...], NT, preferred_element_type=f32
         ).astype(bf16)
+
+    def loaded(s, o):
+        for copy in loads:
+            copy.wait()
 
     def back(s, o):
         block = min(512, n * rows)
@@ -1492,19 +1548,32 @@
     def ops_of(c):
         chips = at.chips
         code_of = lambda kind, e: (kind + e // each, e % each // chips, e % chips)
-        backs = []
+        have = ("loaded", c)
+        ops = [((0, 0, 0), (6, 0, 0), gathered_here("in", c, 0, c), 0.2, [], [(0.0, have)])]
         for s in range(seqs):
             needs = [("done", c, s, o) for o in range(chips)]
-            backs.append(((4, s, 0), (4, s, 0), needs, 8.0, [], []))
+            ops.append(((4, s, 0), (4, s, 0), needs, 8.0, [], []))
         needs = [("done", c, s, o) for s in range(seqs) for o in range(chips)]
-        backs.append(((5, 0, 0), (5, 0, 0), needs, 3.0, [], []))
-        return backs + (
+        ops.append(((5, 0, 0), (5, 0, 0), needs, 3.0, [], []))
+        for rank, code, needs, time, sends, gives in scatter_ops(
+            c, chips, seqs, 1, "out", "part", last=4.0, parts=line.parts
+        ):
+            needs = needs + [have] if code[2] == c else needs
+            ops.append((rank, code, needs, time, sends, gives))
+        return ops + (
             gather_ops(c, chips, seqs, 0, "in")
-            + scatter_ops(c, chips, seqs, 1, "out", "part", last=4.0)
-            + work_ops(c, chips, seqs, 2, lambda s, o: gathered_here("in", c, s, o), "done", 1.0)
+            + work_ops(
+                c,
+                chips,
+                seqs,
+                2,
+                lambda s, o: gathered_here("in", c, s, o) + [have],
+                "done",
+                1.0,
+            )
             + work_ops(c, chips, seqs, 3, lambda s, o: [], "part", 0.3, rank=0, far=True)
             + group_ops(
-                c, at.group_bits, 4, PIECE, lambda e: code_of(8, e), 0, (1,), 0.7, -1, "up"
+                c, at.group_bits, 3, PIECE, lambda e: code_of(8, e), 0, (1,), 0.7, -1, "up"
             )
             + group_ops(
                 c, at.group_bits, 4, PIECE, lambda e: code_of(16, e), 1, (0,), 0.7, -1, "down"
@@ -1512,7 +1581,7 @@
         )
 
     actions = {2: work, 3: share, **ring.actions(0), **line.actions(1, final)}
-    actions[4], actions[5] = back, weight_work
+    actions[4], actions[5], actions[6] = back, weight_work, loaded
     for i in range(-(-up_sum.events() // each)):
         actions[8 + i] = functools.partial(up_event, i * each)
     for i in range(-(-down_sum.events() // each)):
@@ -1564,23 +1633,25 @@
             jax.ShapeDtypeStruct((part, width), bf16),
             jax.ShapeDtypeStruct(sums.shape, f32),
             jax.ShapeDtypeStruct((1, units), f32),
-            jax.ShapeDtypeStruct(up_part.shape, bf16),
+            jax.ShapeDtypeStruct((3,) + up_part.shape[1:], bf16),
             jax.ShapeDtypeStruct(down_part.shape, bf16),
         ),
-        in_specs=[vmem, hbm]
-        + [vmem] * 6
+        in_specs=[vmem, hbm, hbm, vmem, hbm, hbm, vmem, vmem]
         + [hbm] * 3
-        + [pl.BlockSpec(memory_space=pltpu.SMEM), vmem],
+        + [pl.BlockSpec(memory_space=pltpu.SMEM), hbm],
         out_specs=(vmem,) * 5 + (hbm, hbm),
         scratch_shapes=[VMEM((seqs, slots, width), bf16)]
         + Gather.scratch(n, seqs)
-        + Scatter.scratch(n, seqs, rows, width)
+        + Scatter.scratch(n, seqs, rows, width, 2)
         + [DMA((seqs, n // 2)), DMA((2, 4)), DMA((4,))]
-        + GroupSum.scratch(dp, 4, width // 4, units)
+        + GroupSum.scratch(dp, 3, width // 4, units)
         + GroupSum.scratch(dp, 4, units // 4, width, 1)
         + SmallSum.scratch(dp, n, sums.shape[0], width, True)
         + SmallSum.scratch(dp, n, 1, units, False)
-        + [VMEM((seqs, slots, part), bf16), VMEM((slots, HD), f32), VMEM((slots, HD), f32)],
+        + [VMEM((seqs, slots, part), bf16), VMEM((slots, HD), f32), VMEM((slots, HD), f32)]
+        + [VMEM(hidden.shape, f32)]
+        + [VMEM(a.shape, bf16) for a in (weight, mixed, heads)]
+        + [DMA((4,))],
         compiler_params=pltpu.CompilerParams(
             collective_id=4, has_side_effects=True, vmem_limit_bytes=62 * 2**20
         ),
@@ -1603,31 +1674,48 @@
 
 
 def finish_kernel(*refs):
-    sums_two, sums_one = refs[8:10]
-    targets = refs[10:]
-    for source, target in zip(refs[:8], targets):
-        target[...] = source[...].astype(target.dtype)
+    up_last, sums_two, sums_one = refs[8:11]
+    targets = refs[11:]
+    step = pl.program_id(0)
+    last = step == pl.num_programs(0) - 1
+    for i, (source, target) in enumerate(zip(refs[:8], targets)):
+        if i > 0:
+            target[...] = source[...].astype(target.dtype)
+
+    @pl.when(last)
+    def _():
+        targets[0][...] = up_last[...].astype(f32)
+
+    @pl.when(jnp.logical_not(last))
+    def _():
+        targets[0][...] = refs[0][...].astype(f32)
+
     rows = [sums_one[i : i + 1] for i in range(2)] + [sums_two[i : i + 1] for i in range(4)]
     for row, target in zip(rows, targets[8:]):
         target[...] = row
 
 
-def finish(blocks, wholes, sums_two, sums_one, steps=4):
+def finish(blocks, wholes, up_last, sums_two, sums_one, steps=4):
     width = sums_one.shape[1]
-    specs = [pl.BlockSpec((a.shape[0] // steps, a.shape[1]), lambda i: (i, 0)) for a, t in blocks]
-    specs += [pl.BlockSpec(a.shape, lambda i: (0, 0)) for a in wholes]
-    row = pl.BlockSpec((1, width), lambda i: (0, 0))
-    shapes = [jax.ShapeDtypeStruct(a.shape, t) for a, t in blocks]
+    ins, outs, shapes = [], [], []
+    for i, (a, kind, count) in enumerate(blocks):
+        block = (count // steps, a.shape[1])
+        held = a.shape[0] // block[0] - 1
+        ins.append(pl.BlockSpec(block, lambda i, held=held: (jnp.minimum(i, held), 0)))
+        outs.append(pl.BlockSpec(block, lambda i: (i, 0)))
+        shapes.append(jax.ShapeDtypeStruct((count, a.shape[1]), kind))
+    whole_specs = [pl.BlockSpec(a.shape, lambda i: (0, 0)) for a in wholes]
     shapes += [jax.ShapeDtypeStruct(a.shape, f32) for a in wholes]
+    lasts = (up_last, sums_two, sums_one)
     return pl.pallas_call(
         finish_kernel,
         grid=(steps,),
         out_shape=shapes + [jax.ShapeDtypeStruct((1, width), f32)] * 6,
-        in_specs=specs + [pl.BlockSpec(a.shape, lambda i: (0, 0)) for a in (sums_two, sums_one)],
-        out_specs=specs + [row] * 6,
+        in_specs=ins + whole_specs + [pl.BlockSpec(a.shape, lambda i: (0, 0)) for a in lasts],
+        out_specs=outs + whole_specs + [pl.BlockSpec((1, width), lambda i: (0, 0))] * 6,
         compiler_params=pltpu.CompilerParams(vmem_limit_bytes=62 * 2**20),
         name="finish",
-    )(*[a for a, t in blocks], *wholes, sums_two, sums_one)
+    )(*[block[0] for block in blocks], *wholes, *lasts)
 
 
 def body(
@@ -1690,15 +1778,16 @@
         lengths,
         heads,
     )
-    input_grad, sums_one, qkv_weight_grad, out_weight_grad, qkv_bias_grad = heads_scatter(
-        n, grads, qkv_weight, gathered_one, out_part, tokens, ln1_gain[None], hidden_grad
+    input_grad, sums_one, qkv_weight_grad, out_weight_grad, qkv_bias_grad, up_last = heads_scatter(
+        n, grads, qkv_weight, gathered_one, out_part, tokens, ln1_gain[None], hidden_grad, up_part
     )
-    width = tokens.shape[2]
+    width, part, units = tokens.shape[2], qkv_weight.shape[2], up_weight.shape[1]
+    seq_rows = tokens.shape[0] * tokens.shape[1]
     (
+        up_weight_grad,
+        down_weight_grad,
         qkv_weight_grad,
         out_weight_grad,
-        up_weight_grad,
-        down_weight_grad,
         output,
         input_grad,
         qkv_bias_grad,
@@ -1706,14 +1795,15 @@
         *rows,
     ) = finish(
         (
-            (qkv_weight_grad.reshape(-1, qkv_weight.shape[2]), f32),
-            (out_weight_grad.reshape(out_weight.shape), f32),
-            (up_weight_grad.reshape(up_weight.shape), f32),
-            (down_weight_grad.reshape(down_weight.shape), f32),
-            (output.reshape(-1, width), bf16),
-            (input_grad.reshape(-1, width), f32),
+            (up_weight_grad.reshape(-1, units), f32, width),
+            (down_weight_grad.reshape(-1, width), f32, units),
+            (qkv_weight_grad.reshape(-1, part), f32, 3 * width),
+            (out_weight_grad.reshape(-1, width), f32, part),
+            (output.reshape(-1, width), bf16, seq_rows),
+            (input_grad.reshape(-1, width), f32, seq_rows),
         ),
         (qkv_bias_grad, up_bias_grad),
+        up_last[0],
         sums,
         sums_one,
     )

time: 536 us -> 529 us (0.987)
  Pallas kernels: 531 us -> 525 us
    pallas_call x1, Pallas kernels: 127 us -> 115 us  [attn_grad(): pl.pallas_call(functools.partial(attn_grad_kernel, n), out_shape=(jax.Sha...]
    pallas_call x1, Pallas kernels: 97.8 us -> 106 us  [heads_scatter(): pl.pallas_call(functools.partial(heads_scatter_kernel, n), out_shape=(jax...]
where the time goes in v10:
time: 529 us; the launch traced here: 526 us
  Pallas kernels  525 us (99%)
    pallas_call x1, Pallas kernels, attention_block(): pl.pallas_call(functools.partial(attention_block_kernel, n), out_shape=(j...  174 us
    pallas_call x1, Pallas kernels, mlp_block(): pl.pallas_call(functools.partial(mlp_kernel, n), out_shape=(jax.ShapeDtyp...  116 us
    pallas_call x1, Pallas kernels, attn_grad(): pl.pallas_call(functools.partial(attn_grad_kernel, n), out_shape=(jax.Sha...  115 us
    pallas_call x1, Pallas kernels, heads_scatter(): pl.pallas_call(functools.partial(heads_scatter_kernel, n), out_shape=(jax...  106 us
    pallas_call x1, Pallas kernels, finish(): pl.pallas_call(finish_kernel, grid=(steps,), out_shape=shapes + [jax.Shap...  14.6 us

profile of v10, /device:TPU:0, one launch (start us, length us, event | category | flops | bytes accessed | tf_op | source)
XLA Modules:
  0.0 525.7 jit_solution(8335637997394693830)
XLA Ops:
  0.6 174.1 %attention_block.1 = (bf16[2,1024,2048]{2,1,0:T(8,128)(2,1)}, bf16[3,2,1024,256]{3,2,1,0:T(8,128)(2,1)}, bf16[2,1024,256]{2,1,0:T(8,128)(2,1)}, f32[2,128,2048]{...) custom-call(bf16[2,128,2048]{2,1,0:T(8,128)(2,1)} %tokens_hbm.1, ...), custom_call_target="tpu_custom_call" | custom-call | tf_op jit(solution)/shard_map/attention_block/pallas_call | solution.py:934
  174.8 116.0 %mlp_block.1 = (bf16[2,1024,2048]{2,1,0:T(8,128)(2,1)}, f32[2,128,2048]{2,1,0:T(8,128)}, bf16[2,128,2048]{2,1,0:T(8,128)(2,1)}, f32[4,2048]{1,0:T(4,128)}, bf16[...) custom-call(bf16[2,128,2048]{2,1,0:T(8,128)(2,1)} %get-tuple-element, ...), custom_call_target="tpu_custom_call" | custom-call | tf_op jit(solution)/shard_map/mlp_block/pallas_call | solution.py:1385
  290.8 114.6 %attn_grad.1 = (bf16[2,128,2048]{2,1,0:T(8,128)(2,1)}, bf16[3,2,1024,256]{3,2,1,0:T(8,128)(2,1)}, bf16[256,2048]{1,0:T(8,128)(2,1)}, f32[4,2048]{1,0:T(4,128)}, ...) custom-call(bf16[2,128,2048]{2,1,0:T(8,128)(2,1)} %get-tuple-element.58.grad, ...), custom_call_target="tpu_custom_call" | custom-call | tf_op jit(solution)/shard_map/attn_grad/pallas_call | solution.py:1628
  405.4 105.5 %heads_scatter.1 = (f32[2,128,2048]{2,1,0:T(8,128)}, f32[2,2048]{1,0:T(2,128)}, bf16[3,2048,256]{2,1,0:T(8,128)(2,1)}, bf16[1,256,2048]{2,1,0:T(8,128)(2,1)}, f3...) custom-call(bf16[3,2,1024,256]{3,2,1,0:T(8,128)(2,1)} %get-tuple-element.69.grads, bf16[3,2048,256]{2,1,0:T(8,128)(2,1)} %weight.3, ...), custom_call_target="tpu_custom_call" | custom-call | tf_op jit(solution)/shard_map/heads_scatter/pallas_call | solution.py:1134
  510.9 14.6 %finish.1 = (f32[2048,1024]{1,0:T(8,128)}, f32[1024,2048]{1,0:T(8,128)}, f32[6144,256]{1,0:T(8,128)}, f32[256,2048]{1,0:T(8,128)}, bf16[256,2048]{1,0:T(8,128)(2...) custom-call(bf16[1536,1024]{1,0:T(8,128)(2,1)} %bitcast.25, ...), custom_call_target="tpu_custom_call" | custom-call | tf_op jit(solution)/shard_map/finish/pallas_call | solution.py:1710

commit v11 on v10

--- a/solution.py
+++ b/solution.py
@@ -763,13 +763,13 @@
 def attention_block_kernel(
     n,
     tokens,
-    cotangent,
+    cotangent_hbm,
     lengths,
     gain,
     shift,
-    weight,
+    weight_hbm,
     bias,
-    out_weight,
+    out_weight_hbm,
     out_bias,
     gain_two,
     shift_two,
@@ -790,6 +790,10 @@
     grad_recv,
     masked,
     mask_sem,
+    cotangent,
+    weight,
+    out_weight,
+    in_sem,
     *scratch,
 ):
     at = Place(n)
@@ -798,17 +802,37 @@
     grad_ring = Gather(at, rows, grad_all, grad_send, grad_recv)
     line = Scatter(at, rows, *scratch)
 
+    sources = (weight_hbm, weight), (cotangent_hbm, cotangent), (out_weight_hbm, out_weight)
+    loads = [
+        pltpu.make_async_copy(source, target, in_sem.at[i])
+        for i, (source, target) in enumerate(sources)
+    ]
+    for copy in loads:
+        copy.start()
+
     def mask_copy(s):
         return pltpu.make_async_copy(
             masked.at[s], grad_all.at[s, rows_of(at.me, rows)], mask_sem.at[s]
         )
 
-    for s in range(seqs):
+    def norm(s, o):
+        def block(i, carry):
+            first = pl.multiple_of(i * 16, 16)
+            values = tokens[s, pl.ds(first, 16)].astype(f32)
+            values = norm_rows(values, gain[...], shift[...])
+            buf[s, pl.ds(pl.multiple_of(at.me * rows + first, 16), 16)] = values.astype(bf16)
+            return carry
+
+        lax.fori_loop(0, rows // 16, block, 0)
+
+    def loaded(s, o):
+        for copy in loads:
+            copy.wait()
+
+    def mask(s, o):
         def block(i, carry):
             first = pl.multiple_of(i * 16, 16)
             here = pl.ds(first, 16)
-            values = norm_rows(tokens[s, here].astype(f32), gain[...], shift[...])
-            buf[s, pl.ds(pl.multiple_of(at.me * rows + first, 16), 16)] = values.astype(bf16)
             slot = at.me * rows + first + lax.broadcasted_iota(jnp.int32, (16, width), 0)
             grad = jnp.where(slot < lengths[s], cotangent[s, here].astype(f32), 0.0)
             masked[s, here] = grad.astype(bf16)
@@ -816,9 +840,9 @@
 
         lax.fori_loop(0, rows // 16, block, 0)
         mask_copy(s).start()
+        mask_copy(s).wait()
+
     at.greet()
-    for s in range(seqs):
-        mask_copy(s).wait()
 
     def keep(s, o):
         here = rows_of(o, 2 * rows)
@@ -864,21 +888,31 @@
 
     def ops_of(c):
         chips = at.chips
-        mixing = []
+        have = ("loaded", c)
+        singles = [((-1, 9, 0), (8, 0, 0), [("norm", c, seqs - 1)], 0.2, [], [(0.0, have)])]
+        gathers = []
         for s in range(seqs):
             needs = [("heads", c, s, o) for o in range(chips)]
-            mixing.append(((2, s, 0), (2, s, 0), needs, 6.0, [], [(0.0, ("mixed", c, s))]))
+            singles.append(((2, s, 0), (2, s, 0), needs, 6.0, [], [(0.0, ("mixed", c, s))]))
+            singles.append(((-2 + s, 0, 0), (6, s, 0), [], 2.0, [], [(0.0, ("norm", c, s))]))
+            singles.append(((3 + s, 0, 0), (7, s, 0), [have], 2.0, [], [(0.0, ("mask", c, s))]))
+        for ops, first in (
+            (gather_ops(c, chips, seqs, 0, "in", gate=True), "norm"),
+            (gather_ops(c, chips, seqs, 5, "grad", rank=6), "mask"),
+        ):
+            for rank, code, needs, time, sends, gives in ops:
+                needs = needs + [(first, c, code[1])] if code[2] == c else needs
+                gathers.append((rank, code, needs, time, sends, gives))
         return (
-            gather_ops(c, chips, seqs, 0, "in", gate=True)
+            singles
+            + gathers
             + work_ops(
-                c, chips, seqs, 1, lambda s, o: gathered_here("in", c, s, o), "heads", 1.0
+                c, chips, seqs, 1, lambda s, o: gathered_here("in", c, s, o) + [have], "heads", 1.0
             )
-            + mixing
             + work_ops(
                 c, chips, seqs, 3, lambda s, o: [("mixed", c, s)], "part", 1.0, far=True
             )
             + scatter_ops(c, chips, seqs, 4, "out", "part", last=4.0)
-            + gather_ops(c, chips, seqs, 5, "grad", rank=6)
         )
 
     Plan(at, seqs, ops_of).run(
@@ -886,6 +920,9 @@
             1: project,
             2: mix,
             3: project_out,
+            6: norm,
+            7: mask,
+            8: loaded,
             **ring.actions(0),
             **line.actions(4, final),
             **grad_ring.actions(5),
@@ -941,7 +978,7 @@
             jax.ShapeDtypeStruct((seqs, rows, width), bf16),
             jax.ShapeDtypeStruct((seqs, n * rows, width), bf16),
         ),
-        in_specs=[vmem, vmem, smem] + [vmem] * 8,
+        in_specs=[vmem, hbm, smem, vmem, vmem, hbm, vmem, hbm, vmem, vmem, vmem],
         out_specs=(hbm, hbm, hbm, vmem, vmem, hbm),
         scratch_shapes=[
             VMEM((3, seqs, n * rows, part), bf16),
@@ -953,6 +990,8 @@
         + [DMA((seqs, n // 2))]
         + Gather.scratch(n, seqs)
         + [VMEM((seqs, rows, width), bf16), DMA((seqs,))]
+        + [VMEM(a.shape, bf16) for a in (cotangent, weight, out_weight)]
+        + [DMA((3,))]
         + Scatter.scratch(n, seqs, rows, width),
         compiler_params=pltpu.CompilerParams(
             collective_id=0, has_side_effects=True, vmem_limit_bytes=60 * 2**20
@@ -975,8 +1014,8 @@
 
 def heads_scatter_kernel(
     n,
-    grads,
-    weight,
+    grads_hbm,
+    weight_hbm,
     gathered_hbm,
     out_part,
     tokens_hbm,
@@ -998,8 +1037,15 @@
     out_sum = GroupSum(at, out_part.shape[0], *scratch[12:17], out_grad, turn=1)
     small = DirectSum(at, *scratch[17:22])
     small_bias = SmallSum(at, *scratch[22:26], False)
-    gathered, tokens, hidden_grad, in_sem = scratch[26:30]
-    up_sum = GroupSum(at, up_part.shape[1], *scratch[30:35], up_grad, turn=1)
+    gathered, tokens, hidden_grad, grads, weight, in_sem = scratch[26:32]
+    early = [
+        pltpu.make_async_copy(grads_hbm, grads, in_sem.at[4]),
+        pltpu.make_async_copy(weight_hbm, weight, in_sem.at[5]),
+        pltpu.make_async_copy(out_part, out_sum.tiles.at[0], in_sem.at[6]),
+    ]
+    for copy in early:
+        copy.start()
+    up_sum = GroupSum(at, up_part.shape[1], *scratch[32:37], up_grad, turn=1)
     up_load = pltpu.make_async_copy(up_part.at[3], up_sum.tiles.at[0], in_sem.at[3])
     up_load.start()
     sources = ((gathered_hbm, gathered), (tokens_hbm, tokens), (hidden_hbm, hidden_grad))
@@ -1009,9 +1055,10 @@
     ]
     for copy in loads:
         copy.start()
-    out_sum.tiles[0] = out_part[...]
     small.rows[...] = jnp.zeros_like(small.rows)
     at.greet(groups=True, everyone=True)
+    for copy in early:
+        copy.wait()
 
     def bias_sums():
         for row, j, scale in ((0, 0, HD ** (-0.5)), (1, 2, 1.0)):
@@ -1141,7 +1188,7 @@
             jax.ShapeDtypeStruct((2, part), f32),
             jax.ShapeDtypeStruct((1,) + up_part.shape[1:], bf16),
         ),
-        in_specs=[vmem, vmem, hbm, vmem, hbm, vmem, hbm, hbm],
+        in_specs=[hbm, hbm, hbm, hbm, hbm, vmem, hbm, hbm],
         out_specs=(vmem, vmem, hbm, hbm, vmem, hbm),
         scratch_shapes=Scatter.scratch(n, seqs, rows, width, 2)
         + GroupSum.scratch(dp, 3, width, part)
@@ -1152,7 +1199,9 @@
             VMEM(gathered.shape, bf16),
             VMEM(tokens.shape, bf16),
             VMEM(hidden_grad.shape, f32),
-            DMA((4,)),
+            VMEM(grads.shape, bf16),
+            VMEM(weight.shape, bf16),
+            DMA((7,)),
         ]
         + GroupSum.scratch(dp, 1, *up_part.shape[1:]),
         compiler_params=pltpu.CompilerParams(

time: 529 us -> 525 us (level)
  no operation moved by 1% of the time
where the time goes in v11:
time: 525 us; the launch traced here: 522 us
  Pallas kernels  521 us (99%)
    pallas_call x1, Pallas kernels, attention_block(): pl.pallas_call(functools.partial(attention_block_kernel, n), out_shape=(j...  173 us
    pallas_call x1, Pallas kernels, mlp_block(): pl.pallas_call(functools.partial(mlp_kernel, n), out_shape=(jax.ShapeDtyp...  116 us
    pallas_call x1, Pallas kernels, attn_grad(): pl.pallas_call(functools.partial(attn_grad_kernel, n), out_shape=(jax.Sha...  115 us
    pallas_call x1, Pallas kernels, heads_scatter(): pl.pallas_call(functools.partial(heads_scatter_kernel, n), out_shape=(jax...  103 us
    pallas_call x1, Pallas kernels, finish(): pl.pallas_call(finish_kernel, grid=(steps,), out_shape=shapes + [jax.Shap...  14.6 us

profile of v11, /device:TPU:0, one launch (start us, length us, event | category | flops | bytes accessed | tf_op | source)
XLA Modules:
  0.0 521.7 jit_solution(5009421367963067827)
XLA Ops:
  0.6 172.7 %attention_block.1 = (bf16[2,1024,2048]{2,1,0:T(8,128)(2,1)}, bf16[3,2,1024,256]{3,2,1,0:T(8,128)(2,1)}, bf16[2,1024,256]{2,1,0:T(8,128)(2,1)}, f32[2,128,2048]{...) custom-call(bf16[2,128,2048]{2,1,0:T(8,128)(2,1)} %tokens_hbm.1, ...), custom_call_target="tpu_custom_call" | custom-call | tf_op jit(solution)/shard_map/attention_block/pallas_call | solution.py:971
  173.4 116.0 %mlp_block.1 = (bf16[2,1024,2048]{2,1,0:T(8,128)(2,1)}, f32[2,128,2048]{2,1,0:T(8,128)}, bf16[2,128,2048]{2,1,0:T(8,128)(2,1)}, f32[4,2048]{1,0:T(4,128)}, bf16[...) custom-call(bf16[2,128,2048]{2,1,0:T(8,128)(2,1)} %get-tuple-element, ...), custom_call_target="tpu_custom_call" | custom-call | tf_op jit(solution)/shard_map/mlp_block/pallas_call | solution.py:1434
  289.4 114.6 %attn_grad.1 = (bf16[2,128,2048]{2,1,0:T(8,128)(2,1)}, bf16[3,2,1024,256]{3,2,1,0:T(8,128)(2,1)}, bf16[256,2048]{1,0:T(8,128)(2,1)}, f32[4,2048]{1,0:T(4,128)}, ...) custom-call(bf16[2,128,2048]{2,1,0:T(8,128)(2,1)} %get-tuple-element.58.grad, ...), custom_call_target="tpu_custom_call" | custom-call | tf_op jit(solution)/shard_map/attn_grad/pallas_call | solution.py:1677
  404.0 102.9 %heads_scatter.1 = (f32[2,128,2048]{2,1,0:T(8,128)}, f32[2,2048]{1,0:T(2,128)}, bf16[3,2048,256]{2,1,0:T(8,128)(2,1)}, bf16[1,256,2048]{2,1,0:T(8,128)(2,1)}, f3...) custom-call(bf16[3,2,1024,256]{3,2,1,0:T(8,128)(2,1)} %get-tuple-element.69.grads_hbm, bf16[3,2048,256]{2,1,0:T(8,128)(2,1)} %weight_hbm.5, ...), custom_call_target="tpu_custom_call" | custom-call | tf_op jit(solution)/shard_map/heads_scatter/pallas_call | solution.py:1181
  506.9 14.6 %finish.1 = (f32[2048,1024]{1,0:T(8,128)}, f32[1024,2048]{1,0:T(8,128)}, f32[6144,256]{1,0:T(8,128)}, f32[256,2048]{1,0:T(8,128)}, bf16[256,2048]{1,0:T(8,128)(2...) custom-call(bf16[1536,1024]{1,0:T(8,128)(2,1)} %bitcast.25, ...), custom_call_target="tpu_custom_call" | custom-call | tf_op jit(solution)/shard_map/finish/pallas_call | solution.py:1759
